TPU v7x, 256 devices: a whole 4x4x8 slice. The times are simulated.
256 devices in a mesh: dp: 16 (over z_lo, y), seq: 16 (over z_hi, x, core).
Axes of the slice: x: 4, y: 4, z: 8 (z_hi: 2, z_lo: 4; z = z_hi * 4 + z_lo), core: 2. Of those that a mesh axis runs over, the one named last changes fastest.
Arguments:
- layer_input: bfloat16 [16, 2048, 2048], P('dp', 'seq'), may hold values from -6 to 6
- writes_first: bfloat16 [16, 2048, 128], P('dp', 'seq'), may hold values from -0.25 to 0.25
- reads_first: bfloat16 [16, 2048, 128], P('dp', 'seq'), may hold values from -0.25 to 0.25
- decay_first: float32 [16, 32, 2048], P('dp', None, 'seq'), may hold values from -1.5 to 0, as said below
- skip_first: float32 [32], replicated, may hold values from 0.5 to 1.5
- writes_second: bfloat16 [16, 2048, 128], P('dp', 'seq'), may hold values from -0.25 to 0.25
- reads_second: bfloat16 [16, 2048, 128], P('dp', 'seq'), may hold values from -0.25 to 0.25
- decay_second: float32 [16, 32, 2048], P('dp', None, 'seq'), may hold values from -1.5 to 0, as said below
- skip_second: float32 [32], replicated, may hold values from 0.5 to 1.5
- order_first: int32 [2048], P('seq'), may hold values from 0 to 2047, as said below
- order_second: int32 [2048], P('seq'), may hold values from 0 to 2047, as said below
- cotangent: float32 [16, 2048, 2048], P('dp', 'seq'), may hold values from -48 to 48
Outputs:
- grad_input: bfloat16 [16, 2048, 2048], P('dp', 'seq')
- grad_writes_first: bfloat16 [16, 2048, 128], P('dp', 'seq')
- grad_reads_first: bfloat16 [16, 2048, 128], P('dp', 'seq')
- grad_decay_first: float32 [16, 32, 2048], P('dp', None, 'seq')
- grad_skip_first: float32 [32], replicated
- grad_writes_second: bfloat16 [16, 2048, 128], P('dp', 'seq')
- grad_reads_second: bfloat16 [16, 2048, 128], P('dp', 'seq')
- grad_decay_second: float32 [16, 32, 2048], P('dp', None, 'seq')
- grad_skip_second: float32 [32], replicated
Inputs may be any that keep to these rules, and one draw needn't show every extreme that they name: order_first lists the cells of a 64 by 32 grid (cell i * 32 + j for row i, column j) row after row from row 0 on, each row left to right or right to left. order_second lists the same cells column after column from column 0 on, each column top to bottom or bottom to top. `decay_first`: every entry is negative. `decay_second`: every entry is negative.
All inputs are finite; a program needn't handle non-finite values.
Results may differ from a plain program's by a relative error of at most 0.005.
Values may be sent and summed in bfloat16 or wider, within the bound.
No kernel may reach another device: no remote copies, remote signals or barrier semaphores. Data moves between devices by JAX's collectives and lax.ppermute only.
A program may use at most 128 MiB of HBM per device.

v0:
```python
import math

import jax
import jax.numpy as jnp
from jax import lax
from jax.sharding import PartitionSpec as P

GROUP = 128
COLS = 32


highest = lax.Precision.HIGHEST


def entering_2(array, axis, combine, identity, reverse):
    length, position = (lax.axis_size(axis), lax.axis_index(axis))
    everything = jax.tree.map(lambda part: lax.all_gather(part, axis), array)
    start = jax.tree.map(
        lambda part, zero: jnp.broadcast_to(jnp.asarray(zero, part.dtype), part.shape),
        array,
        identity,
    )

    def lap(k, before):
        at = length - 1 - k if reverse else k
        reached = at > position if reverse else at < position
        new = combine(before, jax.tree.map(lambda part: part[at], everything))
        return jax.tree.map(lambda a, b: jnp.where(reached, a, b), new, before)

    return lax.fori_loop(0, length, lap, start)


def group_step(carried, pieces, skip):
    inputs, writes, reads, log_decay = pieces
    running = jnp.cumsum(log_decay, axis=0)
    length = inputs.shape[0]
    causal = jnp.tril(jnp.ones((length, length), dtype=bool))
    scores = jnp.dot(reads, writes.T, precision=highest)
    log_gap = running.T[:, :, None] - running.T[:, None, :]
    weights = (
        jnp.where(causal[None], jnp.exp(jnp.where(causal[None], log_gap, 0.0)), 0.0) * scores[None]
    )
    outputs = jnp.einsum("hts,shp->thp", weights, inputs, precision=highest)
    carried_out = jnp.einsum("hpn,tn->thp", carried, reads, precision=highest)
    outputs = outputs + jnp.exp(running)[:, :, None] * carried_out + skip[None, :, None] * inputs
    totals = running[-1]
    scaled = inputs * jnp.exp(totals[None, :] - running)[:, :, None]
    carried = jnp.exp(totals)[:, None, None] * carried + jnp.einsum(
        "shp,sn->hpn", scaled, writes, precision=highest
    )
    return (carried, outputs)


def run_layer(inputs, writes, reads, log_decay, skip, carried):
    length, features = inputs.shape
    head_count = log_decay.shape[1]
    head_size = features // head_count
    block_count = length // GROUP
    stacked = (
        inputs.reshape(block_count, GROUP, head_count, head_size),
        writes.reshape(block_count, GROUP, writes.shape[1]),
        reads.reshape(block_count, GROUP, reads.shape[1]),
        log_decay.reshape(block_count, GROUP, head_count),
    )
    carried, outputs = lax.scan(
        lambda carry_now, pieces: group_step(carry_now, pieces, skip), carried, stacked
    )
    return (outputs.reshape(length, features), carried)


def local_state(inputs, writes, log_decay, carried):
    length, features = inputs.shape
    head_count = log_decay.shape[1]
    running = jnp.cumsum(log_decay, axis=0)
    totals = running[-1]
    scaled = (
        inputs.reshape(length, head_count, features // head_count)
        * jnp.exp(totals[None, :] - running)[:, :, None]
    )
    return jnp.exp(totals)[:, None, None] * carried + jnp.einsum(
        "shp,sn->hpn", scaled, writes, precision=highest
    )


def combine(earlier, later):
    return (earlier[0] * later[0], later[0][:, None, None] * earlier[1] + later[1])


def carry_chain(log_decay, own_state):
    decays = jnp.exp(jnp.sum(log_decay, axis=0))
    identity = (jnp.ones_like(decays), jnp.zeros_like(own_state))
    return entering_2((decays, own_state), "seq", combine, identity, False)[1]


def pass_back(log_decay, own_adjoint):
    decays = jnp.exp(jnp.sum(log_decay, axis=0))
    identity = (jnp.ones_like(decays), jnp.zeros_like(own_adjoint))
    return entering_2((decays, own_adjoint), "seq", combine, identity, True)[1]


def regrid_forward(values, order_first, order_second):
    length, features = values.shape
    seq_count = lax.axis_size("seq")
    row_count = length // COLS
    col_count = COLS // seq_count
    lattice = values.reshape(row_count, COLS, features)
    row_flip = order_first.reshape(row_count, COLS)[:, 0] % COLS != 0
    lattice = jnp.where(row_flip[:, None, None], lattice[:, ::-1], lattice)
    lattice = lattice.reshape(row_count, seq_count, col_count, features).transpose(1, 2, 0, 3)
    columns = lax.all_to_all(lattice, "seq", split_axis=0, concat_axis=2, tiled=True)
    columns = columns.reshape(col_count, seq_count * row_count, features)
    col_flip = order_second.reshape(col_count, seq_count * row_count)[:, 0] // COLS != 0
    columns = jnp.where(col_flip[:, None, None], columns[:, ::-1], columns)
    return columns.reshape(length, features)


def regrid_back(values, order_first, order_second):
    length, features = values.shape
    seq_count = lax.axis_size("seq")
    row_count = length // COLS
    col_count = COLS // seq_count
    columns = values.reshape(col_count, seq_count * row_count, features)
    col_flip = order_second.reshape(col_count, seq_count * row_count)[:, 0] // COLS != 0
    columns = jnp.where(col_flip[:, None, None], columns[:, ::-1], columns)
    columns = columns.reshape(col_count, seq_count, row_count, features)
    rows_back = lax.all_to_all(columns, "seq", split_axis=1, concat_axis=0, tiled=True)
    lattice = rows_back.reshape(COLS, row_count, features).transpose(1, 0, 2)
    row_flip = order_first.reshape(row_count, COLS)[:, 0] % COLS != 0
    lattice = jnp.where(row_flip[:, None, None], lattice[:, ::-1], lattice)
    return lattice.reshape(length, features)


def backward_layer(inputs, writes, reads, log_decay, skip, entering, upstream):
    length, features = inputs.shape
    head_count = log_decay.shape[1]
    running = jnp.cumsum(log_decay, axis=0)
    weighted = (
        upstream.reshape(length, head_count, features // head_count) * jnp.exp(running)[:, :, None]
    )
    own_adjoint = jnp.einsum("thp,tn->hpn", weighted, reads, precision=highest)

    def whole(inputs_now, writes_now, reads_now, decay_now, skip_now):
        return run_layer(inputs_now, writes_now, reads_now, decay_now, skip_now, entering)

    leaving = pass_back(log_decay, own_adjoint)
    _, pullback = jax.vjp(whole, inputs, writes, reads, log_decay, skip)
    return pullback((upstream, leaving))


def on_device(
    layer_input,
    writes_first,
    reads_first,
    decay_first,
    skip_first,
    writes_second,
    reads_second,
    decay_second,
    skip_second,
    order_first,
    order_second,
    cotangent,
):
    inputs = layer_input[0].astype(jnp.float32)
    writes_one = writes_first[0].astype(jnp.float32)
    reads_one = reads_first[0].astype(jnp.float32)
    decay_one = decay_first[0].T
    writes_two = writes_second[0].astype(jnp.float32)
    reads_two = reads_second[0].astype(jnp.float32)
    decay_two = decay_second[0].T
    length, features = inputs.shape
    head_count = skip_first.shape[0]
    head_size = features // head_count
    empty_state = jnp.zeros((head_count, head_size, writes_one.shape[1]), jnp.float32)
    entering_one = carry_chain(decay_one, local_state(inputs, writes_one, decay_one, empty_state))
    first_out = run_layer(inputs, writes_one, reads_one, decay_one, skip_first, entering_one)[0]
    second_in = regrid_forward(first_out.astype(jnp.bfloat16), order_first, order_second).astype(
        jnp.float32
    )
    entering_two = carry_chain(
        decay_two, local_state(second_in, writes_two, decay_two, empty_state)
    )
    grads_two = backward_layer(
        second_in, writes_two, reads_two, decay_two, skip_second, entering_two, cotangent[0]
    )
    back_rows = regrid_back(grads_two[0].astype(jnp.bfloat16), order_first, order_second).astype(
        jnp.float32
    )
    entering_one = carry_chain(decay_one, local_state(inputs, writes_one, decay_one, empty_state))
    grads_one = backward_layer(
        inputs, writes_one, reads_one, decay_one, skip_first, entering_one, back_rows
    )
    skip_sums = lax.psum((grads_one[4], grads_two[4]), ("dp", "seq"))
    factor = 1.0 / math.sqrt(lax.axis_size("dp") * lax.axis_size("seq") * length * head_size)
    return (
        grads_one[0].astype(jnp.bfloat16)[None],
        grads_one[1].astype(jnp.bfloat16)[None],
        grads_one[2].astype(jnp.bfloat16)[None],
        grads_one[3].T[None],
        skip_sums[0] * factor,
        grads_two[1].astype(jnp.bfloat16)[None],
        grads_two[2].astype(jnp.bfloat16)[None],
        grads_two[3].T[None],
        skip_sums[1] * factor,
    )


def solution(mesh):
    placed = (
        P("dp", "seq", None),
        P("dp", "seq", None),
        P("dp", "seq", None),
        P("dp", None, "seq"),
        P(),
        P("dp", "seq", None),
        P("dp", "seq", None),
        P("dp", None, "seq"),
        P(),
        P("seq"),
        P("seq"),
        P("dp", "seq", None),
    )
    return jax.shard_map(
        on_device,
        mesh=mesh,
        in_specs=placed,
        out_specs=(
            P("dp", "seq", None),
            P("dp", "seq", None),
            P("dp", "seq", None),
            P("dp", None, "seq"),
            P(),
            P("dp", "seq", None),
            P("dp", "seq", None),
            P("dp", None, "seq"),
            P(),
        ),
        check_vma=False,
    )
```

profile of v0, /device:TPU:1, one launch (start us, length us, event | category | flops | bytes accessed | tf_op | source)
XLA Modules:
  0.0 834.8 jit_solution(16885560039588449433)
XLA Ops:
  12.8 1.6 fusion.106
  16.2 46.7 %all-reduce.5 = (f32[512]{0:T(512)S(1)}, f32[512]{0:T(512)S(1)}) all-reduce(f32[512]{0:T(512)S(1)} %exponential_dynamic-update-slice_fusion, f32[512]{0:T(512)S(1)} %exponential_dynamic-update-slice_fusion.1), channel_id=3, replica_groups=mesh['dp'=16,'seq'=16] {'seq'}, use_global_device_ids=true, to_apply=%add.3 | all-reduce | flops 1024 | bytes 8192
  64.0 127.1 %all-gather.15.cloned.1.call-done = f32[512,64,128]{2,1,0:T(8,128)} async-done(((f32[32,64,128]{2,1,0:T(8,128)}), f32[512,64,128]{2,1,0:T(8,128)}) %all-gather.15.cloned.1.call-update) | async-done | bytes 16777232 | tf_op jit(solution)/shard_map/all_gather | solution.py:17
  191.1 24.2 %while.50 = (s32[]{:T(128)}, f32[32,64,128]{2,1,0:T(8,128)S(1)}, s32[]{:T(128)}, f32[16,32]{1,0:T(8,128)S(1)}, f32[16,32,64,128]{3,2,1,0:T(8,128)}, /*index=5*/s32[]{:T(128)}, s32[]{:T(128)}) while((s32[]{:T(128)}, f32[32,64,128]{2,1,0:T(8,128)S(1)}, s32[]{:T(128)}, f32[16,32]{1,0:T(8,128)S(1)}, f32[16,32,64,128]{3,2,1,0:T(8,128)}, ...), condition=%wide.region_10.11_spmd.clone, body=%wide.region_9.10_spmd.clone.sunk | while | flops 1048580 | bytes 3146217 | solution.py:30
  216.9 2.7 fusion.45
  219.7 2.5 copy.302
  222.2 2.0 convert_element_type.149
  224.2 5.1 rev.14
  231.8 3.6 all-to-all-start.1
  235.7 130.3 %all-gather.11.cloned.1.call-done = f32[512,64,128]{2,1,0:T(8,128)} async-done(((f32[32,64,128]{2,1,0:T(8,128)}), f32[512,64,128]{2,1,0:T(8,128)}) %all-gather.11.cloned.1.call-update) | async-done | bytes 16777232 | tf_op jit(solution)/shard_map/all_gather | solution.py:17
  366.1 24.2 %while.48 = (s32[]{:T(128)}, f32[32,64,128]{2,1,0:T(8,128)S(1)}, s32[]{:T(128)}, f32[16,32]{1,0:T(8,128)S(1)}, f32[16,32,64,128]{3,2,1,0:T(8,128)}, /*index=5*/s32[]{:T(128)}, s32[]{:T(128)}, s32[]{:T(128)}, s32[]{:T(128)}) while((s32[]{:T(128)}, f32[32,64,128]{2,1,0:T(8,128)S(1)}, s32[]{:T(128)}, f32[16,32]{1,0:T(8,128)S(1)}, ...), condition=%wide.region_4.5_spmd.clone, body=%wide.region_3.4_spmd.clone.sunk | while | flops 1048584 | bytes 3146279 | solution.py:30
  391.8 5.1 rev.15
  396.9 2.5 fusion.116
  400.3 2.1 convert_element_type.150
  402.4 2.2 copy.307
  404.6 1.6 fusion.70
  407.5 3.4 reshape.913
  410.9 3.9 copy.320
  414.8 2.5 convert_multiply_fusion.11
  417.3 3.0 mul.682
  420.3 5.1 fusion.32
  425.7 4.3 fusion.51
  431.5 2.4 copy.319
  433.9 5.6 rev.12
  442.0 4.2 all-to-all-start
  447.7 2.0 mul.645.clone
  449.6 2.8 mul.646
  452.5 13.7 %all-to-all-done = bf16[2,16,4,2048]{3,0,2,1:T(2,128)(2,1)S(1)} async-done(((bf16[2,16,4,2048]{3,0,2,1:T(2,128)(2,1)}), bf16[2,16,4,2048]{3,0,2,1:T(2,128)(2,1)S(1)}, u32[]{:S(2)}, u32[]{:S(2)}) %all-to-all-start) | async-done | bytes 524320 | tf_op jit(solution)/shard_map/all_to_all | solution.py:126
  466.7 5.1 rev.13
  471.9 1.9 fusion.67
  474.7 2.2 mul.648
  476.9 2.7 copy.287
  479.5 1.6 fusion.96
  481.2 1.7 fusion.72
  483.1 2.9 convolution_bitcast_fusion.5
  486.8 142.7 %all-reduce.4 = (f32[32]{0:T(128)}, f32[32]{0:T(128)}) all-reduce(f32[32]{0:T(128)S(1)} %reduce_sum.316, f32[32]{0:T(128)S(1)} %reduce_sum.327), channel_id=1, replica_groups=mesh['dp'=16,'seq'=16] {'dp','seq'}, use_global_device_ids=true, to_apply=%region_20.21 | all-reduce | flops 64 | bytes 512 | tf_op jit(solution)/shard_map/psum | solution.py:193
  629.5 2.8 convert_element_type.136
  632.3 3.0 copy.290
  635.3 3.0 copy.293
  638.3 1.8 fusion.118
  640.2 5.5 fusion.58
  646.6 1.8 convolution_bitcast_fusion.6
  649.9 54.7 %while.51 = (s32[]{:T(128)}, f32[32,64,128]{2,1,0:T(8,128)}, s32[]{:T(128)}, f32[16,32]{1,0:T(8,128)}, f32[16,32,64,128]{3,2,1,0:T(8,128)}, /*index=5*/s32[]{:T(128)}, s32[]{:T(128)}) while((s32[]{:T(128)}, f32[32,64,128]{2,1,0:T(8,128)}, s32[]{:T(128)}, f32[16,32]{1,0:T(8,128)}, f32[16,32,64,128]{3,2,1,0:T(8,128)}, ...), condition=%wide.region_23.24_spmd.clone, body=%wide.region_22.23_spmd.clone.sunk | while | flops 1048580 | bytes 3146217 | solution.py:30
  650.6 2.4 fusion.150
  653.7 2.7 fusion.150
  657.1 2.7 fusion.150
  660.6 2.7 fusion.150
  664.0 3.0 fusion.150
  667.7 2.7 fusion.150
  671.1 2.7 fusion.150
  674.6 2.7 fusion.150
  678.0 2.7 fusion.150
  681.4 2.7 fusion.150
  684.8 2.7 fusion.150
  688.2 2.7 fusion.150
  691.7 2.7 fusion.150
  695.1 2.7 fusion.150
  698.5 2.7 fusion.150
  701.9 2.7 fusion.150
  706.9 3.4 convolution_bitcast_fusion.4
  711.9 67.6 %all-gather.13.cloned.1.call-done = f32[512,64,128]{2,1,0:T(8,128)} async-done(((f32[32,64,128]{2,1,0:T(8,128)}), f32[512,64,128]{2,1,0:T(8,128)}) %all-gather.13.cloned.1.call-update) | async-done | bytes 16777232 | tf_op jit(solution)/shard_map/all_gather | solution.py:17
  779.5 35.0 %while.49 = (s32[]{:T(128)}, f32[32,64,128]{2,1,0:T(8,128)S(1)}, s32[]{:T(128)}, f32[16,32]{1,0:T(8,128)}, f32[16,32,64,128]{3,2,1,0:T(8,128)}, /*index=5*/s32[]{:T(128)}, s32[]{:T(128)}, s32[]{:T(128)}, s32[]{:T(128)}) while((s32[]{:T(128)}, f32[32,64,128]{2,1,0:T(8,128)S(1)}, s32[]{:T(128)}, f32[16,32]{1,0:T(8,128)}, ...), condition=%wide.region_7.8_spmd.clone, body=%wide.region_6.7_spmd.clone.sunk | while | flops 1048584 | bytes 3146279 | solution.py:30
  817.1 1.8 convolution_bitcast_fusion.7
  824.1 2.9 fusion.48
  (317 shorter events, 131.1 us)
Async XLA Ops:
  7.2 397.4 %copy-start = (bf16[1,128,128]{2,1,0:T(8,128)(2,1)S(1)}, bf16[1,128,128]{2,1,0:T(8,128)(2,1)}, u32[]{:S(2)}) copy-start(bf16[1,128,128]{2,1,0:T(8,128)(2,1)} %param.25) | copy-start | bytes 98308
  7.2 2.8 copy-start.24
  7.2 183.9 %all-gather.15.cloned.1.call-start = ((), (), s32[]{:S(2)}) async-start(), calls=%async_computation.4 | async-start | bytes 17825792 | tf_op jit(solution)/shard_map/all_gather | solution.py:17
  9.9 436.4 %copy-start.2 = (bf16[1,128,2048]{1,2,0:T(8,128)(2,1)}, bf16[1,128,2048]{1,2,0:T(8,128)(2,1)S(1)}, u32[]{:S(2)}) copy-start(bf16[1,128,2048]{1,2,0:T(8,128)(2,1)S(1)} %copy.294) | copy-start | bytes 1572868
  9.9 1.8 copy-start.25
  10.0 2.1 copy-start.16
  11.6 354.4 %all-gather.11.cloned.1.call-start = ((), (), s32[]{:S(2)}) async-start(), calls=%async_computation.2 | async-start | bytes 17825792 | tf_op jit(solution)/shard_map/all_gather | solution.py:17
  12.1 0.8 copy-start.22
  12.4 2.1 copy-start.6
  12.5 2.0 copy-start.9
  12.5 2.1 copy-start.26
  12.5 2.2 copy-start.54
  12.5 50.5 %copy-start.48 = (s32[128]{0:T(128)S(1)}, s32[128]{0:T(128)}, u32[]{:S(2)}) copy-start(s32[128]{0:T(128)} %param.29) | copy-start | bytes 1540
  12.6 50.6 %copy-start.51 = (s32[128]{0:T(128)S(1)}, s32[128]{0:T(128)}, u32[]{:S(2)}) copy-start(s32[128]{0:T(128)} %param.30) | copy-start | bytes 1540
  12.6 51.3 %copy-start.23 = (bf16[1,128,128]{2,1,0:T(8,128)(2,1)S(1)}, bf16[1,128,128]{2,1,0:T(8,128)(2,1)}, u32[]{:S(2)}) copy-start(bf16[1,128,128]{2,1,0:T(8,128)(2,1)} %param.22) | copy-start | bytes 98308
  63.1 152.9 %copy-start.34 = (f32[32,128]{1,0:T(8,128)}, f32[32,128]{1,0:T(8,128)S(1)}, u32[]{:S(2)}) copy-start(f32[32,128]{1,0:T(8,128)S(1)} %copy.291) | copy-start | bytes 49156
  63.6 362.1 %copy-start.43 = (pred[128,128]{1,0:T(8,128)(4,1)}, pred[128,128]{1,0:T(8,128)(4,1)S(1)}, u32[]{:S(2)}) copy-start(pred[128,128]{1,0:T(8,128)(4,1)S(1)} %iota_compare_fusion) | copy-start | bytes 49156
  64.0 152.0 %copy-start.27 = (f32[128,128]{1,0:T(8,128)}, f32[128,128]{1,0:T(8,128)S(1)}, u32[]{:S(2)}) copy-start(f32[128,128]{1,0:T(8,128)S(1)} %fusion.93) | copy-start | bytes 196612
  215.3 0.6 copy-start.45
  215.3 1.6 copy-start.53
  215.9 1.0 copy-start.17
  231.8 158.5 %all-to-all-start.1 = ((bf16[16,2,4,2048]{3,2,1,0:T(4,128)(2,1)}), bf16[16,2,4,2048]{3,2,1,0:T(4,128)(2,1)S(1)}, u32[]{:S(2)}, u32[]{:S(2)}) async-start(bf16[16,2,4,2048]{3,2,1,0:T(4,128)(2,1)} %bitcast.265), calls=%async_computation.1 | async-start | bytes 1048576 | tf_op jit(solution)/shard_map/all_to_all | solution.py:110
  235.4 414.5 %all-gather.17.cloned.1.call-start = ((), (), s32[]{:S(2)}) async-start(), calls=%async_computation.5 | async-start | bytes 17825792 | tf_op jit(solution)/shard_map/all_gather | solution.py:17
  390.3 9.2 %copy-start.46 = (f32[16,32]{1,0:T(8,128)}, f32[16,32]{1,0:T(8,128)S(1)}, u32[]{:S(2)}) copy-start(f32[16,32]{1,0:T(8,128)S(1)} %get-tuple-element.1568) | copy-start | bytes 6148
  390.8 0.8 copy-start.14
  399.5 0.8 copy-start.13
  404.6 6.3 copy-start.10
  420.3 5.4 copy-start.52
  425.5 4.5 copy-start.41
  425.7 4.4 copy-start.30
  442.0 24.1 %all-to-all-start = ((bf16[2,16,4,2048]{3,0,2,1:T(2,128)(2,1)}), bf16[2,16,4,2048]{3,0,2,1:T(2,128)(2,1)S(1)}, u32[]{:S(2)}, u32[]{:S(2)}) async-start(bf16[2,16,4,2048]{3,0,2,1:T(2,128)(2,1)} %bitcast.267), calls=%async_computation | async-start | bytes 1048576 | tf_op jit(solution)/shard_map/all_to_all | solution.py:126
  446.3 333.2 %all-gather.13.cloned.1.call-start = ((), (), s32[]{:S(2)}) async-start(), calls=%async_computation.3 | async-start | bytes 17825792 | tf_op jit(solution)/shard_map/all_gather | solution.py:17
  471.9 2.7 copy-start.15
  473.8 0.8 copy-start.12
  479.5 1.7 copy-start.4
  638.3 1.9 copy-start.7
  638.3 1.9 copy-start.11
  638.3 1.9 copy-start.28
  638.3 1.9 copy-start.31
  638.3 1.9 copy-start.35
  638.3 1.9 copy-start.42
  638.3 1.9 copy-start.44
  640.2 6.4 copy-start.5
  645.7 3.5 copy-start.18
  645.7 3.5 copy-start.19
  645.7 3.7 copy-start.49
  645.7 3.7 copy-start.50
  706.2 4.9 copy-start.1
  706.9 4.2 copy-start.8
  706.9 4.9 copy-start.32
  706.9 4.9 copy-start.33
  814.4 1.0 copy-start.3
  815.5 3.5 copy-start.47
  815.5 3.9 copy-start.37
  815.5 3.9 copy-start.38
  815.5 3.9 copy-start.39
  815.5 3.9 copy-start.40
  817.1 7.0 copy-start.20
  817.1 7.0 copy-start.21
  817.1 7.0 copy-start.29
  817.1 7.0 copy-start.36
Sparse Core Ops, SparseCore 0:
  11.8 179.2 all-gather.14
  193.8 172.2 all-gather.10
  425.6 182.1 all-gather.16
  610.4 169.0 all-gather.12
where the time goes:
time: 846 us; the launch traced here: 835 us
  waiting for transfers between devices  339 us (40%)
  blocking collectives  189 us (22%)
  other arithmetic  132 us (16%)
  local copies, waits for them, and re-layouts  104 us (12%)
  matrix products  45.2 us (5%)
  between operations  15.5 us (2%)
    all_gather x4, waiting for transfers between devices, entering_2(): everything = jax.tree.map(lambda part: lax.all_gather(part, axis), array)  325 us
    psum x1, blocking collectives, on_device(): skip_sums = lax.psum((grads_one[4], grads_two[4]), ('dp', 'seq'))  143 us
    select_n x64, other arithmetic, lap(): return jax.tree.map(lambda a, b: jnp.where(reached, a, b), new, before)  114 us
    unnamed x1, blocking collectives  46.7 us
    mul x64, local copies, waits for them, and re-layouts, combine(): later[0][:, None, None] * earlier[1] + later[1]  22.4 us
    dot_general x5, matrix products, group_step(): outputs = jnp.einsum('hts,shp->thp', weights, inputs, precision=highest)  17.2 us
  transfers between devices with their start and end apart: 6, of which 4 were waited for; matrix products, arithmetic and copies ran while one was open for 23% of the time, Pallas kernels for 0%

commit v1 on v0

v1 whole, which is shorter than its diff:
```python
import functools
import math

import jax
import jax.numpy as jnp
from jax import lax
from jax.experimental import pallas as pl
from jax.experimental.pallas import tpu as pltpu
from jax.sharding import Mesh
from jax.sharding import PartitionSpec as P

COLS = 32
ROWS = 64
BLOCK = 128
HALF = 64
LANES = 128
PART_ROWS = 784
SHARED_ROWS = 528
SEND_ROWS = 2 * PART_ROWS + SHARED_ROWS
OUT_ROWS = 784
BACK_ROWS = 1088

f32 = jnp.float32
bf16 = jnp.bfloat16


def nn(a, b):
    return lax.dot_general(a, b, (((1,), (0,)), ((), ())), preferred_element_type=f32)


def nt(a, b):
    return lax.dot_general(a, b, (((1,), (1,)), ((), ())), preferred_element_type=f32)


def tn(a, b):
    return lax.dot_general(a, b, (((0,), (0,)), ((), ())), preferred_element_type=f32)


def down(*values):
    return jnp.concatenate(values, axis=0)


def across(*values):
    return jnp.concatenate(values, axis=1)


def parts(values):
    hi = values.astype(bf16)
    return hi, (values - hi.astype(f32)).astype(bf16)


def iota(dim):
    return lax.broadcasted_iota(jnp.int32, (BLOCK, BLOCK), dim)


def one_where(cond):
    return jnp.where(cond, f32(1.0), f32(0.0))


def constants():
    row, col = iota(0), iota(1)
    lower = one_where(col <= row)
    before = one_where(row < col)
    after = one_where(row > col).astype(bf16)
    head_a = one_where(col < HALF)
    head_b = 1.0 - head_a
    wide_a, wide_b = across(after, head_a.astype(bf16)), across(after, head_b.astype(bf16))
    head_a, head_b = head_a.astype(bf16), head_b.astype(bf16)
    return {
        "lower": lower,
        "head_a": head_a,
        "head_b": head_b,
        "heads": down(head_a, head_a, head_b, head_b),
        "spread_a": down(wide_a, wide_a),
        "spread_b": down(wide_b, wide_b),
        "lower_bf": lower.astype(bf16),
        "before": before,
        "sums": down(lower, before, jnp.ones((BLOCK, BLOCK), f32)).astype(bf16),
        "same": one_where(row == col),
        "mirror_row": one_where(row + col == 2 * (row - row % COLS) + COLS - 1),
        "mirror_col": one_where(row + col == 2 * (row - row % ROWS) + ROWS - 1),
    }


def masked_decays(c, tok_ref, b, layer, group):
    small = tok_ref[b, 768:784, :].astype(f32)
    at = 4 * layer + 2 * group

    def one(k):
        return across(
            (c["lower"] * small[at + k : at + k + 1]).astype(bf16),
            (c["lower"] * small[8 + at + k : 9 + at + k]).astype(bf16),
        )

    return one(0), one(1)


def scales(running):
    total = running[BLOCK - 1 : BLOCK, :]
    return jnp.exp(running), jnp.exp(total - running), jnp.exp(total)


def decay_scales(c, tok_ref, b, layer, group):
    a, h = masked_decays(c, tok_ref, b, layer, group)
    return scales(nn(across(a, h), c["heads"]))


def decay_block(c, tok_ref, b, layer, group):
    a, h = masked_decays(c, tok_ref, b, layer, group)
    a, h = nn(a, c["spread_a"]), nn(h, c["spread_b"])
    decay_a = jnp.exp(a[:, :BLOCK]) * c["lower"]
    decay_b = jnp.exp(h[:, :BLOCK]) * c["lower"]
    return (decay_a, decay_b, *scales(a[:, BLOCK:] + h[:, BLOCK:]))


def by_head(c, values):
    return down(values * c["head_a"], values * c["head_b"])


def mirror(c, sh_ref, b, layer):
    flags = sh_ref[b, 512:528, :].astype(f32)[layer : layer + 1]
    turned = c["mirror_col"] if layer else c["mirror_row"]
    return (flags * turned + (1.0 - flags) * c["same"]).astype(bf16)


def vectors(sh_ref, b, layer):
    at = 256 * layer
    return sh_ref[b, at : at + 128, :], sh_ref[b, at + 128 : at + 256, :]


def inputs_of(tok_ref, b, group):
    return tok_ref[b, 128 * group : 128 * group + 128, :]


def cotangent_of(tok_ref, b, group):
    at = 256 + 128 * group
    return tok_ref[b, at : at + 128, :], tok_ref[b, at + 256 : at + 384, :]


def pack_kernel(u_ref, cot_ref, decay_ref, w1, r1, w2, r2, flags_ref, out_ref):
    for dest in range(8):
        x, core = dest // 2, dest % 2
        at = core * PART_ROWS
        for group in range(2):
            lanes = slice((2 * dest + group) * LANES, (2 * dest + group + 1) * LANES)
            row = at + 128 * group
            out_ref[x, row : row + 128, :] = u_ref[:, lanes]
            hi, lo = parts(cot_ref[:, lanes])
            out_ref[x, row + 256 : row + 384, :] = hi
            out_ref[x, row + 512 : row + 640, :] = lo
        decays = down(*(decay_ref[layer, 4 * dest : 4 * dest + 4, :] for layer in range(2)))
        hi, lo = parts(decays)
        out_ref[x, at + 768 : at + 784, :] = down(hi.astype(f32), lo.astype(f32)).astype(bf16)
    for x in range(4):
        at = 2 * PART_ROWS
        for k, ref in enumerate((w1, r1, w2, r2)):
            out_ref[x, at + 128 * k : at + 128 * (k + 1), :] = ref[...]
        out_ref[x, at + 512 : at + 528, :] = flags_ref[...]


def update(c, scale, carry, vector, values):
    return scale * carry + tn(down(vector, vector), down(*parts(values)))


def gather_kernel(place_ref, own_ref, other_ref, tok_ref, sh_ref, ends_ref, s_ref, a_ref):
    z, core = place_ref[0], place_ref[2]
    for x in range(4):
        start = pl.multiple_of(core * PART_ROWS, 16)
        tok_ref[2 * x + core] = own_ref[x, pl.ds(start, PART_ROWS), :]
        tok_ref[2 * x + 1 - core] = other_ref[x, 0:PART_ROWS, :]
        sh_ref[2 * x + core] = own_ref[x, 2 * PART_ROWS :, :]
        sh_ref[2 * x + 1 - core] = other_ref[x, PART_ROWS:, :]
    c = constants()
    s_ref[...] = jnp.zeros_like(s_ref)
    a_ref[...] = jnp.zeros_like(a_ref)

    def step(i, _):
        b = i
        writes, _reads = vectors(sh_ref, b, 0)
        for group in range(2):
            _grown, left, total = decay_scales(c, tok_ref, b, 0, group)
            u = inputs_of(tok_ref, b, group).astype(f32)
            s_ref[group] = update(c, total, s_ref[group], writes, u * left)
        b = 7 - i
        _writes, reads = vectors(sh_ref, b, 1)
        for group in range(2):
            grown, _left, total = decay_scales(c, tok_ref, b, 1, group)
            hi, lo = cotangent_of(tok_ref, b, group)
            dy = hi.astype(f32) + lo.astype(f32)
            a_ref[group] = update(c, total, a_ref[group], reads, dy * grown)
        return 0

    lax.fori_loop(0, 8, step, 0)
    ends_ref[...] = jnp.where(z == 0, s_ref[...], a_ref[...])


def first_kernel(
    place_ref, tok_ref, sh_ref, skip_ref, ends_ref, keep_ref, send_ref, state_ref, adjoint_ref, s_ref, a_ref
):
    z = place_ref[0]
    c = constants()
    s_ref[...] = jnp.where(z == 1, ends_ref[...], 0.0)
    a_ref[...] = jnp.where(z == 0, ends_ref[...], 0.0)

    def step(i, _):
        b = i
        writes, reads = vectors(sh_ref, b, 0)
        scores = nt(reads, writes)
        turn = mirror(c, sh_ref, b, 0)
        for group in range(2):
            decay_a, decay_b, grown, left, total = decay_block(c, tok_ref, b, 0, group)
            u = inputs_of(tok_ref, b, group)
            mixed = across(*parts(across(decay_a * scores, decay_b * scores)))
            state = s_ref[group]
            state_both = down(*parts(state))
            state_ref[b, group] = state_both
            u32 = u.astype(f32)
            heads = by_head(c, u)
            y = (
                nn(mixed, down(heads, heads))
                + grown * nn(across(reads, reads), state_both)
                + skip_ref[group : group + 1, :] * u32
            )
            s_ref[group] = update(c, total, state, writes, u32 * left)
            grid = nn(turn, y.astype(bf16)).astype(bf16)
            for k in range(4):
                near, far = grid[32 * k : 32 * k + 16], grid[32 * k + 16 : 32 * k + 32]
                at = pl.multiple_of(64 * b + 16 * k, 16)
                keep_ref[0, group, pl.ds(at, 16), :] = jnp.where(z == 0, near, far)
                send_ref[0, group, pl.ds(at, 16), :] = jnp.where(z == 0, far, near)

        b = 7 - i
        writes, reads = vectors(sh_ref, b, 1)
        scores = nt(reads, writes)
        turn = mirror(c, sh_ref, b, 1)
        for group in range(2):
            decay_a, decay_b, grown, left, total = decay_block(c, tok_ref, b, 1, group)
            hi, lo = cotangent_of(tok_ref, b, group)
            mixed, mixed_low = parts(down(decay_a * scores, decay_b * scores))
            adjoint = a_ref[group]
            adjoint_both = down(*parts(adjoint))
            adjoint_ref[b, group] = adjoint_both
            dy = hi.astype(f32) + lo.astype(f32)
            hi_heads, lo_heads = by_head(c, hi), by_head(c, lo)
            du = (
                tn(down(mixed, mixed_low, mixed), down(hi_heads, hi_heads, lo_heads))
                + left * nn(across(writes, writes), adjoint_both)
                + skip_ref[2 + group : 3 + group, :] * dy
            )
            a_ref[group] = update(c, total, adjoint, reads, dy * grown)
            grid = nn(turn, du.astype(bf16)).astype(bf16)
            for k in range(2):
                near, far = grid[64 * k : 64 * k + 32], grid[64 * k + 32 : 64 * k + 64]
                at = pl.multiple_of(64 * b + 32 * k, 32)
                keep_ref[1, group, pl.ds(at, 32), :] = jnp.where(z == 0, near, far)
                send_ref[1, group, pl.ds(at, 32), :] = jnp.where(z == 0, far, near)
        return 0

    lax.fori_loop(0, 8, step, 0)


def regrid_kernel(
    place_ref, tok_ref, sh_ref, keep_ref, got_ref, u2_ref, dy1_ref, ends_ref, skip_ref, grid_ref, s_ref, a_ref
):
    z = place_ref[0]
    c = constants()
    grid_ref[z] = keep_ref[...].astype(f32)
    grid_ref[1 - z] = got_ref[...].astype(f32)
    s_ref[...] = jnp.zeros_like(s_ref)
    a_ref[...] = jnp.zeros_like(a_ref)
    skip_ref[...] = jnp.zeros_like(skip_ref)

    def step(i, _):
        b = i
        writes, _reads = vectors(sh_ref, b, 1)
        turn = mirror(c, sh_ref, b, 1)
        for group in range(2):
            picked = down(
                *(
                    grid_ref[part, 0, group, pl.ds(2 * b + k, 32, stride=16), :]
                    for k in range(2)
                    for part in range(2)
                )
            )
            u32 = nn(turn, picked.astype(bf16))
            u2_ref[b, group] = u32.astype(bf16)
            _grown, left, total = decay_scales(c, tok_ref, b, 1, group)
            s_ref[group] = update(c, total, s_ref[group], writes, u32 * left)
            hi, lo = cotangent_of(tok_ref, b, group)
            dy = hi.astype(f32) + lo.astype(f32)
            skip_ref[2 + group : 3 + group, :] += jnp.sum(u32 * dy, axis=0, keepdims=True)
        b = 7 - i
        _writes, reads = vectors(sh_ref, b, 0)
        turn = mirror(c, sh_ref, b, 0)
        for group in range(2):
            picked = down(
                *(
                    grid_ref[part, 1, group, pl.ds(4 * b + k, 16, stride=32), :]
                    for k in range(4)
                    for part in range(2)
                )
            )
            dy = nn(turn, picked.astype(bf16))
            dy1_ref[b, group] = dy.astype(bf16)
            grown, _left, total = decay_scales(c, tok_ref, b, 0, group)
            a_ref[group] = update(c, total, a_ref[group], reads, dy * grown)
            u = inputs_of(tok_ref, b, group).astype(f32)
            skip_ref[group : group + 1, :] += jnp.sum(u * dy, axis=0, keepdims=True)
        return 0

    lax.fori_loop(0, 8, step, 0)
    ends_ref[...] = jnp.where(z == 0, s_ref[...], a_ref[...])


def block_gradients(c, tok_ref, sh_ref, b, layer, u_of, dy_of, state_of, adjoint_of):
    writes, reads = vectors(sh_ref, b, layer)
    reads_two, writes_two = down(reads, reads), down(writes, writes)
    scores = nt(reads, writes)
    d_scores, d_writes, d_reads = 0.0, 0.0, 0.0
    decay_rows, kept = [], []
    for group in range(2):
        decay_a, decay_b, grown, left, total = decay_block(c, tok_ref, b, layer, group)
        u, (dy, dy_low) = u_of(group), dy_of(group)
        u32, dy32 = u.astype(f32), dy.astype(f32)
        dy_heads = by_head(c, dy)
        if dy_low is None:
            pairs = nt(dy_heads, u)
        else:
            pairs = nt(across(dy_heads, by_head(c, dy_low)), across(u, u))
            dy32 = dy32 + dy_low.astype(f32)
        pair_a, pair_b = decay_a * pairs[:BLOCK], decay_b * pairs[BLOCK:]
        d_scores = d_scores + pair_a + pair_b
        u_left, dy_grown = u32 * left, dy32 * grown
        u_hi, u_lo = parts(u_left)
        dy_hi, dy_lo = parts(dy_grown)
        state, adjoint = state_of(group), adjoint_of(group)
        read_state = nn(across(reads, reads), state)
        write_adjoint = nn(across(writes, writes), adjoint)
        state_hi, adjoint_hi = state[:LANES], adjoint[:LANES]
        d_writes = (
            d_writes
            + nt(across(u_hi, u_lo), across(adjoint_hi, adjoint_hi))
            + nt(u_hi, adjoint[LANES:])
        )
        d_reads = (
            d_reads
            + nt(across(dy_hi, dy_lo), across(state_hi, state_hi))
            + nt(dy_hi, state[LANES:])
        )
        crossing = across((pair_a * scores).astype(bf16), (pair_b * scores).astype(bf16))
        inner = tn(crossing, c["lower_bf"])
        products = down(
            (dy_grown * read_state).astype(bf16),
            (u_left * write_adjoint).astype(bf16),
            (total * (state_hi.astype(f32) * adjoint_hi.astype(f32))).astype(bf16),
        )
        outer = tn(products, c["sums"])
        for k in range(2):
            decay_rows.append(
                jnp.sum(c["before"] * inner[BLOCK * k : BLOCK * (k + 1)], axis=0, keepdims=True)
                + jnp.sum(outer[HALF * k : HALF * (k + 1)], axis=0, keepdims=True)
            )
        kept.append(
            {
                "total": total,
                "left": left,
                "u_left": down(u_hi, u_lo),
                "dy_grown": down(dy_hi, dy_lo),
                "write_adjoint": write_adjoint,
                "dy_heads": dy_heads,
                "dy": dy32,
                "mixed": lambda a=decay_a, h=decay_b: down(
                    (a * scores).astype(bf16), (h * scores).astype(bf16)
                ),
            }
        )
    low = parts(d_scores)
    d_writes = d_writes + tn(down(*low), reads_two)
    d_reads = d_reads + nn(across(*low), writes_two)
    return d_writes, d_reads, down(*decay_rows), kept, writes_two, reads_two


def second_kernel(
    place_ref,
    tok_ref,
    sh_ref,
    skip_ref,
    u2_ref,
    dy1_ref,
    state_ref,
    adjoint_ref,
    ends_ref,
    out_ref,
    s_ref,
    a_ref,
):
    z, core = place_ref[0], place_ref[2]
    c = constants()
    s_ref[...] = jnp.where(z == 1, ends_ref[...], 0.0)
    a_ref[...] = jnp.where(z == 0, ends_ref[...], 0.0)

    def put(b, layer, d_writes, d_reads, decay_rows):
        slot, x = jnp.bitwise_xor(b % 2, core), b // 2
        at = 256 + 256 * layer
        out_ref[slot, x, at : at + 128, :] = d_writes.astype(bf16)
        out_ref[slot, x, at + 128 : at + 256, :] = d_reads.astype(bf16)
        return decay_rows

    def step(i, _):
        b = i
        d_writes, d_reads, rows, kept, writes_two, _ = block_gradients(
            c,
            tok_ref,
            sh_ref,
            b,
            1,
            lambda g: u2_ref[b, g],
            lambda g: cotangent_of(tok_ref, b, g),
            lambda g: down(*parts(s_ref[g])),
            lambda g: adjoint_ref[b, g],
        )
        put(b, 1, d_writes, d_reads, rows)
        decay_ref_rows(out_ref, b, core, 1, rows)
        for group in range(2):
            k = kept[group]
            s_ref[group] = k["total"] * s_ref[group] + tn(writes_two, k["u_left"])
        r = 7 - i
        d_writes, d_reads, rows, kept, _, reads_two = block_gradients(
            c,
            tok_ref,
            sh_ref,
            r,
            0,
            lambda g: inputs_of(tok_ref, r, g),
            lambda g: (dy1_ref[r, g], None),
            lambda g: state_ref[r, g],
            lambda g: down(*parts(a_ref[g])),
        )
        put(r, 0, d_writes, d_reads, rows)
        decay_ref_rows(out_ref, r, core, 0, rows)
        for group in range(2):
            k = kept[group]
            du = (
                tn(k["mixed"](), k["dy_heads"])
                + k["left"] * k["write_adjoint"]
                + skip_ref[group : group + 1, :] * k["dy"]
            )
            slot = jnp.bitwise_xor(r % 2, core)
            out_ref[slot, r // 2, 128 * group : 128 * group + 128, :] = du.astype(bf16)
            a_ref[group] = k["total"] * a_ref[group] + tn(reads_two, k["dy_grown"])
        return 0

    lax.fori_loop(0, 8, step, 0)


def decay_ref_rows(out_ref, b, core, layer, rows):
    hi, lo = parts(rows)
    slot = jnp.bitwise_xor(b % 2, core)
    at = 768 + 8 * layer
    both = down(hi.astype(f32), lo.astype(f32)).astype(bf16)
    out_ref[slot, b // 2, at : at + 8, :] = both


def pair_kernel(own_ref, other_ref, skip_ref, skip_other_ref, out_ref):
    pieces = []
    for ref in (skip_ref, skip_other_ref):
        total = ref[0:4, :]
        hi, rest = parts(total)
        rest = total - hi.astype(f32)
        mid, low = parts(rest)
        pieces.append(down(hi.astype(f32), mid.astype(f32), low.astype(f32), jnp.zeros((4, LANES), f32)))
    skips = down(*pieces).astype(bf16)
    for x in range(4):
        out_ref[x, 0:256, :] = own_ref[x, 0:256, :]
        out_ref[x, 256:512, :] = other_ref[x, 0:256, :]
        out_ref[x, 512:1024, :] = (
            own_ref[x, 256:768, :].astype(f32) + other_ref[x, 256:768, :].astype(f32)
        ).astype(bf16)
        out_ref[x, 1024:1040, :] = own_ref[x, 768:784, :]
        out_ref[x, 1040:1056, :] = other_ref[x, 768:784, :]
        out_ref[x, 1056:1088, :] = skips


def last_kernel(place_ref, back_ref, grad_ref, w1, r1, w2, r2, decay1_ref, decay2_ref, skip_ref):
    core = place_ref[2]
    for x in range(4):
        for owner in range(2):
            for group in range(2):
                near = back_ref[x, 128 * group : 128 * group + 128, :]
                far = back_ref[x, 256 + 128 * group : 384 + 128 * group, :]
                at = ((2 * x + owner) * 2 + group) * LANES
                grad_ref[:, at : at + LANES] = jnp.where(core == owner, near, far)
            near = back_ref[x, 1024:1040, :].astype(f32)
            far = back_ref[x, 1040:1056, :].astype(f32)
            small = jnp.where(core == owner, near, far)
            at = (2 * x + owner) * 4
            decay1_ref[at : at + 4, :] = small[0:4] + small[4:8]
            decay2_ref[at : at + 4, :] = small[8:12] + small[12:16]
            near = back_ref[x, 1056:1072, :].astype(f32)
            far = back_ref[x, 1072:1088, :].astype(f32)
            small = jnp.where(core == owner, near, far)
            skip_ref[at : at + 4, :] = small[0:4] + small[4:8] + small[8:12]
    for k, ref in enumerate((w1, r1, w2, r2)):
        rows = slice(512 + 128 * k, 640 + 128 * k)
        total = back_ref[0, rows, :].astype(f32)
        for x in range(1, 4):
            total = total + back_ref[x, rows, :].astype(f32)
        ref[...] = total.astype(bf16)


def call(kernel, outs, scratch, *args, scalars=1):
    shapes = [jax.ShapeDtypeStruct(s, d) for s, d in outs]
    many = len(shapes) > 1
    in_specs = [pl.BlockSpec(memory_space=pltpu.SMEM)] * scalars
    in_specs += [pl.BlockSpec(memory_space=pltpu.VMEM)] * (len(args) - scalars)
    return pl.pallas_call(
        kernel,
        out_shape=shapes if many else shapes[0],
        in_specs=in_specs,
        out_specs=[pl.BlockSpec(memory_space=pltpu.VMEM)] * len(shapes)
        if many
        else pl.BlockSpec(memory_space=pltpu.VMEM),
        scratch_shapes=[pltpu.VMEM(s, d) for s, d in scratch],
        compiler_params=pltpu.CompilerParams(vmem_limit_bytes=40 * 2**20),
        name=kernel.__name__,
    )(*args)


def swap(values, axis):
    return lax.ppermute(values, axis, [(0, 1), (1, 0)])


def on_device(
    layer_input,
    writes_first,
    reads_first,
    decay_first,
    skip_first,
    writes_second,
    reads_second,
    decay_second,
    skip_second,
    order_first,
    order_second,
    cotangent,
):
    length, features = layer_input.shape[1:]
    head_count = skip_first.shape[0]
    head_size = features // head_count
    z, x, core = (lax.axis_index(a) for a in ("z", "x", "core"))
    place = jnp.stack([z, x, core]).astype(jnp.int32)

    row_flip = order_first.reshape(-1, COLS)[:, :1] % COLS != 0
    col_flip = order_second.reshape(-1, ROWS)[:, :1] // COLS != 0
    flags = jnp.concatenate(
        [
            jnp.broadcast_to(row_flip, (length // COLS, COLS)).reshape(1, length),
            jnp.broadcast_to(col_flip, (length // ROWS, ROWS)).reshape(1, length),
            jnp.zeros((14, length), bool),
        ]
    ).astype(bf16)
    packed = call(
        pack_kernel,
        [((4, SEND_ROWS, LANES), bf16)],
        [],
        layer_input[0],
        cotangent[0],
        jnp.stack([decay_first[0], decay_second[0]]),
        writes_first[0],
        reads_first[0],
        writes_second[0],
        reads_second[0],
        flags,
        scalars=0,
    )
    own = lax.all_to_all(packed, "x", split_axis=0, concat_axis=0, tiled=True)
    theirs = lax.dynamic_slice_in_dim(own, (1 - core) * PART_ROWS, PART_ROWS, axis=1)
    other = swap(jnp.concatenate([theirs, own[:, 2 * PART_ROWS :]], axis=1), "core")

    skips = jnp.stack([skip_first, skip_second])
    skips = lax.dynamic_slice_in_dim(skips, 4 * (2 * x + core), 4, axis=1)
    skips = jnp.repeat(skips, head_size, axis=1).reshape(4, LANES)
    skips = jnp.concatenate([skips, jnp.zeros((4, LANES), f32)], axis=0)

    carry = ((2, LANES, LANES), f32)
    saved = ((8, 2, 2 * LANES, LANES), bf16)
    half_grid = ((2, 2, 512, LANES), bf16)
    tok, sh, ends = call(
        gather_kernel,
        [((8, PART_ROWS, LANES), bf16), ((8, SHARED_ROWS, LANES), bf16), carry],
        [carry, carry],
        place,
        own,
        other,
    )
    ends = swap(ends, "z")
    keep, send, states, adjoints = call(
        first_kernel, [half_grid, half_grid, saved, saved], [carry, carry], place, tok, sh, skips, ends
    )
    got = swap(send, "z")
    block = ((8, 2, BLOCK, LANES), bf16)
    u2, dy1, ends, skip_sums = call(
        regrid_kernel,
        [block, block, carry, ((8, LANES), f32)],
        [((2, 2, 2, 512, LANES), f32), carry, carry],
        place,
        tok,
        sh,
        keep,
        got,
    )
    ends = swap(ends, "z")
    others = lax.axis_size("dp") * lax.axis_size("z")
    skip_sums = jnp.broadcast_to(skip_sums[None], (others, 8, LANES))
    skip_sums = lax.all_to_all(skip_sums, ("dp", "z"), split_axis=0, concat_axis=0, tiled=True)
    skip_sums = skip_sums.sum(0)
    skip_other = swap(skip_sums, "core")
    out = call(
        second_kernel,
        [((2, 4, OUT_ROWS, LANES), bf16)],
        [carry, carry],
        place,
        tok,
        sh,
        skips,
        u2,
        dy1,
        states,
        adjoints,
        ends,
    )
    from_other = swap(out[1], "core")
    back = call(
        pair_kernel,
        [((4, BACK_ROWS, LANES), bf16)],
        [],
        out[0],
        from_other,
        skip_sums,
        skip_other,
        scalars=0,
    )
    back = lax.all_to_all(back, "x", split_axis=0, concat_axis=0, tiled=True)
    vector = ((length, LANES), bf16)
    decay = ((head_count, length), f32)
    grad_input, w1, r1, w2, r2, decay1, decay2, skip_lanes = call(
        last_kernel,
        [((length, features), bf16), vector, vector, vector, vector, decay, decay, ((head_count, LANES), f32)],
        [],
        place,
        back,
    )
    seq_count = lax.axis_size("z") * lax.axis_size("x") * lax.axis_size("core")
    factor = 1.0 / math.sqrt(lax.axis_size("dp") * seq_count * length * head_size)
    skip_grads = skip_lanes.reshape(8, 2, 2, 2, head_size).sum(-1)
    skip_grads = skip_grads.transpose(1, 0, 2, 3).reshape(2, head_count) * factor
    return (
        grad_input[None],
        w1[None],
        r1[None],
        decay1[None],
        skip_grads[0],
        w2[None],
        r2[None],
        decay2[None],
        skip_grads[1],
    )


def solution(mesh):
    clips = mesh.devices.shape[0]
    finer = Mesh(mesh.devices.reshape(clips, 2, 4, 2), ("dp", "z", "x", "core"))
    seq = ("z", "x", "core")
    by_token, by_decay = P("dp", seq, None), P("dp", None, seq)
    return jax.shard_map(
        on_device,
        mesh=finer,
        in_specs=(
            by_token,
            by_token,
            by_token,
            by_decay,
            P(),
            by_token,
            by_token,
            by_decay,
            P(),
            P(seq),
            P(seq),
            by_token,
        ),
        out_specs=(
            by_token,
            by_token,
            by_token,
            by_decay,
            P(),
            by_token,
            by_token,
            by_decay,
            P(),
        ),
        check_vma=False,
    )
```

time: 846 us -> 192 us (0.23); the launches traced: 835 us -> 191 us
  waiting for transfers between devices: 339 us -> 49.3 us
  blocking collectives: 189 us -> 49.7 us
  other arithmetic: 132 us -> 2.49 us
  local copies, waits for them, and re-layouts: 104 us -> 12.9 us
  Pallas kernels: 0 us -> 48.6 us
  matrix products: 45.2 us -> 0 us
  starting transfers between devices: 8.33 us -> 27.6 us
  between operations: 15.5 us -> 0.78 us
    all_gather x4 -> x0, waiting for transfers between devices: 325 us -> none  [entering_2(): everything = jax.tree.map(lambda part: lax.all_gather(part, axis), array)]
    psum x1 -> x0, blocking collectives: 143 us -> none  [on_device(): skip_sums = lax.psum((grads_one[4], grads_two[4]), ('dp', 'seq'))]
    select_n x66 -> x0, other arithmetic: 116 us -> none  [the longest x64 114 us: lap(): return jax.tree.map(lambda a, b: jnp.where(reached, a, b), new, before)]
    all_to_all x0 -> x2, blocking collectives: none -> 49.7 us  [the longest x1 32 us: on_device(): lax.all_to_all(skip_sums, ('dp', 'z'), split_axis=0, concat_axis=0, tiled...]
    pallas_call x0 -> x7, Pallas kernels: none -> 48.6 us  [call(): pl.pallas_call(kernel, out_shape=shapes if many else shapes[0], in_specs=...]
    unnamed x1 -> x0, blocking collectives: 46.7 us -> none
    dot_general x23 -> x0, matrix products: 45.2 us -> none  [the longest x5 17.2 us: group_step(): outputs = jnp.einsum('hts,shp->thp', weights, inputs, precision=highest)]
    mul x72 -> x0, local copies, waits for them, and re-layouts: 43.5 us -> none  [the longest x64 22.4 us: combine(): later[0][:, None, None] * earlier[1] + later[1]]
  transfers between devices with their start and end apart: 6 -> 7, of which waited for: 4 -> 6; matrix products, arithmetic and copies ran while one was open for 23% -> 0% of each run, Pallas kernels for 0% -> 0%
where the time goes in v1:
time: 192 us; the launch traced here: 191 us
  blocking collectives  49.7 us (26%)
  waiting for transfers between devices  49.3 us (26%)
  Pallas kernels  48.6 us (25%)
  starting transfers between devices  27.6 us (14%)
  local copies, waits for them, and re-layouts  12.9 us (7%)
  other arithmetic  2.49 us (1%)
    pallas_call x7, Pallas kernels, call(): pl.pallas_call(kernel, out_shape=shapes if many else shapes[0], in_specs=...  48.6 us
    all_to_all x1, blocking collectives, on_device(): lax.all_to_all(skip_sums, ('dp', 'z'), split_axis=0, concat_axis=0, tiled...  32 us
    all_to_all x1, waiting for transfers between devices, on_device(): own = lax.all_to_all(packed, 'x', split_axis=0, concat_axis=0, tiled=True)  24.9 us
    ppermute x6, waiting for transfers between devices, swap(): return lax.ppermute(values, axis, [(0, 1), (1, 0)])  24.4 us
    ppermute x6, starting transfers between devices, swap(): return lax.ppermute(values, axis, [(0, 1), (1, 0)])  22.8 us
    all_to_all x1, blocking collectives, on_device(): back = lax.all_to_all(back, 'x', split_axis=0, concat_axis=0, tiled=True)  17.7 us
    unnamed x22, local copies, waits for them, and re-layouts  9.23 us
    all_to_all x1, starting transfers between devices, on_device(): own = lax.all_to_all(packed, 'x', split_axis=0, concat_axis=0, tiled=True)  4.84 us
  transfers between devices with their start and end apart: 7, of which 6 were waited for; matrix products, arithmetic and copies ran while one was open for 0% of the time, Pallas kernels for 0%

profile of v1, /device:TPU:1, one launch (start us, length us, event | category | flops | bytes accessed | tf_op | source)
XLA Modules:
  0.0 191.4 jit_solution(8789762955064437417)
XLA Ops:
  0.6 0.7 reshape.41
  1.4 0.1 fusion.2
  1.5 0.1 broadcast_in_dim.49
  1.6 0.1 reshape.42
  1.7 0.7 reshape.43
  2.4 0.1 compare_reduce_fusion
  2.5 0.1 broadcast_in_dim.51
  2.6 0.1 reshape.44
  2.7 0.1 pad.7.clone
  2.8 0.7 pad_maximum_fusion.1.decay_ref
  3.5 0.1 add_convert_fusion.flags_ref
  3.6 0.0 copy-start.3
  3.6 1.2 copy-done.3
  4.8 0.0 copy-start.4
  4.8 1.0 copy-done.4
  5.9 0.8 copy-done.5
  6.6 0.0 copy-start.6
  6.6 0.8 copy-done.6
  7.4 0.0 copy-start.7
  7.4 0.8 copy-done.7
  8.1 0.0 copy-start.8
  8.1 0.8 copy-done.8
  8.9 0.2 pack_kernel.1
  9.1 0.0 copy-start.2
  9.1 1.3 copy-done.2
  10.5 4.8 %all-to-all-start = ((bf16[4,2096,128]{2,1,0:T(8,128)(2,1)}), bf16[4,2096,128]{2,1,0:T(8,128)(2,1)S(1)}, u32[]{:S(2)}, u32[]{:S(2)}) async-start(bf16[4,2096,128]{2,1,0:T(8,128)(2,1)} %copy-done.2), calls=%async_computation | async-start | bytes 4292608 | tf_op jit(solution)/shard_map/all_to_all | solution.py:576
  15.3 24.9 %all-to-all-done.own_ref = bf16[4,2096,128]{2,1,0:T(8,128)(2,1)S(1)} async-done(((bf16[4,2096,128]{2,1,0:T(8,128)(2,1)}), bf16[4,2096,128]{2,1,0:T(8,128)(2,1)S(1)}, u32[]{:S(2)}, u32[]{:S(2)}) %all-to-all-start) | async-done | bytes 2146336 | tf_op jit(solution)/shard_map/all_to_all | solution.py:576
  40.3 0.1 constant_dynamic-slice_fusion.1
  40.3 1.2 pad_maximum_fusion
  41.5 2.9 %collective-permute-start = (bf16[4,1312,128]{2,1,0:T(8,128)(2,1)}, bf16[4,1312,128]{2,1,0:T(8,128)(2,1)}, u32[]{:S(2)}, u32[]{:S(2)}) collective-permute-start(bf16[4,1312,128]{2,1,0:T(8,128)(2,1)} %pad_maximum_fusion), channel_id=1, source_target_pairs={{0,1},{1,0},{2,3},{3,2},{4,5},{5,4},{6,7},{7,6},{8,9},{9,8},{10,11... | collective-permute-start | bytes 4030472 | tf_op jit(solution)/shard_map/ppermute | solution.py:530
  44.4 0.1 pad_add_fusion.place_ref
  44.5 0.0 copy-start.9
  44.5 3.0 %collective-permute-done.other_ref = bf16[4,1312,128]{2,1,0:T(8,128)(2,1)} collective-permute-done((bf16[4,1312,128]{2,1,0:T(8,128)(2,1)}, bf16[4,1312,128]{2,1,0:T(8,128)(2,1)}, u32[]{:S(2)}, u32[]{:S(2)}) %collective-permute-start) | collective-permute-done | bytes 1343520 | tf_op jit(solution)/shard_map/ppermute | solution.py:530
  47.5 9.3 %gather_kernel.1 = (bf16[8,784,128]{2,1,0:T(8,128)(2,1)S(1)}, bf16[8,528,128]{2,1,0:T(8,128)(2,1)S(1)}, f32[2,128,128]{2,1,0:T(8,128)S(1)}) custom-call(s32[3]{0:T(128)S(1)} %pad_add_fusion.place_ref, bf16[4,2096,128]{2,1,0:T(8,128)(2,1)S(1)} %all-to-all-done.own_ref, bf16[4,1312,128]{2,1,0:T(8,128)(2,1)} %collective-permute-done.other_ref), custom_call_target="tpu_custom_call" | custom-call | tf_op jit(solution)/shard_map/gather_kernel/pallas_call | solution.py:516
  56.7 0.0 copy-start
  56.7 1.2 copy-done
  57.9 6.9 %collective-permute-start.1 = (f32[2,128,128]{2,1,0:T(8,128)S(1)}, f32[2,128,128]{2,1,0:T(8,128)S(1)}, u32[]{:S(2)}, u32[]{:S(2)}) collective-permute-start(f32[2,128,128]{2,1,0:T(8,128)S(1)} %get-tuple-element.30), channel_id=1, source_target_pairs={{0,8},{8,0},{1,9},{9,1},{2,10},{10,2},{3,11},{11,3},{4,12},{12,4},... | collective-permute-start | bytes 393224 | tf_op jit(solution)/shard_map/ppermute | solution.py:530
  64.8 0.0 copy-done.9
  64.8 0.0 copy-done.10
  64.8 0.1 constant_dynamic-slice_fusion
  64.9 0.1 broadcast_in_dim.53
  65.0 0.1 reshape_reshape.3
  65.1 3.3 %collective-permute-done.1.ends_ref = f32[2,128,128]{2,1,0:T(8,128)S(1)} collective-permute-done((f32[2,128,128]{2,1,0:T(8,128)S(1)}, f32[2,128,128]{2,1,0:T(8,128)S(1)}, u32[]{:S(2)}, u32[]{:S(2)}) %collective-permute-start.1) | collective-permute-done | bytes 131104 | tf_op jit(solution)/shard_map/ppermute | solution.py:530
  68.4 1.4 copy-done.1
  69.8 14.3 %first_kernel.1 = (bf16[2,2,512,128]{3,2,1,0:T(8,128)(2,1)S(1)}, bf16[2,2,512,128]{3,2,1,0:T(8,128)(2,1)S(1)}, bf16[8,2,256,128]{3,2,1,0:T(8,128)(2,1)S(1)}, bf16[8,2,256,128]{3,2,1,0:T(8,128)(2,1)S(1)}) custom-call(s32[3]{0:T(128)S(1)} %pad_add_fusion.place_ref, bf16[8,784,128]{2,1,0:T(8,128)(2,1)S(1)} %copy-done.1, ...), custom_call_target="tpu_custom_call" | custom-call | tf_op jit(solution)/shard_map/first_kernel/pallas_call | solution.py:516
  84.1 5.1 %collective-permute-start.2 = (bf16[2,2,512,128]{3,2,1,0:T(8,128)(2,1)S(1)}, bf16[2,2,512,128]{3,2,1,0:T(8,128)(2,1)S(1)}, u32[]{:S(2)}, u32[]{:S(2)}) collective-permute-start(bf16[2,2,512,128]{3,2,1,0:T(8,128)(2,1)S(1)} %get-tuple-element.32), channel_id=1, source_target_pairs={{0,8},{8,0},{1,9},{9,1},{2,10},{10,2},{3,11},{11,3},{4,12},{12,4},... | collective-permute-start | bytes 1572872 | tf_op jit(solution)/shard_map/ppermute | solution.py:530
  89.2 9.7 %collective-permute-done.2.got_ref = bf16[2,2,512,128]{3,2,1,0:T(8,128)(2,1)S(1)} collective-permute-done((bf16[2,2,512,128]{3,2,1,0:T(8,128)(2,1)S(1)}, bf16[2,2,512,128]{3,2,1,0:T(8,128)(2,1)S(1)}, u32[]{:S(2)}, u32[]{:S(2)}) %collective-permute-start.2) | collective-permute-done | bytes 524320 | tf_op jit(solution)/shard_map/ppermute | solution.py:530
  98.9 8.9 %regrid_kernel.1 = (bf16[8,2,128,128]{3,2,1,0:T(8,128)(2,1)S(1)}, bf16[8,2,128,128]{3,2,1,0:T(8,128)(2,1)S(1)}, f32[2,128,128]{2,1,0:T(8,128)S(1)}, f32[8,128]{1,0:T(8,128)S(1)}) custom-call(s32[3]{0:T(128)S(1)} %pad_add_fusion.place_ref, bf16[8,784,128]{2,1,0:T(8,128)(2,1)S(1)} %copy-done.1, bf16[8,528,128]{2,1,0:T(8,128)(2,1)S(1)} %get-tuple-element.29.sh_ref, ...), custom_call_target="tpu_custom_call" | custom-call | tf_op jit(solution)/shard_map/regrid_kernel/pallas_call | solution.py:516
  107.9 4.7 %collective-permute-start.3 = (f32[2,128,128]{2,1,0:T(8,128)S(1)}, f32[2,128,128]{2,1,0:T(8,128)S(1)}, u32[]{:S(2)}, u32[]{:S(2)}) collective-permute-start(f32[2,128,128]{2,1,0:T(8,128)S(1)} %get-tuple-element.37), channel_id=1, source_target_pairs={{0,8},{8,0},{1,9},{9,1},{2,10},{10,2},{3,11},{11,3},{4,12},{12,4},... | collective-permute-start | bytes 393224 | tf_op jit(solution)/shard_map/ppermute | solution.py:530
  112.5 7.6 %collective-permute-done.3.ends_ref = f32[2,128,128]{2,1,0:T(8,128)S(1)} collective-permute-done((f32[2,128,128]{2,1,0:T(8,128)S(1)}, f32[2,128,128]{2,1,0:T(8,128)S(1)}, u32[]{:S(2)}, u32[]{:S(2)}) %collective-permute-start.3) | collective-permute-done | bytes 131104 | tf_op jit(solution)/shard_map/ppermute | solution.py:530
  120.1 14.2 %second_kernel.1 = bf16[2,4,784,128]{3,2,1,0:T(8,128)(2,1)S(1)} custom-call(s32[3]{0:T(128)S(1)} %pad_add_fusion.place_ref, bf16[8,784,128]{2,1,0:T(8,128)(2,1)S(1)} %copy-done.1, bf16[8,528,128]{2,1,0:T(8,128)(2,1)S(1)} %get-tuple-element.29.sh_ref, f32[8,128]{1,0:T(8,128)S(1)} %concatenate.11.skip_ref, ...), custom_call_target="tpu_custom_call" | custom-call | tf_op jit(solution)/shard_map/second_kernel/pallas_call | solution.py:516
  134.3 0.1 slice_bitcast_fusion
  134.4 1.2 collective-permute-start.4
  135.7 32.0 %all_to_all.15 = f32[32,8,128]{2,1,0:T(8,128)S(1)} all-to-all(f32[32,8,128]{2,1,0:T(8,128)S(1)} %broadcast_in_dim.54), channel_id=1, replica_groups=mesh['dp'=16,'z'=2,'x'=4,'core'=2] {'dp','z'}, dimensions={0} | all-to-all | bytes 262144 | tf_op jit(solution)/shard_map/all_to_all | solution.py:615
  167.7 2.0 %collective-permute-start.5 = (f32[8,128]{1,0:T(8,128)S(1)}, f32[8,128]{1,0:T(8,128)S(1)}, u32[]{:S(2)}, u32[]{:S(2)}) collective-permute-start(f32[8,128]{1,0:T(8,128)S(1)} %reduce_sum.18.skip_ref), channel_id=1, source_target_pairs={{0,1},{1,0},{2,3},{3,2},{4,5},{5,4},{6,7},{7,6},{8,9},{9,8},{10,11... | collective-permute-start | bytes 12296 | tf_op jit(solution)/shard_map/ppermute | solution.py:530
  169.7 0.8 collective-permute-done.5.skip_other_ref
  170.5 0.0 collective-permute-done.4.other_ref
  170.5 0.1 pair_kernel.1
  170.7 17.7 %all_to_all.16.back_ref = bf16[4,1088,128]{2,1,0:T(8,128)(2,1)S(1)} all-to-all(bf16[4,1088,128]{2,1,0:T(8,128)(2,1)S(1)} %pair_kernel.1), channel_id=1, replica_groups=mesh['dp'=16,'z'=2,'x'=4,'core'=2] {'x'}, dimensions={0} | all-to-all | bytes 2228224 | tf_op jit(solution)/shard_map/all_to_all | solution.py:643
  188.4 1.5 last_kernel.1
  189.9 0.1 reshape.45
  190.0 0.1 reduce_sum.19
  190.1 0.6 squeeze.38
  190.8 0.6 squeeze.39
  (11 shorter events, 0.1 us)
Async XLA Ops:
  3.6 1.2 copy-start.3
  4.8 1.0 copy-start.4
  5.9 0.8 copy-start.5
  6.6 0.8 copy-start.6
  7.4 0.8 copy-start.7
  8.1 0.8 copy-start.8
  9.1 1.3 copy-start.2
  10.5 29.7 %all-to-all-start = ((bf16[4,2096,128]{2,1,0:T(8,128)(2,1)}), bf16[4,2096,128]{2,1,0:T(8,128)(2,1)S(1)}, u32[]{:S(2)}, u32[]{:S(2)}) async-start(bf16[4,2096,128]{2,1,0:T(8,128)(2,1)} %copy-done.2), calls=%async_computation | async-start | bytes 4292608 | tf_op jit(solution)/shard_map/all_to_all | solution.py:576
  41.5 6.0 %collective-permute-start = (bf16[4,1312,128]{2,1,0:T(8,128)(2,1)}, bf16[4,1312,128]{2,1,0:T(8,128)(2,1)}, u32[]{:S(2)}, u32[]{:S(2)}) collective-permute-start(bf16[4,1312,128]{2,1,0:T(8,128)(2,1)} %pad_maximum_fusion), channel_id=1, source_target_pairs={{0,1},{1,0},{2,3},{3,2},{4,5},{5,4},{6,7},{7,6},{8,9},{9,8},{10,11... | collective-permute-start | bytes 4030472 | tf_op jit(solution)/shard_map/ppermute | solution.py:530
  44.5 20.3 %copy-start.9 = (f32[32]{0:T(128)S(1)}, f32[32]{0:T(128)}, u32[]{:S(2)}) copy-start(f32[32]{0:T(128)} %param.20) | copy-start | bytes 388
  44.5 20.3 %copy-start.10 = (f32[32]{0:T(128)S(1)}, f32[32]{0:T(128)}, u32[]{:S(2)}) copy-start(f32[32]{0:T(128)} %param.16) | copy-start | bytes 388
  56.7 1.2 copy-start
  57.9 10.5 %collective-permute-start.1 = (f32[2,128,128]{2,1,0:T(8,128)S(1)}, f32[2,128,128]{2,1,0:T(8,128)S(1)}, u32[]{:S(2)}, u32[]{:S(2)}) collective-permute-start(f32[2,128,128]{2,1,0:T(8,128)S(1)} %get-tuple-element.30), channel_id=1, source_target_pairs={{0,8},{8,0},{1,9},{9,1},{2,10},{10,2},{3,11},{11,3},{4,12},{12,4},... | collective-permute-start | bytes 393224 | tf_op jit(solution)/shard_map/ppermute | solution.py:530
  68.4 1.4 copy-start.1
  84.1 14.8 %collective-permute-start.2 = (bf16[2,2,512,128]{3,2,1,0:T(8,128)(2,1)S(1)}, bf16[2,2,512,128]{3,2,1,0:T(8,128)(2,1)S(1)}, u32[]{:S(2)}, u32[]{:S(2)}) collective-permute-start(bf16[2,2,512,128]{3,2,1,0:T(8,128)(2,1)S(1)} %get-tuple-element.32), channel_id=1, source_target_pairs={{0,8},{8,0},{1,9},{9,1},{2,10},{10,2},{3,11},{11,3},{4,12},{12,4},... | collective-permute-start | bytes 1572872 | tf_op jit(solution)/shard_map/ppermute | solution.py:530
  107.9 12.3 %collective-permute-start.3 = (f32[2,128,128]{2,1,0:T(8,128)S(1)}, f32[2,128,128]{2,1,0:T(8,128)S(1)}, u32[]{:S(2)}, u32[]{:S(2)}) collective-permute-start(f32[2,128,128]{2,1,0:T(8,128)S(1)} %get-tuple-element.37), channel_id=1, source_target_pairs={{0,8},{8,0},{1,9},{9,1},{2,10},{10,2},{3,11},{11,3},{4,12},{12,4},... | collective-permute-start | bytes 393224 | tf_op jit(solution)/shard_map/ppermute | solution.py:530
  134.4 36.1 %collective-permute-start.4 = (bf16[4,784,128]{2,1,0:T(8,128)(2,1)S(1)}, bf16[4,784,128]{2,1,0:T(8,128)(2,1)S(1)}, u32[]{:S(2)}, u32[]{:S(2)}) collective-permute-start(bf16[4,784,128]{2,1,0:T(8,128)(2,1)S(1)} %get-tuple-element.47), channel_id=1, source_target_pairs={{0,1},{1,0},{2,3},{3,2},{4,5},{5,4},{6,7},{7,6},{8,9},{9,8},{10,11... | collective-permute-start | bytes 2408456 | tf_op jit(solution)/shard_map/ppermute | solution.py:530
  167.7 2.8 %collective-permute-start.5 = (f32[8,128]{1,0:T(8,128)S(1)}, f32[8,128]{1,0:T(8,128)S(1)}, u32[]{:S(2)}, u32[]{:S(2)}) collective-permute-start(f32[8,128]{1,0:T(8,128)S(1)} %reduce_sum.18.skip_ref), channel_id=1, source_target_pairs={{0,1},{1,0},{2,3},{3,2},{4,5},{5,4},{6,7},{7,6},{8,9},{9,8},{10,11... | collective-permute-start | bytes 12296 | tf_op jit(solution)/shard_map/ppermute | solution.py:530

commit v2 on v1

v2 whole, which is shorter than its diff:
```python
import math

import jax
import jax.numpy as jnp
from jax import lax
from jax.experimental import pallas as pl
from jax.experimental.pallas import tpu as pltpu
from jax.sharding import Mesh
from jax.sharding import PartitionSpec as P

COLS = 32
ROWS = 64
BLOCK = 128
HALF = 64
LANES = 128
PART_ROWS = 784
TOKEN_ROWS = 272
SHARED_ROWS = 528
SEND_ROWS = 2 * PART_ROWS + SHARED_ROWS
COT_ROWS = 512
BLOCKS = 8
UNROLL = {"gather": 8, "first": 4, "regrid": 8, "second": 4}

f32 = jnp.float32
bf16 = jnp.bfloat16


def nn(a, b):
    return lax.dot_general(a, b, (((1,), (0,)), ((), ())), preferred_element_type=f32)


def nt(a, b):
    return lax.dot_general(a, b, (((1,), (1,)), ((), ())), preferred_element_type=f32)


def tn(a, b):
    return lax.dot_general(a, b, (((0,), (0,)), ((), ())), preferred_element_type=f32)


def down(*values):
    return jnp.concatenate(values, axis=0)


def across(*values):
    return jnp.concatenate(values, axis=1)


def parts(values):
    hi = values.astype(bf16)
    return hi, (values - hi.astype(f32)).astype(bf16)


def iota(dim):
    return lax.broadcasted_iota(jnp.int32, (BLOCK, BLOCK), dim)


def one_where(cond):
    return jnp.where(cond, f32(1.0), f32(0.0))


def constants():
    row, col = iota(0), iota(1)
    lower = one_where(col <= row)
    before = one_where(row < col)
    head_a = one_where(col < HALF)
    head_b = 1.0 - head_a
    return {
        "head_a": head_a.astype(bf16),
        "head_b": head_b.astype(bf16),
        "causal": col <= row,
        "lower_bf": lower.astype(bf16),
        "grown": spread_matrix(12, 4, 2, HALF),
        "left": spread_matrix(20, 4, 2, HALF),
        "all": across(
            spread_matrix(0, 4, 3, LANES), spread_matrix(12, 4, 2, HALF), spread_matrix(20, 4, 2, HALF)
        ),
        "before": before,
        "sums": down(lower, before, jnp.ones((BLOCK, BLOCK), f32)).astype(bf16),
        "same": one_where(row == col),
        "mirror_row": one_where(row + col == 2 * (row - row % COLS) + COLS - 1),
        "mirror_col": one_where(row + col == 2 * (row - row % ROWS) + ROWS - 1),
    }


def decay_rows_of(tok_ref):
    small = down(*(tok_ref[b, 256:272, :] for b in range(BLOCKS)))
    row, col = iota(0), iota(1)
    sums = nn(small, one_where(row <= col).astype(bf16)).reshape(BLOCKS, 16, LANES)
    running = sums[:, 0:8] + sums[:, 8:16]
    hi = running.astype(bf16).astype(f32)
    mid = (running - hi).astype(bf16).astype(f32)
    grown = jnp.exp(running)
    left = jnp.exp(running[:, :, LANES - 1 :] - running)
    grown_hi, left_hi = grown.astype(bf16).astype(f32), left.astype(bf16).astype(f32)
    pieces = (hi, mid, running - hi - mid, grown_hi, grown - grown_hi, left_hi, left - left_hi)
    zeros = jnp.zeros((BLOCKS, 4, LANES), f32)
    layers = [
        jnp.concatenate([p[:, 4 * k : 4 * k + 4] for p in pieces] + [zeros], axis=1) for k in range(2)
    ]
    return running, [one.astype(bf16) for one in layers]


def spread_matrix(first, count, copies, width):
    row = lax.broadcasted_iota(jnp.int32, (32, count * width), 0)
    col = lax.broadcasted_iota(jnp.int32, (32, count * width), 1)
    inside = (row >= first) & (row < first + copies * count)
    return one_where(inside & ((row - first) % count == col // width)).astype(bf16)


def decay_scales(c, rows_ref, b, layer, which):
    rows = rows_ref[layer, b]
    values = tn(rows, c[which])
    if which == "grown":
        total = values[BLOCK - 1 :, :]
    else:
        total = tn(rows, c["grown"])[BLOCK - 1 :, :]
    return [(values[:, LANES * g : LANES * g + LANES], total[:, LANES * g : LANES * g + LANES]) for g in range(2)]


def decay_block(c, rows_ref, run_ref, b, layer):
    rows = rows_ref[layer, b]
    values = tn(rows, c["all"])
    running = run_ref[b]
    decays = [
        jnp.where(
            c["causal"],
            jnp.exp(
                jnp.minimum(
                    values[:, LANES * k : LANES * k + LANES] - running[4 * layer + k : 4 * layer + k + 1], 0.0
                )
            ),
            0.0,
        )
        for k in range(4)
    ]
    both = []
    for g in range(2):
        grown = values[:, 512 + LANES * g : 640 + LANES * g]
        left = values[:, 768 + LANES * g : 896 + LANES * g]
        both.append((decays[2 * g], decays[2 * g + 1], grown, left, grown[BLOCK - 1 :, :]))
    return both


def by_head(c, values):
    return down(values * c["head_a"], values * c["head_b"])


def mirror(c, sh_ref, b, layer):
    flags = sh_ref[b, 512:528, :].astype(f32)[layer : layer + 1]
    turned = c["mirror_col"] if layer else c["mirror_row"]
    return (flags * turned + (1.0 - flags) * c["same"]).astype(bf16)


def vectors(sh_ref, b, layer):
    at = 256 * layer
    return sh_ref[b, at : at + 128, :], sh_ref[b, at + 128 : at + 256, :]


def inputs_of(tok_ref, b, group):
    return tok_ref[b, 128 * group : 128 * group + 128, :]


def cotangent_of(cot_ref, b, group):
    at = 128 * group
    return cot_ref[b, at : at + 128, :], cot_ref[b, at + 256 : at + 384, :]


def skip_row(place_ref, skip_ref, group):
    at = 4 * (2 * place_ref[1] + place_ref[2]) + 2 * group
    lane = lax.broadcasted_iota(jnp.int32, (1, LANES), 1)
    return jnp.where(lane < HALF, skip_ref[at], skip_ref[at + 1])


def update(c, scale, carry, vector, values):
    return scale * carry + tn(down(vector, vector), down(*parts(values)))


def load(pairs, sems):
    copies = [pltpu.make_async_copy(a, b, sems.at[i]) for i, (a, b) in enumerate(pairs)]
    for one in copies:
        one.start()
    for one in copies:
        one.wait()


def over_blocks(step, kind):
    lax.fori_loop(0, BLOCKS, lambda i, _: step(i), None, unroll=UNROLL[kind])


def pack_kernel(
    u_any, d1_any, d2_any, w1, r1, w2, r2, o1_any, o2_any, cot_any, out_ref, u_ref, d_ref, v_ref, o_ref, cot_ref, sems
):
    load(
        [(cot_any, cot_ref), (u_any, u_ref), (d1_any, d_ref.at[0]), (d2_any, d_ref.at[1])]
        + [(ref, v_ref.at[k]) for k, ref in enumerate((w1, r1, w2, r2))]
        + [(o1_any, o_ref.at[0]), (o2_any, o_ref.at[1])],
        sems,
    )
    lane = lax.broadcasted_iota(jnp.int32, (1, LANES), 1)
    row_flip = one_where(jnp.bitwise_and(o_ref[0], COLS - 1) != jnp.bitwise_and(lane, COLS - 1))
    col_flip = one_where(
        lax.shift_right_logical(o_ref[1], COLS.bit_length() - 1) != jnp.bitwise_and(lane, ROWS - 1)
    )
    flags = down(row_flip, col_flip, jnp.zeros((14, LANES), f32)).astype(bf16)
    for dest in range(8):
        x, core = dest // 2, dest % 2
        at = core * (PART_ROWS + SHARED_ROWS)
        for group in range(2):
            lanes = slice((2 * dest + group) * LANES, (2 * dest + group + 1) * LANES)
            row = at + 128 * group
            out_ref[x, row : row + 128, :] = u_ref[:, lanes]
            hi, lo = parts(cot_ref[:, lanes])
            row += TOKEN_ROWS
            out_ref[x, row : row + 128, :] = hi
            out_ref[x, row + 256 : row + 384, :] = lo
        decays = down(*(d_ref[layer, 4 * dest : 4 * dest + 4, :] for layer in range(2)))
        hi, lo = parts(decays)
        out_ref[x, at + 256 : at + 272, :] = down(hi.astype(f32), lo.astype(f32)).astype(bf16)
    for x in range(4):
        for k in range(4):
            at = PART_ROWS + 128 * k
            out_ref[x, at : at + 128, :] = v_ref[k]
        out_ref[x, PART_ROWS + 512 : PART_ROWS + 528, :] = flags


def gather_kernel(
    place_ref, own, other, tok_ref, cot_ref, sh_ref, ends_ref, rows_ref, run_ref, s_ref, a_ref, sems
):
    z, core = place_ref[0], place_ref[2]
    mine = pl.multiple_of(core * (PART_ROWS + SHARED_ROWS), 16)
    part = pl.multiple_of(core * SHARED_ROWS, 16)
    share = pl.multiple_of((1 - core) * PART_ROWS, 16)
    pairs = []
    for x in range(4):
        near, far = 2 * x + core, 2 * x + 1 - core
        pairs += [
            (own.at[x, pl.ds(mine, TOKEN_ROWS)], tok_ref.at[near]),
            (own.at[x, pl.ds(mine + TOKEN_ROWS, COT_ROWS)], cot_ref.at[near]),
            (own.at[x, pl.ds(PART_ROWS, SHARED_ROWS)], sh_ref.at[near]),
            (other.at[x, pl.ds(part, TOKEN_ROWS)], tok_ref.at[far]),
            (other.at[x, pl.ds(part + TOKEN_ROWS, COT_ROWS)], cot_ref.at[far]),
            (other.at[x, pl.ds(share, SHARED_ROWS)], sh_ref.at[far]),
        ]
    load(pairs, sems)
    c = constants()
    running, layers = decay_rows_of(tok_ref)
    run_ref[...] = running
    for k in range(2):
        rows_ref[k] = layers[k]
    s_ref[...] = jnp.zeros_like(s_ref)
    a_ref[...] = jnp.zeros_like(a_ref)

    def step(i):
        b = i
        writes, _ = vectors(sh_ref, b, 0)
        for group, (left, total) in enumerate(decay_scales(c, rows_ref, b, 0, "left")):
            u = inputs_of(tok_ref, b, group).astype(f32)
            s_ref[group] = update(c, total, s_ref[group], writes, u * left)
        b = BLOCKS - 1 - i
        _, reads = vectors(sh_ref, b, 1)
        for group, (grown, total) in enumerate(decay_scales(c, rows_ref, b, 1, "grown")):
            hi, lo = cotangent_of(cot_ref, b, group)
            dy = hi.astype(f32) + lo.astype(f32)
            a_ref[group] = update(c, total, a_ref[group], reads, dy * grown)

    over_blocks(step, "gather")
    ends_ref[...] = jnp.where(z == 0, s_ref[...], a_ref[...])


def pick_second(source, out_ref, sems):
    load([(source.at[1, x], out_ref.at[x]) for x in range(4)], sems)


def first_forward(place_ref, skip_ref, rows_ref, run_ref, tok_ref, sh_ref, ends_ref, keep_ref, send_ref, state_ref, s_ref):
    z = place_ref[0]
    c = constants()
    s_ref[...] = jnp.where(z == 1, ends_ref[...], 0.0)

    def step(b):
        writes, reads = vectors(sh_ref, b, 0)
        scores = nt(reads, writes)
        turn = mirror(c, sh_ref, b, 0)
        for group, (decay_a, decay_b, grown, left, total) in enumerate(
            decay_block(c, rows_ref, run_ref, b, 0)
        ):
            u = inputs_of(tok_ref, b, group)
            mixed = across(*parts(across(decay_a * scores, decay_b * scores)))
            state = s_ref[group]
            state_both = down(*parts(state))
            state_ref[b, group] = state_both
            u32 = u.astype(f32)
            heads = by_head(c, u)
            y = (
                nn(mixed, down(heads, heads))
                + grown * nn(across(reads, reads), state_both)
                + skip_row(place_ref, skip_ref, group) * u32
            )
            s_ref[group] = update(c, total, state, writes, u32 * left)
            grid = nn(turn, y.astype(bf16)).astype(bf16)
            for k in range(4):
                near, far = grid[32 * k : 32 * k + 16], grid[32 * k + 16 : 32 * k + 32]
                at = pl.multiple_of(64 * b + 16 * k, 16)
                keep_ref[group, pl.ds(at, 16), :] = jnp.where(z == 0, near, far)
                send_ref[group, pl.ds(at, 16), :] = jnp.where(z == 0, far, near)

    over_blocks(step, "first")


def first_backward(place_ref, skip_ref, rows_ref, run_ref, sh_ref, cot_ref, ends_ref, keep_ref, send_ref, adjoint_ref, a_ref):
    z = place_ref[0]
    c = constants()
    a_ref[...] = jnp.where(z == 0, ends_ref[...], 0.0)

    def step(i):
        b = BLOCKS - 1 - i
        writes, reads = vectors(sh_ref, b, 1)
        scores = nt(reads, writes)
        turn = mirror(c, sh_ref, b, 1)
        for group, (decay_a, decay_b, grown, left, total) in enumerate(
            decay_block(c, rows_ref, run_ref, b, 1)
        ):
            hi, lo = cotangent_of(cot_ref, b, group)
            mixed, mixed_low = parts(down(decay_a * scores, decay_b * scores))
            adjoint = a_ref[group]
            adjoint_both = down(*parts(adjoint))
            adjoint_ref[b, group] = adjoint_both
            dy = hi.astype(f32) + lo.astype(f32)
            hi_heads, lo_heads = by_head(c, hi), by_head(c, lo)
            du = (
                tn(down(mixed, mixed_low, mixed), down(hi_heads, hi_heads, lo_heads))
                + left * nn(across(writes, writes), adjoint_both)
                + skip_row(place_ref, skip_ref, group) * dy
            )
            a_ref[group] = update(c, total, adjoint, reads, dy * grown)
            grid = nn(turn, du.astype(bf16)).astype(bf16)
            for k in range(2):
                near, far = grid[64 * k : 64 * k + 32], grid[64 * k + 32 : 64 * k + 64]
                at = pl.multiple_of(64 * b + 32 * k, 32)
                keep_ref[group, pl.ds(at, 32), :] = jnp.where(z == 0, near, far)
                send_ref[group, pl.ds(at, 32), :] = jnp.where(z == 0, far, near)

    over_blocks(step, "first")


def regrid_forward(
    place_ref, rows_ref, sh_ref, cot_ref, keep_ref, got_ref, u2_ref, s_ref, skip_ref, grid_ref
):
    z = place_ref[0]
    c = constants()
    grid_ref[z] = keep_ref[...].astype(f32)
    grid_ref[1 - z] = got_ref[...].astype(f32)
    s_ref[...] = jnp.zeros_like(s_ref)
    skip_ref[...] = jnp.zeros_like(skip_ref)

    def step(b):
        writes, _ = vectors(sh_ref, b, 1)
        turn = mirror(c, sh_ref, b, 1)
        scale = decay_scales(c, rows_ref, b, 1, "left")
        for group in range(2):
            picked = down(
                *(
                    grid_ref[part, group, pl.ds(2 * b + k, 32, stride=16), :]
                    for k in range(2)
                    for part in range(2)
                )
            )
            u32 = nn(turn, picked.astype(bf16))
            u2_ref[b, group] = u32.astype(bf16)
            left, total = scale[group]
            s_ref[group] = update(c, total, s_ref[group], writes, u32 * left)
            hi, lo = cotangent_of(cot_ref, b, group)
            dy = hi.astype(f32) + lo.astype(f32)
            skip_ref[group : group + 1, :] += jnp.sum(u32 * dy, axis=0, keepdims=True)

    over_blocks(step, "regrid")


def regrid_backward(
    place_ref, rows_ref, tok_ref, sh_ref, keep_ref, got_ref, skip_two_ref, _, dy1_ref, ends_ref, grid_ref, skip_ref, a_ref
):
    z = place_ref[0]
    c = constants()
    grid_ref[z] = keep_ref[...].astype(f32)
    grid_ref[1 - z] = got_ref[...].astype(f32)
    a_ref[...] = jnp.zeros_like(a_ref)
    skip_ref[0:2, :] = jnp.zeros((2, LANES), f32)
    skip_ref[2:8, :] = skip_two_ref[0:6, :]

    def step(i):
        b = BLOCKS - 1 - i
        _, reads = vectors(sh_ref, b, 0)
        turn = mirror(c, sh_ref, b, 0)
        scale = decay_scales(c, rows_ref, b, 0, "grown")
        for group in range(2):
            picked = down(
                *(
                    grid_ref[part, group, pl.ds(4 * b + k, 16, stride=32), :]
                    for k in range(4)
                    for part in range(2)
                )
            )
            dy = nn(turn, picked.astype(bf16))
            dy1_ref[b, group] = dy.astype(bf16)
            grown, total = scale[group]
            a_ref[group] = update(c, total, a_ref[group], reads, dy * grown)
            u = inputs_of(tok_ref, b, group).astype(f32)
            skip_ref[group : group + 1, :] += jnp.sum(u * dy, axis=0, keepdims=True)

    over_blocks(step, "regrid")
    for group in range(2):
        ends_ref[LANES * group : LANES * (group + 1), :] = a_ref[group]
    ends_ref[2 * LANES :, :] = skip_ref[...]


def block_gradients(c, rows_ref, run_ref, sh_ref, b, layer, u_of, dy_of, state_of, adjoint_of):
    writes, reads = vectors(sh_ref, b, layer)
    reads_two, writes_two = down(reads, reads), down(writes, writes)
    scores = nt(reads, writes)
    d_scores, d_writes, d_reads = 0.0, 0.0, 0.0
    decay_rows, kept = [], []
    for group, (decay_a, decay_b, grown, left, total) in enumerate(
        decay_block(c, rows_ref, run_ref, b, layer)
    ):
        u, (dy, dy_low) = u_of(group), dy_of(group)
        u32, dy32 = u.astype(f32), dy.astype(f32)
        dy_heads = by_head(c, dy)
        if dy_low is None:
            pairs = nt(dy_heads, u)
        else:
            pairs = nt(across(dy_heads, by_head(c, dy_low)), across(u, u))
            dy32 = dy32 + dy_low.astype(f32)
        pair_a, pair_b = decay_a * pairs[:BLOCK], decay_b * pairs[BLOCK:]
        d_scores = d_scores + pair_a + pair_b
        u_left, dy_grown = u32 * left, dy32 * grown
        u_hi, u_lo = parts(u_left)
        dy_hi, dy_lo = parts(dy_grown)
        state, adjoint = state_of(group), adjoint_of(group)
        read_state = nn(across(reads, reads), state)
        write_adjoint = nn(across(writes, writes), adjoint)
        state_hi, adjoint_hi = state[:LANES], adjoint[:LANES]
        d_writes = (
            d_writes
            + nt(across(u_hi, u_lo), across(adjoint_hi, adjoint_hi))
        )
        d_reads = (
            d_reads
            + nt(across(dy_hi, dy_lo), across(state_hi, state_hi))
        )
        crossing = across((pair_a * scores).astype(bf16), (pair_b * scores).astype(bf16))
        inner = tn(crossing, c["lower_bf"])
        products = down(
            (dy_grown * read_state).astype(bf16),
            (u_left * write_adjoint).astype(bf16),
            (total * (state_hi.astype(f32) * adjoint_hi.astype(f32))).astype(bf16),
        )
        outer = tn(products, c["sums"])
        for k in range(2):
            decay_rows.append(
                jnp.sum(c["before"] * inner[BLOCK * k : BLOCK * (k + 1)], axis=0, keepdims=True)
                + jnp.sum(outer[HALF * k : HALF * (k + 1)], axis=0, keepdims=True)
            )
        kept.append(
            {
                "total": total,
                "left": left,
                "u_left": down(u_hi, u_lo),
                "dy_grown": down(dy_hi, dy_lo),
                "write_adjoint": write_adjoint,
                "dy_heads": dy_heads,
                "dy": dy32,
                "mixed": lambda a=decay_a, h=decay_b: down(
                    (a * scores).astype(bf16), (h * scores).astype(bf16)
                ),
            }
        )
    low = parts(d_scores)
    d_writes = d_writes + tn(down(*low), reads_two)
    d_reads = d_reads + nn(across(*low), writes_two)
    return d_writes, d_reads, down(*decay_rows), kept, writes_two, reads_two


def put_gradients(out_ref, core, b, at, d_writes, d_reads, rows):
    slot, x = jnp.bitwise_xor(b % 2, core), b // 2
    out_ref[slot, x, at : at + 128, :] = d_writes.astype(bf16)
    out_ref[slot, x, at + 128 : at + 256, :] = d_reads.astype(bf16)
    hi, lo = parts(rows)
    small = down(hi.astype(f32), lo.astype(f32), jnp.zeros((8, LANES), f32))
    out_ref[slot, x, at + 256 : at + 272, :] = small.astype(bf16)


def second_forward(place_ref, rows_ref, run_ref, sh_ref, cot_ref, u2_ref, adjoint_ref, ends_ref, out_ref, s_ref):
    core = place_ref[2]
    c = constants()
    s_ref[...] = ends_ref[...]

    def step(b):
        d_writes, d_reads, rows, kept, writes_two, _ = block_gradients(
            c,
            rows_ref,
            run_ref,
            sh_ref,
            b,
            1,
            lambda g: u2_ref[b, g],
            lambda g: cotangent_of(cot_ref, b, g),
            lambda g: down(*parts(s_ref[g])),
            lambda g: adjoint_ref[b, g],
        )
        put_gradients(out_ref, core, b, 0, d_writes, d_reads, rows)
        for group in range(2):
            k = kept[group]
            s_ref[group] = k["total"] * s_ref[group] + tn(writes_two, k["u_left"])

    over_blocks(step, "second")


def second_backward(
    place_ref, skip_ref, rows_ref, run_ref, tok_ref, sh_ref, dy1_ref, state_ref, ends_ref, own_ref, _second, out_ref, sums_ref, a_ref
):
    core = place_ref[2]
    c = constants()
    for group in range(2):
        arrived = ends_ref[LANES * group : LANES * (group + 1), :]
        a_ref[group] = jnp.where(place_ref[0] == 0, arrived, 0.0)
    total = own_ref[2 * LANES :, :] + ends_ref[2 * LANES :, :]
    for k in range(sums_ref.shape[0]):
        sums_ref[k] = total

    def step(i):
        b = BLOCKS - 1 - i
        d_writes, d_reads, rows, kept, _, reads_two = block_gradients(
            c,
            rows_ref,
            run_ref,
            sh_ref,
            b,
            0,
            lambda g: inputs_of(tok_ref, b, g),
            lambda g: (dy1_ref[b, g], None),
            lambda g: state_ref[b, g],
            lambda g: down(*parts(a_ref[g])),
        )
        put_gradients(out_ref, core, b, 256, d_writes, d_reads, rows)
        slot = jnp.bitwise_xor(b % 2, core)
        for group in range(2):
            k = kept[group]
            du = (
                tn(k["mixed"](), k["dy_heads"])
                + k["left"] * k["write_adjoint"]
                + skip_row(place_ref, skip_ref, group) * k["dy"]
            )
            out_ref[slot, b // 2, 128 * group : 128 * group + 128, :] = du.astype(bf16)
            a_ref[group] = k["total"] * a_ref[group] + tn(reads_two, k["dy_grown"])

    over_blocks(step, "second")


def pair_kernel(own_ref, other_ref, own_two_ref, other_two_ref, skip_ref, skip_other_ref, out_ref):
    skips = []
    for ref in (skip_ref, skip_other_ref):
        total = ref[0, 0:4, :]
        for k in range(1, ref.shape[0]):
            total = total + ref[k, 0:4, :]
        hi = total.astype(bf16).astype(f32)
        mid, low = parts(total - hi)
        skips.append(down(hi, mid.astype(f32), low.astype(f32), jnp.zeros((4, LANES), f32)))
    skips = down(*skips).astype(bf16)
    for x in range(4):
        out_ref[x, 0:256, :] = own_ref[0, x, 0:256, :]
        out_ref[x, 256:512, :] = other_ref[x, 0:256, :]
        out_ref[x, 512:768, :] = (
            own_ref[0, x, 256:512, :].astype(f32) + other_ref[x, 256:512, :].astype(f32)
        ).astype(bf16)
        out_ref[x, 768:784, :] = own_ref[0, x, 512:528, :]
        out_ref[x, 784:800, :] = other_ref[x, 512:528, :]
        out_ref[x, 800:832, :] = skips
        out_ref[x, 832:1088, :] = (
            own_two_ref[0, x, 0:256, :].astype(f32) + other_two_ref[x, 0:256, :].astype(f32)
        ).astype(bf16)
        out_ref[x, 1088:1104, :] = own_two_ref[0, x, 256:272, :]
        out_ref[x, 1104:1120, :] = other_two_ref[x, 256:272, :]


def last_kernel(place_ref, back_ref, grad_ref, w1, r1, w2, r2, decay1_ref, decay2_ref, skip_ref):
    core = place_ref[2]

    def chosen(ref, x, at, size, owner):
        near, far = ref[x, at : at + size, :], ref[x, at + size : at + 2 * size, :]
        return jnp.where(core == owner, near, far)

    for x in range(4):
        for owner in range(2):
            both = chosen(back_ref, x, 0, 256, owner)
            for group in range(2):
                at = ((2 * x + owner) * 2 + group) * LANES
                grad_ref[:, at : at + LANES] = both[128 * group : 128 * group + 128]
            at = (2 * x + owner) * 4
            small = chosen(back_ref, x, 768, 16, owner).astype(f32)
            decay1_ref[at : at + 4, :] = small[0:4] + small[4:8]
            small = chosen(back_ref, x, 1088, 16, owner).astype(f32)
            decay2_ref[at : at + 4, :] = small[0:4] + small[4:8]
            small = chosen(back_ref, x, 800, 16, owner).astype(f32)
            skip_ref[at : at + 4, :] = small[0:4] + small[4:8] + small[8:12]
    for ref, at in ((w1, 512), (r1, 640), (w2, 832), (r2, 960)):
        total = back_ref[0, at : at + 128, :].astype(f32)
        for x in range(1, 4):
            total = total + back_ref[x, at : at + 128, :].astype(f32)
        ref[...] = total.astype(bf16)


def call(kernel, outs, scratch, *args, scalars=1, anywhere=(), copies=0, us=5, mib=12):
    shapes = [jax.ShapeDtypeStruct(s, d) for s, d in outs]
    many = len(shapes) > 1
    in_specs = [
        pl.BlockSpec(
            memory_space=pltpu.SMEM if i < scalars else pl.ANY if i in anywhere else pltpu.VMEM
        )
        for i in range(len(args))
    ]
    out_specs = [pl.BlockSpec(memory_space=pltpu.VMEM)] * len(shapes)
    scratch = [pltpu.VMEM(s, d) for s, d in scratch]
    if copies:
        scratch.append(pltpu.SemaphoreType.DMA((copies,)))
    return pl.pallas_call(
        kernel,
        out_shape=shapes if many else shapes[0],
        in_specs=in_specs,
        out_specs=out_specs if many else out_specs[0],
        scratch_shapes=scratch,
        cost_estimate=pl.CostEstimate(flops=us * 10**9, bytes_accessed=10**6, transcendentals=0),
        compiler_params=pltpu.CompilerParams(vmem_limit_bytes=mib * 2**20),
        name=kernel.__name__,
    )(*args)


def pick_slot(values):
    out = (values.shape[1:], bf16)
    return call(pick_second, [out], [], values, scalars=0, anywhere=(0,), copies=4, us=1)


def swap(values, axis):
    return lax.ppermute(values, axis, [(0, 1), (1, 0)])


def over_x(values):
    return lax.all_to_all(values, "x", split_axis=0, concat_axis=0, tiled=True)


def on_device(
    layer_input,
    writes_first,
    reads_first,
    decay_first,
    skip_first,
    writes_second,
    reads_second,
    decay_second,
    skip_second,
    order_first,
    order_second,
    cotangent,
):
    length, features = layer_input.shape[1:]
    head_count = skip_first.shape[0]
    head_size = features // head_count
    z, x, core = (lax.axis_index(a) for a in ("z", "x", "core"))
    place = jnp.stack([z, x, core]).astype(jnp.int32)

    own = over_x(
        call(
            pack_kernel,
            [((4, SEND_ROWS, LANES), bf16)],
            [
                ((length, features), bf16),
                ((2, head_count, length), f32),
                ((4, length, LANES), bf16),
                ((2, 1, length), jnp.int32),
                ((length, features), f32),
            ],
            layer_input[0],
            decay_first[0],
            decay_second[0],
            writes_first[0],
            reads_first[0],
            writes_second[0],
            reads_second[0],
            order_first.reshape(1, length),
            order_second.reshape(1, length),
            cotangent[0],
            scalars=0,
            anywhere=range(10),
            mib=60,
            copies=10,
            us=2,
        )
    )
    theirs = lax.dynamic_slice_in_dim(own, (1 - core) * PART_ROWS, PART_ROWS + SHARED_ROWS, axis=1)
    other = swap(theirs, "core")

    carry = ((2, LANES, LANES), f32)
    saved = ((BLOCKS, 2, 2 * LANES, LANES), bf16)
    half_grid = ((2, 512, LANES), bf16)
    block = ((BLOCKS, 2, BLOCK, LANES), bf16)
    grids = ((2, 2, 512, LANES), f32)
    few = ((8, LANES), f32)

    tok, cot, sh, end, rows, run = call(
        gather_kernel,
        [
            ((BLOCKS, TOKEN_ROWS, LANES), bf16),
            ((BLOCKS, COT_ROWS, LANES), bf16),
            ((BLOCKS, SHARED_ROWS, LANES), bf16),
            carry,
            ((2, BLOCKS, 32, LANES), bf16),
            ((BLOCKS, 8, LANES), f32),
        ],
        [carry, carry],
        place,
        own,
        other,
        anywhere=(1, 2),
        copies=24,
    )
    end = swap(end, "z")
    keep, send, states = call(
        first_forward,
        [half_grid, half_grid, saved],
        [carry],
        place,
        skip_first,
        rows,
        run,
        tok,
        sh,
        end,
        scalars=2,
    )
    got = swap(send, "z")
    keep_back, send_back, adjoints = call(
        first_backward,
        [half_grid, half_grid, saved],
        [carry],
        place,
        skip_second,
        rows,
        run,
        sh,
        cot,
        end,
        scalars=2,
    )
    got_back = swap(send_back, "z")
    u2, end, skip_two = call(
        regrid_forward, [block, carry, few], [grids], place, rows, sh, cot, keep, got
    )
    end = lax.ppermute(end, "z", [(0, 1)])
    dy1, end_own = call(
        regrid_backward,
        [block, ((2 * LANES + 8, LANES), f32)],
        [grids, few, carry],
        place,
        rows,
        tok,
        sh,
        keep_back,
        got_back,
        skip_two,
        end,
        anywhere=(7,),
    )
    end_back = swap(end_own, "z")

    out_two = call(
        second_forward,
        [((2, 4, 272, LANES), bf16)],
        [carry],
        place,
        rows,
        run,
        sh,
        cot,
        u2,
        adjoints,
        end,
        us=8,
    )
    clips = lax.axis_size("dp")
    out, skip_sums = call(
        second_backward,
        [((2, 4, 528, LANES), bf16), ((clips, 8, LANES), f32)],
        [carry],
        place,
        skip_first,
        rows,
        run,
        tok,
        sh,
        dy1,
        states,
        end_back,
        end_own,
        out_two,
        scalars=2,
        anywhere=(10,),
        us=8,
    )
    skip_sums = lax.all_to_all(skip_sums, "dp", split_axis=0, concat_axis=0, tiled=True)
    back = over_x(
        call(
            pair_kernel,
            [((4, 1120, LANES), bf16)],
            [],
            out,
            swap(pick_slot(out), "core"),
            out_two,
            swap(pick_slot(out_two), "core"),
            skip_sums,
            swap(skip_sums, "core"),
            scalars=0,
            us=1,
        )
    )
    vector = ((length, LANES), bf16)
    decay = ((head_count, length), f32)
    grad_input, w1, r1, w2, r2, decay1, decay2, skip_lanes = call(
        last_kernel,
        [((length, features), bf16), vector, vector, vector, vector, decay, decay, ((head_count, LANES), f32)],
        [],
        place,
        back,
        us=1,
    )
    seq_count = lax.axis_size("z") * lax.axis_size("x") * lax.axis_size("core")
    factor = 1.0 / math.sqrt(clips * seq_count * length * head_size)
    skip_grads = skip_lanes.reshape(8, 2, 2, 2, head_size).sum(-1)
    skip_grads = skip_grads.transpose(1, 0, 2, 3).reshape(2, head_count) * factor
    return (
        grad_input[None],
        w1[None],
        r1[None],
        decay1[None],
        skip_grads[0],
        w2[None],
        r2[None],
        decay2[None],
        skip_grads[1],
    )


def solution(mesh):
    finer = Mesh(mesh.devices.reshape(-1, 2, 4, 2), ("dp", "z", "x", "core"))
    seq = ("z", "x", "core")
    by_token, by_decay = P("dp", seq, None), P("dp", None, seq)
    return jax.shard_map(
        on_device,
        mesh=finer,
        in_specs=(
            by_token,
            by_token,
            by_token,
            by_decay,
            P(),
            by_token,
            by_token,
            by_decay,
            P(),
            P(seq),
            P(seq),
            by_token,
        ),
        out_specs=(
            by_token,
            by_token,
            by_token,
            by_decay,
            P(),
            by_token,
            by_token,
            by_decay,
            P(),
        ),
        check_vma=False,
    )
```

time: 192 us -> 162 us (0.84)
  blocking collectives: 49.7 us -> 36.2 us
  local copies, waits for them, and re-layouts: 12.9 us -> 2.49 us
  starting transfers between devices: 27.6 us -> 34.7 us
  Pallas kernels: 48.6 us -> 43 us
  waiting for transfers between devices: 49.3 us -> 44.6 us
  other arithmetic: 2.49 us -> 0.21 us
    all_to_all x2, blocking collectives: 49.7 us -> 36.2 us  [the longest x1 18.3 us: over_x(): return lax.all_to_all(values, 'x', split_axis=0, concat_axis=0, tiled=True)]
    unnamed x22 -> x4, local copies, waits for them, and re-layouts: 9.23 us -> 0.01 us
    ppermute x0 -> x1, starting transfers between devices: none -> 7.15 us  [on_device(): end = lax.ppermute(end, 'z', [(0, 1)])]
    pallas_call x7 -> x12, Pallas kernels: 48.6 us -> 43 us  [call(): pl.pallas_call(kernel, out_shape=shapes if many else shapes[0], in_specs=...]
    ppermute x6 -> x8, waiting for transfers between devices: 24.4 us -> 19.7 us  [swap(): return lax.ppermute(values, axis, [(0, 1), (1, 0)])]
    ppermute x6 -> x8, starting transfers between devices: 22.8 us -> 22.7 us  [swap(): return lax.ppermute(values, axis, [(0, 1), (1, 0)])]
  transfers between devices with their start and end apart: 7 -> 10, of which waited for: 6 -> 5; matrix products, arithmetic and copies ran while one was open for 0% -> 0% of each run, Pallas kernels for 0% -> 10%
where the time goes in v2:
time: 162 us
  waiting for transfers between devices  44.6 us (28%)
  Pallas kernels  43 us (27%)
  blocking collectives  36.2 us (22%)
  starting transfers between devices  34.7 us (21%)
  local copies, waits for them, and re-layouts  2.49 us (2%)
    pallas_call x12, Pallas kernels, call(): pl.pallas_call(kernel, out_shape=shapes if many else shapes[0], in_specs=...  43 us
    all_to_all x1, waiting for transfers between devices, over_x(): return lax.all_to_all(values, 'x', split_axis=0, concat_axis=0, tiled=True)  24.9 us
    ppermute x8, starting transfers between devices, swap(): return lax.ppermute(values, axis, [(0, 1), (1, 0)])  22.7 us
    ppermute x8, waiting for transfers between devices, swap(): return lax.ppermute(values, axis, [(0, 1), (1, 0)])  19.7 us
    all_to_all x1, blocking collectives, over_x(): return lax.all_to_all(values, 'x', split_axis=0, concat_axis=0, tiled=True)  18.3 us
    all_to_all x1, blocking collectives, on_device(): lax.all_to_all(skip_sums, 'dp', split_axis=0, concat_axis=0, tiled=True)  17.9 us
    ppermute x1, starting transfers between devices, on_device(): end = lax.ppermute(end, 'z', [(0, 1)])  7.15 us
    all_to_all x1, starting transfers between devices, over_x(): return lax.all_to_all(values, 'x', split_axis=0, concat_axis=0, tiled=True)  4.85 us
  transfers between devices with their start and end apart: 10, of which 5 were waited for; matrix products, arithmetic and copies ran while one was open for 0% of the time, Pallas kernels for 10%

profile of v2, /device:TPU:1, one launch (start us, length us, event | category | flops | bytes accessed | tf_op | source)
XLA Modules:
  0.0 161.9 jit_solution(543697064455959040)
XLA Ops:
  0.6 3.0 %pack_kernel.1 = bf16[4,2096,128]{2,1,0:T(8,128)(2,1)} custom-call(bf16[128,2048]{1,0:T(8,128)(2,1)} %bitcast.27, f32[32,128]{1,0:T(8,128)} %bitcast.32, f32[32,128]{1,0:T(8,128)} %bitcast.33, bf16[128,128]{1,0:T(8,128)(2,1)} %bitcast.28, bf16[128,128]{1,0:T(8,128)(2,1)} %bitcast.29, bf16[128,128]{1,0:T(8,128)(2,1)} %bitcast.30, bf16[128,128]{1,0:T(8,128)(2,1)} %bitcast.31, ...), custom_call_target="tpu_custom_call" | custom-call | flops 2000000000 | bytes 1000000 | tf_op jit(solution)/shard_map/pack_kernel/pallas_call | solution.py:624
  3.7 4.9 %all-to-all-start = ((bf16[4,2096,128]{2,1,0:T(8,128)(2,1)}), bf16[4,2096,128]{2,1,0:T(8,128)(2,1)S(1)}, u32[]{:S(2)}, u32[]{:S(2)}) async-start(bf16[4,2096,128]{2,1,0:T(8,128)(2,1)} %pack_kernel.1), calls=%async_computation | async-start | bytes 4292608 | tf_op jit(solution)/shard_map/all_to_all | solution.py:646
  8.5 24.9 %all-to-all-done.own = bf16[4,2096,128]{2,1,0:T(8,128)(2,1)S(1)} async-done(((bf16[4,2096,128]{2,1,0:T(8,128)(2,1)}), bf16[4,2096,128]{2,1,0:T(8,128)(2,1)S(1)}, u32[]{:S(2)}, u32[]{:S(2)}) %all-to-all-start) | async-done | bytes 2146336 | tf_op jit(solution)/shard_map/all_to_all | solution.py:646
  33.4 1.2 constant_dynamic-slice_fusion
  34.6 2.9 %collective-permute-start = (bf16[4,1312,128]{2,1,0:T(8,128)(2,1)}, bf16[4,1312,128]{2,1,0:T(8,128)(2,1)S(1)}, u32[]{:S(2)}, u32[]{:S(2)}) collective-permute-start(bf16[4,1312,128]{2,1,0:T(8,128)(2,1)} %constant_dynamic-slice_fusion), channel_id=1, source_target_pairs={{0,1},{1,0},{2,3},{3,2},{4,5},{5,4},{6,7},{7,6},{8,9},{9,8},{10,11... | collective-permute-start | bytes 4030472 | tf_op jit(solution)/shard_map/ppermute | solution.py:642
  37.5 0.1 pad_add_fusion.place_ref
  37.6 0.0 copy-start.1
  37.6 2.8 %collective-permute-done.other = bf16[4,1312,128]{2,1,0:T(8,128)(2,1)S(1)} collective-permute-done((bf16[4,1312,128]{2,1,0:T(8,128)(2,1)}, bf16[4,1312,128]{2,1,0:T(8,128)(2,1)S(1)}, u32[]{:S(2)}, u32[]{:S(2)}) %collective-permute-start) | collective-permute-done | bytes 1343520 | tf_op jit(solution)/shard_map/ppermute | solution.py:642
  40.5 7.8 %gather_kernel.1 = (bf16[8,272,128]{2,1,0:T(8,128)(2,1)S(1)}, bf16[8,512,128]{2,1,0:T(8,128)(2,1)S(1)}, bf16[8,528,128]{2,1,0:T(8,128)(2,1)S(1)}, f32[2,128,128]...) custom-call(s32[3]{0:T(128)S(1)} %pad_add_fusion.place_ref, ...), custom_call_target="tpu_custom_call" | custom-call | flops 5000000000 | bytes 1000000 | tf_op jit(solution)/shard_map/gather_kernel/pallas_call | solution.py:624
  48.3 7.0 %collective-permute-start.1 = (f32[2,128,128]{2,1,0:T(8,128)S(1)}, f32[2,128,128]{2,1,0:T(8,128)S(1)}, u32[]{:S(2)}, u32[]{:S(2)}) collective-permute-start(f32[2,128,128]{2,1,0:T(8,128)S(1)} %get-tuple-element.41), channel_id=1, source_target_pairs={{0,8},{8,0},{1,9},{9,1},{2,10},{10,2},{3,11},{11,3},{4,12},{12,4},... | collective-permute-start | bytes 393224 | tf_op jit(solution)/shard_map/ppermute | solution.py:642
  55.3 3.6 %collective-permute-done.1.ends_ref = f32[2,128,128]{2,1,0:T(8,128)S(1)} collective-permute-done((f32[2,128,128]{2,1,0:T(8,128)S(1)}, f32[2,128,128]{2,1,0:T(8,128)S(1)}, u32[]{:S(2)}, u32[]{:S(2)}) %collective-permute-start.1) | collective-permute-done | bytes 131104 | tf_op jit(solution)/shard_map/ppermute | solution.py:642
  58.9 0.0 copy-done.1
  58.9 0.0 copy-start
  58.9 5.0 %first_forward.1 = (bf16[2,512,128]{2,1,0:T(8,128)(2,1)S(1)}, bf16[2,512,128]{2,1,0:T(8,128)(2,1)S(1)}, bf16[8,2,256,128]{3,2,1,0:T(8,128)(2,1)S(1)}) custom-call(s32[3]{0:T(128)S(1)} %pad_add_fusion.place_ref, f32[32]{0:T(128)S(1)} %copy-done.1, bf16[2,8,32,128]{3,2,1,0:T(8,128)(2,1)S(1)} %get-tuple-element.36.rows_ref, ...), custom_call_target="tpu_custom_call" | custom-call | flops 5000000000 | bytes 1000000 | tf_op jit(solution)/shard_map/first_forward/pallas_call | solution.py:624
  63.9 5.1 %collective-permute-start.3 = (bf16[2,512,128]{2,1,0:T(8,128)(2,1)S(1)}, bf16[2,512,128]{2,1,0:T(8,128)(2,1)S(1)}, u32[]{:S(2)}, u32[]{:S(2)}) collective-permute-start(bf16[2,512,128]{2,1,0:T(8,128)(2,1)S(1)} %get-tuple-element.45), channel_id=1, source_target_pairs={{0,8},{8,0},{1,9},{9,1},{2,10},{10,2},{3,11},{11,3},{4,12},{12,4},... | collective-permute-start | bytes 786440 | tf_op jit(solution)/shard_map/ppermute | solution.py:642
  69.0 0.0 copy-done
  69.0 5.9 %first_backward.1 = (bf16[2,512,128]{2,1,0:T(8,128)(2,1)S(1)}, bf16[2,512,128]{2,1,0:T(8,128)(2,1)S(1)}, bf16[8,2,256,128]{3,2,1,0:T(8,128)(2,1)S(1)}) custom-call(s32[3]{0:T(128)S(1)} %pad_add_fusion.place_ref, f32[32]{0:T(128)S(1)} %copy-done, bf16[2,8,32,128]{3,2,1,0:T(8,128)(2,1)S(1)} %get-tuple-element.36.rows_ref, ...), custom_call_target="tpu_custom_call" | custom-call | flops 5000000000 | bytes 1000000 | tf_op jit(solution)/shard_map/first_backward/pallas_call | solution.py:624
  74.9 0.4 collective-permute-start.2
  75.3 0.0 collective-permute-done.3.got_ref
  75.3 2.5 %regrid_forward.1 = (bf16[8,2,128,128]{3,2,1,0:T(8,128)(2,1)S(1)}, f32[2,128,128]{2,1,0:T(8,128)S(1)}, f32[8,128]{1,0:T(8,128)S(1)}) custom-call(s32[3]{0:T(128)S(1)} %pad_add_fusion.place_ref, bf16[2,8,32,128]{3,2,1,0:T(8,128)(2,1)S(1)} %get-tuple-element.36.rows_ref, bf16[8,528,128]{2,1,0:T(8,128)(2,1)S(1)} %get-tuple-element.39.sh_ref, ...), custom_call_target="tpu_custom_call" | custom-call | flops 5000000000 | bytes 1000000 | tf_op jit(solution)/shard_map/regrid_forward/pallas_call | solution.py:624
  77.8 7.1 %collective-permute-start.4 = (f32[2,128,128]{2,1,0:T(8,128)S(1)}, f32[2,128,128]{2,1,0:T(8,128)S(1)}, u32[]{:S(2)}, u32[]{:S(2)}) collective-permute-start(f32[2,128,128]{2,1,0:T(8,128)S(1)} %get-tuple-element.47), channel_id=1, source_target_pairs={{0,8},{1,9},{2,10},{3,11},{4,12},{5,13},{6,14},{7,15},{16,24},{17,... | collective-permute-start | bytes 393224 | tf_op jit(solution)/shard_map/ppermute | solution.py:756
  85.0 12.4 %collective-permute-done.2.got_ref = bf16[2,512,128]{2,1,0:T(8,128)(2,1)S(1)} collective-permute-done((bf16[2,512,128]{2,1,0:T(8,128)(2,1)S(1)}, bf16[2,512,128]{2,1,0:T(8,128)(2,1)S(1)}, u32[]{:S(2)}, u32[]{:S(2)}) %collective-permute-start.2) | collective-permute-done | bytes 262176 | tf_op jit(solution)/shard_map/ppermute | solution.py:642
  97.4 0.0 collective-permute-done.4._.ends_ref
  97.4 2.6 %regrid_backward.1 = (bf16[8,2,128,128]{3,2,1,0:T(8,128)(2,1)S(1)}, f32[264,128]{1,0:T(8,128)S(1)}) custom-call(s32[3]{0:T(128)S(1)} %pad_add_fusion.place_ref, bf16[2,8,32,128]{3,2,1,0:T(8,128)(2,1)S(1)} %get-tuple-element.36.rows_ref, bf16[8,272,128]{2,1,0:T(8,128)(2,1)S(1)} %get-tuple-element.38.tok_ref, ...), custom_call_target="tpu_custom_call" | custom-call | flops 5000000000 | bytes 1000000 | tf_op jit(solution)/shard_map/regrid_backward/pallas_call | solution.py:624
  100.0 3.2 %collective-permute-start.5 = (f32[264,128]{1,0:T(8,128)S(1)}, f32[264,128]{1,0:T(8,128)S(1)}, u32[]{:S(2)}, u32[]{:S(2)}) collective-permute-start(f32[264,128]{1,0:T(8,128)S(1)} %get-tuple-element.50.own_ref), channel_id=1, source_target_pairs={{0,8},{8,0},{1,9},{9,1},{2,10},{10,2},{3,11},{11,3},{4,12},{12,4},... | collective-permute-start | bytes 405512 | tf_op jit(solution)/shard_map/ppermute | solution.py:642
  103.2 6.7 %second_forward.1._second.source.own_two_ref = bf16[2,4,272,128]{3,2,1,0:T(8,128)(2,1)S(1)} custom-call(s32[3]{0:T(128)S(1)} %pad_add_fusion.place_ref, bf16[2,8,32,128]{3,2,1,0:T(8,128)(2,1)S(1)} %get-tuple-element.36.rows_ref, f32[8,8,128]{2,1,0:T(8,128)S(1)} %get-tuple-element.37.run_ref, bf16[8,528,128]{2,1,0:T(8,128)(2,1)S(1)} %get-tuple-element.39.sh_ref, ...), custom_call_target="tpu_custom_call" | custom-call | flops 8000000000 | bytes 1000000 | tf_op jit(solution)/shard_map/second_forward/pallas_call | solution.py:624
  109.9 0.0 collective-permute-done.5.ends_ref
  109.9 6.6 %second_backward.1 = (bf16[2,4,528,128]{3,2,1,0:T(8,128)(2,1)S(1)}, f32[16,8,128]{2,1,0:T(8,128)S(1)}) custom-call(s32[3]{0:T(128)S(1)} %pad_add_fusion.place_ref, f32[32]{0:T(128)S(1)} %copy-done.1, bf16[2,8,32,128]{3,2,1,0:T(8,128)(2,1)S(1)} %get-tuple-element.36.rows_ref, f32[8,8,128]{2,1,0:T(8,128)S(1)} %get-tuple-element.37.run_ref, ...), custom_call_target="tpu_custom_call" | custom-call | flops 8000000000 | bytes 1000000 | tf_op jit(solution)/shard_map/second_backward/pallas_call | solution.py:624
  116.5 0.7 pick_second.2
  117.3 2.0 %collective-permute-start.6 = (bf16[4,528,128]{2,1,0:T(8,128)(2,1)S(1)}, bf16[4,528,128]{2,1,0:T(8,128)(2,1)S(1)}, u32[]{:S(2)}, u32[]{:S(2)}) collective-permute-start(bf16[4,528,128]{2,1,0:T(8,128)(2,1)S(1)} %pick_second.2), channel_id=1, source_target_pairs={{0,1},{1,0},{2,3},{3,2},{4,5},{5,4},{6,7},{7,6},{8,9},{9,8},{10,11... | collective-permute-start | bytes 1622024 | tf_op jit(solution)/shard_map/ppermute | solution.py:642
  119.3 0.4 pick_second.3
  119.6 0.1 collective-permute-start.7
  119.8 17.9 %all_to_all.15.skip_ref = f32[16,8,128]{2,1,0:T(8,128)S(1)} all-to-all(f32[16,8,128]{2,1,0:T(8,128)S(1)} %get-tuple-element.54), channel_id=1, replica_groups=mesh['dp'=16,'z'=2,'x'=4,'core'=2] {'dp'}, dimensions={0} | all-to-all | bytes 131072 | tf_op jit(solution)/shard_map/all_to_all | solution.py:807
  137.6 1.9 %collective-permute-start.8 = (f32[16,8,128]{2,1,0:T(8,128)S(1)}, f32[16,8,128]{2,1,0:T(8,128)S(1)}, u32[]{:S(2)}, u32[]{:S(2)}) collective-permute-start(f32[16,8,128]{2,1,0:T(8,128)S(1)} %all_to_all.15.skip_ref), channel_id=1, source_target_pairs={{0,1},{1,0},{2,3},{3,2},{4,5},{5,4},{6,7},{7,6},{8,9},{9,8},{10,11... | collective-permute-start | bytes 196616 | tf_op jit(solution)/shard_map/ppermute | solution.py:642
  139.5 0.0 collective-permute-done.7.other_two_ref
  139.5 0.9 collective-permute-done.8.skip_other_ref
  140.4 0.0 collective-permute-done.6.other_ref
  140.4 0.1 pair_kernel.1
  140.6 18.3 %all_to_all.16.back_ref = bf16[4,1120,128]{2,1,0:T(8,128)(2,1)S(1)} all-to-all(bf16[4,1120,128]{2,1,0:T(8,128)(2,1)S(1)} %pair_kernel.1), channel_id=1, replica_groups=mesh['dp'=16,'z'=2,'x'=4,'core'=2] {'x'}, dimensions={0} | all-to-all | bytes 2293760 | tf_op jit(solution)/shard_map/all_to_all | solution.py:646
  158.9 1.5 last_kernel.1
  160.4 0.1 reshape.36
  160.5 0.1 reduce_sum.9
  160.7 0.6 squeeze.39
  161.3 0.6 squeeze.38
  (2 shorter events, 0.0 us)
Async XLA Ops:
  3.7 29.8 %all-to-all-start = ((bf16[4,2096,128]{2,1,0:T(8,128)(2,1)}), bf16[4,2096,128]{2,1,0:T(8,128)(2,1)S(1)}, u32[]{:S(2)}, u32[]{:S(2)}) async-start(bf16[4,2096,128]{2,1,0:T(8,128)(2,1)} %pack_kernel.1), calls=%async_computation | async-start | bytes 4292608 | tf_op jit(solution)/shard_map/all_to_all | solution.py:646
  34.6 5.8 %collective-permute-start = (bf16[4,1312,128]{2,1,0:T(8,128)(2,1)}, bf16[4,1312,128]{2,1,0:T(8,128)(2,1)S(1)}, u32[]{:S(2)}, u32[]{:S(2)}) collective-permute-start(bf16[4,1312,128]{2,1,0:T(8,128)(2,1)} %constant_dynamic-slice_fusion), channel_id=1, source_target_pairs={{0,1},{1,0},{2,3},{3,2},{4,5},{5,4},{6,7},{7,6},{8,9},{9,8},{10,11... | collective-permute-start | bytes 4030472 | tf_op jit(solution)/shard_map/ppermute | solution.py:642
  37.6 21.3 %copy-start.1 = (f32[32]{0:T(128)S(1)}, f32[32]{0:T(128)}, u32[]{:S(2)}) copy-start(f32[32]{0:T(128)} %skip_ref.5) | copy-start | bytes 388
  48.3 10.6 %collective-permute-start.1 = (f32[2,128,128]{2,1,0:T(8,128)S(1)}, f32[2,128,128]{2,1,0:T(8,128)S(1)}, u32[]{:S(2)}, u32[]{:S(2)}) collective-permute-start(f32[2,128,128]{2,1,0:T(8,128)S(1)} %get-tuple-element.41), channel_id=1, source_target_pairs={{0,8},{8,0},{1,9},{9,1},{2,10},{10,2},{3,11},{11,3},{4,12},{12,4},... | collective-permute-start | bytes 393224 | tf_op jit(solution)/shard_map/ppermute | solution.py:642
  58.9 10.2 %copy-start = (f32[32]{0:T(128)S(1)}, f32[32]{0:T(128)}, u32[]{:S(2)}) copy-start(f32[32]{0:T(128)} %skip_ref.3) | copy-start | bytes 388
  63.9 11.4 %collective-permute-start.3 = (bf16[2,512,128]{2,1,0:T(8,128)(2,1)S(1)}, bf16[2,512,128]{2,1,0:T(8,128)(2,1)S(1)}, u32[]{:S(2)}, u32[]{:S(2)}) collective-permute-start(bf16[2,512,128]{2,1,0:T(8,128)(2,1)S(1)} %get-tuple-element.45), channel_id=1, source_target_pairs={{0,8},{8,0},{1,9},{9,1},{2,10},{10,2},{3,11},{11,3},{4,12},{12,4},... | collective-permute-start | bytes 786440 | tf_op jit(solution)/shard_map/ppermute | solution.py:642
  74.9 22.5 %collective-permute-start.2 = (bf16[2,512,128]{2,1,0:T(8,128)(2,1)S(1)}, bf16[2,512,128]{2,1,0:T(8,128)(2,1)S(1)}, u32[]{:S(2)}, u32[]{:S(2)}) collective-permute-start(bf16[2,512,128]{2,1,0:T(8,128)(2,1)S(1)} %get-tuple-element.43), channel_id=1, source_target_pairs={{0,8},{8,0},{1,9},{9,1},{2,10},{10,2},{3,11},{11,3},{4,12},{12,4},... | collective-permute-start | bytes 786440 | tf_op jit(solution)/shard_map/ppermute | solution.py:642
  77.8 19.5 %collective-permute-start.4 = (f32[2,128,128]{2,1,0:T(8,128)S(1)}, f32[2,128,128]{2,1,0:T(8,128)S(1)}, u32[]{:S(2)}, u32[]{:S(2)}) collective-permute-start(f32[2,128,128]{2,1,0:T(8,128)S(1)} %get-tuple-element.47), channel_id=1, source_target_pairs={{0,8},{1,9},{2,10},{3,11},{4,12},{5,13},{6,14},{7,15},{16,24},{17,... | collective-permute-start | bytes 393224 | tf_op jit(solution)/shard_map/ppermute | solution.py:756
  100.0 9.9 %collective-permute-start.5 = (f32[264,128]{1,0:T(8,128)S(1)}, f32[264,128]{1,0:T(8,128)S(1)}, u32[]{:S(2)}, u32[]{:S(2)}) collective-permute-start(f32[264,128]{1,0:T(8,128)S(1)} %get-tuple-element.50.own_ref), channel_id=1, source_target_pairs={{0,8},{8,0},{1,9},{9,1},{2,10},{10,2},{3,11},{11,3},{4,12},{12,4},... | collective-permute-start | bytes 405512 | tf_op jit(solution)/shard_map/ppermute | solution.py:642
  117.3 23.1 %collective-permute-start.6 = (bf16[4,528,128]{2,1,0:T(8,128)(2,1)S(1)}, bf16[4,528,128]{2,1,0:T(8,128)(2,1)S(1)}, u32[]{:S(2)}, u32[]{:S(2)}) collective-permute-start(bf16[4,528,128]{2,1,0:T(8,128)(2,1)S(1)} %pick_second.2), channel_id=1, source_target_pairs={{0,1},{1,0},{2,3},{3,2},{4,5},{5,4},{6,7},{7,6},{8,9},{9,8},{10,11... | collective-permute-start | bytes 1622024 | tf_op jit(solution)/shard_map/ppermute | solution.py:642
  119.6 19.9 %collective-permute-start.7 = (bf16[4,272,128]{2,1,0:T(8,128)(2,1)S(1)}, bf16[4,272,128]{2,1,0:T(8,128)(2,1)S(1)}, u32[]{:S(2)}, u32[]{:S(2)}) collective-permute-start(bf16[4,272,128]{2,1,0:T(8,128)(2,1)S(1)} %pick_second.3), channel_id=1, source_target_pairs={{0,1},{1,0},{2,3},{3,2},{4,5},{5,4},{6,7},{7,6},{8,9},{9,8},{10,11... | collective-permute-start | bytes 835592 | tf_op jit(solution)/shard_map/ppermute | solution.py:642
  137.6 2.8 %collective-permute-start.8 = (f32[16,8,128]{2,1,0:T(8,128)S(1)}, f32[16,8,128]{2,1,0:T(8,128)S(1)}, u32[]{:S(2)}, u32[]{:S(2)}) collective-permute-start(f32[16,8,128]{2,1,0:T(8,128)S(1)} %all_to_all.15.skip_ref), channel_id=1, source_target_pairs={{0,1},{1,0},{2,3},{3,2},{4,5},{5,4},{6,7},{7,6},{8,9},{9,8},{10,11... | collective-permute-start | bytes 196616 | tf_op jit(solution)/shard_map/ppermute | solution.py:642

commit v3 on v2

--- a/solution.py
+++ b/solution.py
@@ -19,6 +19,7 @@
 SEND_ROWS = 2 * PART_ROWS + SHARED_ROWS
 COT_ROWS = 512
 BLOCKS = 8
+SKIP_SCALE = 1.0 / math.sqrt(16 * 2048 * 64)
 UNROLL = {"gather": 8, "first": 4, "regrid": 8, "second": 4}
 
 f32 = jnp.float32
@@ -171,7 +172,17 @@
     return jnp.where(lane < HALF, skip_ref[at], skip_ref[at + 1])
 
 
-def update(c, scale, carry, vector, values):
+def update(carry_ref, totals, vector, values):
+    halves = [parts(v) if not isinstance(v, tuple) else v for v in values]
+    moved = tn(vector, across(halves[0][0], halves[1][0], halves[0][1], halves[1][1]))
+    for g in range(2):
+        at = LANES * g
+        carry_ref[g] = (
+            totals[g] * carry_ref[g] + moved[:, at : at + LANES] + moved[:, 2 * LANES + at : 3 * LANES + at]
+        )
+
+
+def update_pair(scale, carry, vector, values):
     return scale * carry + tn(down(vector, vector), down(*parts(values)))
 
 
@@ -230,40 +241,59 @@
     mine = pl.multiple_of(core * (PART_ROWS + SHARED_ROWS), 16)
     part = pl.multiple_of(core * SHARED_ROWS, 16)
     share = pl.multiple_of((1 - core) * PART_ROWS, 16)
-    pairs = []
+    tokens, vectors_in, cotangents = [], [], []
     for x in range(4):
         near, far = 2 * x + core, 2 * x + 1 - core
-        pairs += [
+        tokens += [
             (own.at[x, pl.ds(mine, TOKEN_ROWS)], tok_ref.at[near]),
-            (own.at[x, pl.ds(mine + TOKEN_ROWS, COT_ROWS)], cot_ref.at[near]),
+            (other.at[x, pl.ds(part, TOKEN_ROWS)], tok_ref.at[far]),
+        ]
+        vectors_in += [
             (own.at[x, pl.ds(PART_ROWS, SHARED_ROWS)], sh_ref.at[near]),
-            (other.at[x, pl.ds(part, TOKEN_ROWS)], tok_ref.at[far]),
-            (other.at[x, pl.ds(part + TOKEN_ROWS, COT_ROWS)], cot_ref.at[far]),
             (other.at[x, pl.ds(share, SHARED_ROWS)], sh_ref.at[far]),
         ]
-    load(pairs, sems)
+        cotangents += [
+            (own.at[x, pl.ds(mine + TOKEN_ROWS, COT_ROWS)], cot_ref.at[near]),
+            (other.at[x, pl.ds(part + TOKEN_ROWS, COT_ROWS)], cot_ref.at[far]),
+        ]
+    copies = [
+        pltpu.make_async_copy(a, b, sems.at[i])
+        for i, (a, b) in enumerate(tokens + vectors_in + cotangents)
+    ]
+    for one in copies:
+        one.start()
     c = constants()
+    s_ref[...] = jnp.zeros_like(s_ref)
+    a_ref[...] = jnp.zeros_like(a_ref)
+    for one in copies[:8]:
+        one.wait()
     running, layers = decay_rows_of(tok_ref)
     run_ref[...] = running
     for k in range(2):
         rows_ref[k] = layers[k]
-    s_ref[...] = jnp.zeros_like(s_ref)
-    a_ref[...] = jnp.zeros_like(a_ref)
-
-    def step(i):
-        b = i
+    for one in copies[8:16]:
+        one.wait()
+
+    def forward(b):
         writes, _ = vectors(sh_ref, b, 0)
-        for group, (left, total) in enumerate(decay_scales(c, rows_ref, b, 0, "left")):
-            u = inputs_of(tok_ref, b, group).astype(f32)
-            s_ref[group] = update(c, total, s_ref[group], writes, u * left)
+        scale = decay_scales(c, rows_ref, b, 0, "left")
+        values = [inputs_of(tok_ref, b, g).astype(f32) * scale[g][0] for g in range(2)]
+        update(s_ref, [one[1] for one in scale], writes, values)
+
+    def backward(i):
         b = BLOCKS - 1 - i
         _, reads = vectors(sh_ref, b, 1)
-        for group, (grown, total) in enumerate(decay_scales(c, rows_ref, b, 1, "grown")):
+        scale = decay_scales(c, rows_ref, b, 1, "grown")
+        values = []
+        for group in range(2):
             hi, lo = cotangent_of(cot_ref, b, group)
-            dy = hi.astype(f32) + lo.astype(f32)
-            a_ref[group] = update(c, total, a_ref[group], reads, dy * grown)
-
-    over_blocks(step, "gather")
+            values.append((hi.astype(f32) + lo.astype(f32)) * scale[group][0])
+        update(a_ref, [one[1] for one in scale], reads, values)
+
+    over_blocks(forward, "gather")
+    for one in copies[16:]:
+        one.wait()
+    over_blocks(backward, "gather")
     ends_ref[...] = jnp.where(z == 0, s_ref[...], a_ref[...])
 
 
@@ -295,7 +325,7 @@
                 + grown * nn(across(reads, reads), state_both)
                 + skip_row(place_ref, skip_ref, group) * u32
             )
-            s_ref[group] = update(c, total, state, writes, u32 * left)
+            s_ref[group] = update_pair(total, state, writes, u32 * left)
             grid = nn(turn, y.astype(bf16)).astype(bf16)
             for k in range(4):
                 near, far = grid[32 * k : 32 * k + 16], grid[32 * k + 16 : 32 * k + 32]
@@ -331,7 +361,7 @@
                 + left * nn(across(writes, writes), adjoint_both)
                 + skip_row(place_ref, skip_ref, group) * dy
             )
-            a_ref[group] = update(c, total, adjoint, reads, dy * grown)
+            a_ref[group] = update_pair(total, adjoint, reads, dy * grown)
             grid = nn(turn, du.astype(bf16)).astype(bf16)
             for k in range(2):
                 near, far = grid[64 * k : 64 * k + 32], grid[64 * k + 32 : 64 * k + 64]
@@ -356,6 +386,7 @@
         writes, _ = vectors(sh_ref, b, 1)
         turn = mirror(c, sh_ref, b, 1)
         scale = decay_scales(c, rows_ref, b, 1, "left")
+        values = []
         for group in range(2):
             picked = down(
                 *(
@@ -366,17 +397,17 @@
             )
             u32 = nn(turn, picked.astype(bf16))
             u2_ref[b, group] = u32.astype(bf16)
-            left, total = scale[group]
-            s_ref[group] = update(c, total, s_ref[group], writes, u32 * left)
+            values.append(u32 * scale[group][0])
             hi, lo = cotangent_of(cot_ref, b, group)
             dy = hi.astype(f32) + lo.astype(f32)
             skip_ref[group : group + 1, :] += jnp.sum(u32 * dy, axis=0, keepdims=True)
+        update(s_ref, [one[1] for one in scale], writes, values)
 
     over_blocks(step, "regrid")
 
 
 def regrid_backward(
-    place_ref, rows_ref, tok_ref, sh_ref, keep_ref, got_ref, skip_two_ref, _, dy1_ref, ends_ref, grid_ref, skip_ref, a_ref
+    place_ref, rows_ref, tok_ref, sh_ref, keep_ref, got_ref, skip_two_ref, dy1_ref, ends_ref, grid_ref, skip_ref, a_ref
 ):
     z = place_ref[0]
     c = constants()
@@ -391,6 +422,7 @@
         _, reads = vectors(sh_ref, b, 0)
         turn = mirror(c, sh_ref, b, 0)
         scale = decay_scales(c, rows_ref, b, 0, "grown")
+        values = []
         for group in range(2):
             picked = down(
                 *(
@@ -401,10 +433,10 @@
             )
             dy = nn(turn, picked.astype(bf16))
             dy1_ref[b, group] = dy.astype(bf16)
-            grown, total = scale[group]
-            a_ref[group] = update(c, total, a_ref[group], reads, dy * grown)
+            values.append(dy * scale[group][0])
             u = inputs_of(tok_ref, b, group).astype(f32)
             skip_ref[group : group + 1, :] += jnp.sum(u * dy, axis=0, keepdims=True)
+        update(a_ref, [one[1] for one in scale], reads, values)
 
     over_blocks(step, "regrid")
     for group in range(2):
@@ -581,13 +613,14 @@
         out_ref[x, 1104:1120, :] = other_two_ref[x, 256:272, :]
 
 
-def last_kernel(place_ref, back_ref, grad_ref, w1, r1, w2, r2, decay1_ref, decay2_ref, skip_ref):
+def last_kernel(place_ref, back_ref, grad_ref, w1, r1, w2, r2, decay1_ref, decay2_ref, skip1_ref, skip2_ref):
     core = place_ref[2]
 
     def chosen(ref, x, at, size, owner):
         near, far = ref[x, at : at + size, :], ref[x, at + size : at + 2 * size, :]
         return jnp.where(core == owner, near, far)
 
+    lanes = []
     for x in range(4):
         for owner in range(2):
             both = chosen(back_ref, x, 0, 256, owner)
@@ -600,7 +633,21 @@
             small = chosen(back_ref, x, 1088, 16, owner).astype(f32)
             decay2_ref[at : at + 4, :] = small[0:4] + small[4:8]
             small = chosen(back_ref, x, 800, 16, owner).astype(f32)
-            skip_ref[at : at + 4, :] = small[0:4] + small[4:8] + small[8:12]
+            lanes.append(small[0:4] + small[4:8] + small[8:12])
+    lanes = down(*lanes)
+    row, head = (lax.broadcasted_iota(jnp.int32, (32, 32), k) for k in range(2))
+    lane, side = (lax.broadcasted_iota(jnp.int32, (LANES, 32), k) for k in range(2))
+    folded = lax.dot_general(
+        lanes,
+        one_where(lane // HALF == side % 2),
+        (((1,), (0,)), ((), ())),
+        precision=lax.Precision.HIGHEST,
+        preferred_element_type=f32,
+    )
+    owner = (row // 4 == head // 4) & (row % 2 == head // 2 % 2)
+    for layer, ref in enumerate((skip1_ref, skip2_ref)):
+        kept = jnp.where(owner & (row // 2 % 2 == layer), folded, 0.0)
+        ref[...] = jnp.sum(kept, axis=0, keepdims=True) * SKIP_SCALE
     for ref, at in ((w1, 512), (r1, 640), (w2, 832), (r2, 960)):
         total = back_ref[0, at : at + 128, :].astype(f32)
         for x in range(1, 4):
@@ -765,8 +812,6 @@
         keep_back,
         got_back,
         skip_two,
-        end,
-        anywhere=(7,),
     )
     end_back = swap(end_own, "z")
 
@@ -822,28 +867,25 @@
     )
     vector = ((length, LANES), bf16)
     decay = ((head_count, length), f32)
-    grad_input, w1, r1, w2, r2, decay1, decay2, skip_lanes = call(
+    skip = ((1, head_count), f32)
+    grad_input, w1, r1, w2, r2, decay1, decay2, skip1, skip2 = call(
         last_kernel,
-        [((length, features), bf16), vector, vector, vector, vector, decay, decay, ((head_count, LANES), f32)],
+        [((length, features), bf16), vector, vector, vector, vector, decay, decay, skip, skip],
         [],
         place,
         back,
         us=1,
     )
-    seq_count = lax.axis_size("z") * lax.axis_size("x") * lax.axis_size("core")
-    factor = 1.0 / math.sqrt(clips * seq_count * length * head_size)
-    skip_grads = skip_lanes.reshape(8, 2, 2, 2, head_size).sum(-1)
-    skip_grads = skip_grads.transpose(1, 0, 2, 3).reshape(2, head_count) * factor
     return (
         grad_input[None],
         w1[None],
         r1[None],
         decay1[None],
-        skip_grads[0],
+        skip1.reshape(head_count),
         w2[None],
         r2[None],
         decay2[None],
-        skip_grads[1],
+        skip2.reshape(head_count),
     )
 
 

time: 162 us -> 153 us (0.944)
  blocking collectives: 36.2 us -> 31 us
  starting transfers between devices: 34.7 us -> 31.2 us
  waiting for transfers between devices: 44.6 us -> 47.3 us
  Pallas kernels: 43 us -> 41 us
    all_to_all x1, blocking collectives: 17.9 us -> 12.8 us  [on_device(): lax.all_to_all(skip_sums, 'dp', split_axis=0, concat_axis=0, tiled=True)]
    ppermute x8, starting transfers between devices: 22.7 us -> 19.4 us  [swap(): return lax.ppermute(values, axis, [(0, 1), (1, 0)])]
    ppermute x8, waiting for transfers between devices: 19.7 us -> 22.4 us  [swap(): return lax.ppermute(values, axis, [(0, 1), (1, 0)])]
    pallas_call x12, Pallas kernels: 43 us -> 41 us  [call(): pl.pallas_call(kernel, out_shape=shapes if many else shapes[0], in_specs=...]
  transfers between devices with their start and end apart: 10 -> 10, of which waited for: 5 -> 6; matrix products, arithmetic and copies ran while one was open for 0% -> 0% of each run, Pallas kernels for 10% -> 11%
where the time goes in v3:
time: 153 us
  waiting for transfers between devices  47.3 us (31%)
  Pallas kernels  41 us (27%)
  starting transfers between devices  31.2 us (20%)
  blocking collectives  31 us (20%)
    pallas_call x12, Pallas kernels, call(): pl.pallas_call(kernel, out_shape=shapes if many else shapes[0], in_specs=...  41 us
    all_to_all x1, waiting for transfers between devices, over_x(): return lax.all_to_all(values, 'x', split_axis=0, concat_axis=0, tiled=True)  24.9 us
    ppermute x8, waiting for transfers between devices, swap(): return lax.ppermute(values, axis, [(0, 1), (1, 0)])  22.4 us
    ppermute x8, starting transfers between devices, swap(): return lax.ppermute(values, axis, [(0, 1), (1, 0)])  19.4 us
    all_to_all x1, blocking collectives, over_x(): return lax.all_to_all(values, 'x', split_axis=0, concat_axis=0, tiled=True)  18.2 us
    all_to_all x1, blocking collectives, on_device(): lax.all_to_all(skip_sums, 'dp', split_axis=0, concat_axis=0, tiled=True)  12.8 us
    ppermute x1, starting transfers between devices, on_device(): end = lax.ppermute(end, 'z', [(0, 1)])  6.97 us
    all_to_all x1, starting transfers between devices, over_x(): return lax.all_to_all(values, 'x', split_axis=0, concat_axis=0, tiled=True)  4.85 us
  transfers between devices with their start and end apart: 10, of which 6 were waited for; matrix products, arithmetic and copies ran while one was open for 0% of the time, Pallas kernels for 11%

profile of v3, /device:TPU:1, one launch (start us, length us, event | category | flops | bytes accessed | tf_op | source)
XLA Modules:
  0.0 152.5 jit_solution(16343831331192962337)
XLA Ops:
  0.6 3.0 %pack_kernel.1 = bf16[4,2096,128]{2,1,0:T(8,128)(2,1)} custom-call(bf16[128,2048]{1,0:T(8,128)(2,1)} %bitcast.23, f32[32,128]{1,0:T(8,128)} %bitcast.28, f32[32,128]{1,0:T(8,128)} %bitcast.29, bf16[128,128]{1,0:T(8,128)(2,1)} %bitcast.24, bf16[128,128]{1,0:T(8,128)(2,1)} %bitcast.25, bf16[128,128]{1,0:T(8,128)(2,1)} %bitcast.26, bf16[128,128]{1,0:T(8,128)(2,1)} %bitcast.27, ...), custom_call_target="tpu_custom_call" | custom-call | flops 2000000000 | bytes 1000000 | tf_op jit(solution)/shard_map/pack_kernel/pallas_call | solution.py:671
  3.7 4.9 %all-to-all-start = ((bf16[4,2096,128]{2,1,0:T(8,128)(2,1)}), bf16[4,2096,128]{2,1,0:T(8,128)(2,1)S(1)}, u32[]{:S(2)}, u32[]{:S(2)}) async-start(bf16[4,2096,128]{2,1,0:T(8,128)(2,1)} %pack_kernel.1), calls=%async_computation | async-start | bytes 4292608 | tf_op jit(solution)/shard_map/all_to_all | solution.py:693
  8.5 24.9 %all-to-all-done.own = bf16[4,2096,128]{2,1,0:T(8,128)(2,1)S(1)} async-done(((bf16[4,2096,128]{2,1,0:T(8,128)(2,1)}), bf16[4,2096,128]{2,1,0:T(8,128)(2,1)S(1)}, u32[]{:S(2)}, u32[]{:S(2)}) %all-to-all-start) | async-done | bytes 2146336 | tf_op jit(solution)/shard_map/all_to_all | solution.py:693
  33.4 1.2 constant_dynamic-slice_fusion
  34.6 2.9 %collective-permute-start = (bf16[4,1312,128]{2,1,0:T(8,128)(2,1)}, bf16[4,1312,128]{2,1,0:T(8,128)(2,1)S(1)}, u32[]{:S(2)}, u32[]{:S(2)}) collective-permute-start(bf16[4,1312,128]{2,1,0:T(8,128)(2,1)} %constant_dynamic-slice_fusion), channel_id=1, source_target_pairs={{0,1},{1,0},{2,3},{3,2},{4,5},{5,4},{6,7},{7,6},{8,9},{9,8},{10,11... | collective-permute-start | bytes 4030472 | tf_op jit(solution)/shard_map/ppermute | solution.py:689
  37.5 0.1 pad_add_fusion.place_ref
  37.6 0.0 copy-start.1
  37.6 2.8 %collective-permute-done.other = bf16[4,1312,128]{2,1,0:T(8,128)(2,1)S(1)} collective-permute-done((bf16[4,1312,128]{2,1,0:T(8,128)(2,1)}, bf16[4,1312,128]{2,1,0:T(8,128)(2,1)S(1)}, u32[]{:S(2)}, u32[]{:S(2)}) %collective-permute-start) | collective-permute-done | bytes 1343520 | tf_op jit(solution)/shard_map/ppermute | solution.py:689
  40.4 6.5 %gather_kernel.1 = (bf16[8,272,128]{2,1,0:T(8,128)(2,1)S(1)}, bf16[8,512,128]{2,1,0:T(8,128)(2,1)S(1)}, bf16[8,528,128]{2,1,0:T(8,128)(2,1)S(1)}, f32[2,128,128]...) custom-call(s32[3]{0:T(128)S(1)} %pad_add_fusion.place_ref, ...), custom_call_target="tpu_custom_call" | custom-call | flops 5000000000 | bytes 1000000 | tf_op jit(solution)/shard_map/gather_kernel/pallas_call | solution.py:671
  47.0 7.0 %collective-permute-start.1 = (f32[2,128,128]{2,1,0:T(8,128)S(1)}, f32[2,128,128]{2,1,0:T(8,128)S(1)}, u32[]{:S(2)}, u32[]{:S(2)}) collective-permute-start(f32[2,128,128]{2,1,0:T(8,128)S(1)} %get-tuple-element.42), channel_id=1, source_target_pairs={{0,8},{8,0},{1,9},{9,1},{2,10},{10,2},{3,11},{11,3},{4,12},{12,4},... | collective-permute-start | bytes 393224 | tf_op jit(solution)/shard_map/ppermute | solution.py:689
  54.0 3.6 %collective-permute-done.1.ends_ref = f32[2,128,128]{2,1,0:T(8,128)S(1)} collective-permute-done((f32[2,128,128]{2,1,0:T(8,128)S(1)}, f32[2,128,128]{2,1,0:T(8,128)S(1)}, u32[]{:S(2)}, u32[]{:S(2)}) %collective-permute-start.1) | collective-permute-done | bytes 131104 | tf_op jit(solution)/shard_map/ppermute | solution.py:689
  57.5 0.0 copy-done.1
  57.5 0.0 copy-start
  57.5 5.0 %first_forward.1 = (bf16[2,512,128]{2,1,0:T(8,128)(2,1)S(1)}, bf16[2,512,128]{2,1,0:T(8,128)(2,1)S(1)}, bf16[8,2,256,128]{3,2,1,0:T(8,128)(2,1)S(1)}) custom-call(s32[3]{0:T(128)S(1)} %pad_add_fusion.place_ref, f32[32]{0:T(128)S(1)} %copy-done.1, bf16[2,8,32,128]{3,2,1,0:T(8,128)(2,1)S(1)} %get-tuple-element.37.rows_ref, ...), custom_call_target="tpu_custom_call" | custom-call | flops 5000000000 | bytes 1000000 | tf_op jit(solution)/shard_map/first_forward/pallas_call | solution.py:671
  62.6 5.1 %collective-permute-start.3 = (bf16[2,512,128]{2,1,0:T(8,128)(2,1)S(1)}, bf16[2,512,128]{2,1,0:T(8,128)(2,1)S(1)}, u32[]{:S(2)}, u32[]{:S(2)}) collective-permute-start(bf16[2,512,128]{2,1,0:T(8,128)(2,1)S(1)} %get-tuple-element.46), channel_id=1, source_target_pairs={{0,8},{8,0},{1,9},{9,1},{2,10},{10,2},{3,11},{11,3},{4,12},{12,4},... | collective-permute-start | bytes 786440 | tf_op jit(solution)/shard_map/ppermute | solution.py:689
  67.7 0.0 copy-done
  67.7 5.9 %first_backward.1 = (bf16[2,512,128]{2,1,0:T(8,128)(2,1)S(1)}, bf16[2,512,128]{2,1,0:T(8,128)(2,1)S(1)}, bf16[8,2,256,128]{3,2,1,0:T(8,128)(2,1)S(1)}) custom-call(s32[3]{0:T(128)S(1)} %pad_add_fusion.place_ref, f32[32]{0:T(128)S(1)} %copy-done, bf16[2,8,32,128]{3,2,1,0:T(8,128)(2,1)S(1)} %get-tuple-element.37.rows_ref, ...), custom_call_target="tpu_custom_call" | custom-call | flops 5000000000 | bytes 1000000 | tf_op jit(solution)/shard_map/first_backward/pallas_call | solution.py:671
  73.6 0.4 collective-permute-start.2
  74.0 0.0 collective-permute-done.3.got_ref
  74.0 2.5 %regrid_forward.1 = (bf16[8,2,128,128]{3,2,1,0:T(8,128)(2,1)S(1)}, f32[2,128,128]{2,1,0:T(8,128)S(1)}, f32[8,128]{1,0:T(8,128)S(1)}) custom-call(s32[3]{0:T(128)S(1)} %pad_add_fusion.place_ref, bf16[2,8,32,128]{3,2,1,0:T(8,128)(2,1)S(1)} %get-tuple-element.37.rows_ref, bf16[8,528,128]{2,1,0:T(8,128)(2,1)S(1)} %get-tuple-element.40.sh_ref, ...), custom_call_target="tpu_custom_call" | custom-call | flops 5000000000 | bytes 1000000 | tf_op jit(solution)/shard_map/regrid_forward/pallas_call | solution.py:671
  76.5 7.0 %collective-permute-start.5 = (f32[2,128,128]{2,1,0:T(8,128)S(1)}, f32[2,128,128]{2,1,0:T(8,128)S(1)}, u32[]{:S(2)}, u32[]{:S(2)}) collective-permute-start(f32[2,128,128]{2,1,0:T(8,128)S(1)} %get-tuple-element.53), channel_id=1, source_target_pairs={{0,8},{1,9},{2,10},{3,11},{4,12},{5,13},{6,14},{7,15},{16,24},{17,... | collective-permute-start | bytes 393224 | tf_op jit(solution)/shard_map/ppermute | solution.py:803
  83.5 12.5 %collective-permute-done.2.got_ref = bf16[2,512,128]{2,1,0:T(8,128)(2,1)S(1)} collective-permute-done((bf16[2,512,128]{2,1,0:T(8,128)(2,1)S(1)}, bf16[2,512,128]{2,1,0:T(8,128)(2,1)S(1)}, u32[]{:S(2)}, u32[]{:S(2)}) %collective-permute-start.2) | collective-permute-done | bytes 262176 | tf_op jit(solution)/shard_map/ppermute | solution.py:689
  96.0 1.9 %regrid_backward.1 = (bf16[8,2,128,128]{3,2,1,0:T(8,128)(2,1)S(1)}, f32[264,128]{1,0:T(8,128)S(1)}) custom-call(s32[3]{0:T(128)S(1)} %pad_add_fusion.place_ref, bf16[2,8,32,128]{3,2,1,0:T(8,128)(2,1)S(1)} %get-tuple-element.37.rows_ref, bf16[8,272,128]{2,1,0:T(8,128)(2,1)S(1)} %get-tuple-element.39.tok_ref, ...), custom_call_target="tpu_custom_call" | custom-call | flops 5000000000 | bytes 1000000 | tf_op jit(solution)/shard_map/regrid_backward/pallas_call | solution.py:671
  97.9 1.3 collective-permute-start.4
  99.2 0.0 collective-permute-done.5.ends_ref
  99.2 6.7 %second_forward.1._second.source.own_two_ref = bf16[2,4,272,128]{3,2,1,0:T(8,128)(2,1)S(1)} custom-call(s32[3]{0:T(128)S(1)} %pad_add_fusion.place_ref, bf16[2,8,32,128]{3,2,1,0:T(8,128)(2,1)S(1)} %get-tuple-element.37.rows_ref, f32[8,8,128]{2,1,0:T(8,128)S(1)} %get-tuple-element.38.run_ref, bf16[8,528,128]{2,1,0:T(8,128)(2,1)S(1)} %get-tuple-element.40.sh_ref, ...), custom_call_target="tpu_custom_call" | custom-call | flops 8000000000 | bytes 1000000 | tf_op jit(solution)/shard_map/second_forward/pallas_call | solution.py:671
  105.9 2.6 %collective-permute-done.4.ends_ref = f32[264,128]{1,0:T(8,128)S(1)} collective-permute-done((f32[264,128]{1,0:T(8,128)S(1)}, f32[264,128]{1,0:T(8,128)S(1)}, u32[]{:S(2)}, u32[]{:S(2)}) %collective-permute-start.4) | collective-permute-done | bytes 135200 | tf_op jit(solution)/shard_map/ppermute | solution.py:689
  108.5 6.6 %second_backward.1 = (bf16[2,4,528,128]{3,2,1,0:T(8,128)(2,1)S(1)}, f32[16,8,128]{2,1,0:T(8,128)S(1)}) custom-call(s32[3]{0:T(128)S(1)} %pad_add_fusion.place_ref, f32[32]{0:T(128)S(1)} %copy-done.1, bf16[2,8,32,128]{3,2,1,0:T(8,128)(2,1)S(1)} %get-tuple-element.37.rows_ref, f32[8,8,128]{2,1,0:T(8,128)S(1)} %get-tuple-element.38.run_ref, ...), custom_call_target="tpu_custom_call" | custom-call | flops 8000000000 | bytes 1000000 | tf_op jit(solution)/shard_map/second_backward/pallas_call | solution.py:671
  115.1 0.7 pick_second.2
  115.8 0.6 collective-permute-start.6
  116.5 0.4 pick_second.3
  116.9 0.1 collective-permute-start.7
  117.0 12.8 %all_to_all.15.skip_ref = f32[16,8,128]{2,1,0:T(8,128)S(1)} all-to-all(f32[16,8,128]{2,1,0:T(8,128)S(1)} %get-tuple-element.55), channel_id=1, replica_groups=mesh['dp'=16,'z'=2,'x'=4,'core'=2] {'dp'}, dimensions={0} | all-to-all | bytes 131072 | tf_op jit(solution)/shard_map/all_to_all | solution.py:852
  129.8 1.9 %collective-permute-start.8 = (f32[16,8,128]{2,1,0:T(8,128)S(1)}, f32[16,8,128]{2,1,0:T(8,128)S(1)}, u32[]{:S(2)}, u32[]{:S(2)}) collective-permute-start(f32[16,8,128]{2,1,0:T(8,128)S(1)} %all_to_all.15.skip_ref), channel_id=1, source_target_pairs={{0,1},{1,0},{2,3},{3,2},{4,5},{5,4},{6,7},{7,6},{8,9},{9,8},{10,11... | collective-permute-start | bytes 196616 | tf_op jit(solution)/shard_map/ppermute | solution.py:689
  131.7 0.9 collective-permute-done.8.skip_other_ref
  132.6 0.0 collective-permute-done.7.other_two_ref
  132.6 0.0 collective-permute-done.6.other_ref
  132.6 0.1 pair_kernel.1
  132.8 18.2 %all_to_all.16.back_ref = bf16[4,1120,128]{2,1,0:T(8,128)(2,1)S(1)} all-to-all(bf16[4,1120,128]{2,1,0:T(8,128)(2,1)S(1)} %pair_kernel.1), channel_id=1, replica_groups=mesh['dp'=16,'z'=2,'x'=4,'core'=2] {'x'}, dimensions={0} | all-to-all | bytes 2293760 | tf_op jit(solution)/shard_map/all_to_all | solution.py:693
  150.9 1.6 %last_kernel.1 = (bf16[128,2048]{1,0:T(8,128)(2,1)}, bf16[128,128]{1,0:T(8,128)(2,1)}, bf16[128,128]{1,0:T(8,128)(2,1)}, bf16[128,128]{1,0:T(8,128)(2,1)}, bf16[...) custom-call(s32[3]{0:T(128)S(1)} %pad_add_fusion.place_ref, ...), custom_call_target="tpu_custom_call" | custom-call | flops 1000000000 | bytes 1000000 | tf_op jit(solution)/shard_map/last_kernel/pallas_call | solution.py:671
Async XLA Ops:
  3.7 29.8 %all-to-all-start = ((bf16[4,2096,128]{2,1,0:T(8,128)(2,1)}), bf16[4,2096,128]{2,1,0:T(8,128)(2,1)S(1)}, u32[]{:S(2)}, u32[]{:S(2)}) async-start(bf16[4,2096,128]{2,1,0:T(8,128)(2,1)} %pack_kernel.1), calls=%async_computation | async-start | bytes 4292608 | tf_op jit(solution)/shard_map/all_to_all | solution.py:693
  34.6 5.8 %collective-permute-start = (bf16[4,1312,128]{2,1,0:T(8,128)(2,1)}, bf16[4,1312,128]{2,1,0:T(8,128)(2,1)S(1)}, u32[]{:S(2)}, u32[]{:S(2)}) collective-permute-start(bf16[4,1312,128]{2,1,0:T(8,128)(2,1)} %constant_dynamic-slice_fusion), channel_id=1, source_target_pairs={{0,1},{1,0},{2,3},{3,2},{4,5},{5,4},{6,7},{7,6},{8,9},{9,8},{10,11... | collective-permute-start | bytes 4030472 | tf_op jit(solution)/shard_map/ppermute | solution.py:689
  37.6 19.9 %copy-start.1 = (f32[32]{0:T(128)S(1)}, f32[32]{0:T(128)}, u32[]{:S(2)}) copy-start(f32[32]{0:T(128)} %skip_ref.5) | copy-start | bytes 388
  47.0 10.6 %collective-permute-start.1 = (f32[2,128,128]{2,1,0:T(8,128)S(1)}, f32[2,128,128]{2,1,0:T(8,128)S(1)}, u32[]{:S(2)}, u32[]{:S(2)}) collective-permute-start(f32[2,128,128]{2,1,0:T(8,128)S(1)} %get-tuple-element.42), channel_id=1, source_target_pairs={{0,8},{8,0},{1,9},{9,1},{2,10},{10,2},{3,11},{11,3},{4,12},{12,4},... | collective-permute-start | bytes 393224 | tf_op jit(solution)/shard_map/ppermute | solution.py:689
  57.5 10.2 %copy-start = (f32[32]{0:T(128)S(1)}, f32[32]{0:T(128)}, u32[]{:S(2)}) copy-start(f32[32]{0:T(128)} %skip_ref.3) | copy-start | bytes 388
  62.6 11.4 %collective-permute-start.3 = (bf16[2,512,128]{2,1,0:T(8,128)(2,1)S(1)}, bf16[2,512,128]{2,1,0:T(8,128)(2,1)S(1)}, u32[]{:S(2)}, u32[]{:S(2)}) collective-permute-start(bf16[2,512,128]{2,1,0:T(8,128)(2,1)S(1)} %get-tuple-element.46), channel_id=1, source_target_pairs={{0,8},{8,0},{1,9},{9,1},{2,10},{10,2},{3,11},{11,3},{4,12},{12,4},... | collective-permute-start | bytes 786440 | tf_op jit(solution)/shard_map/ppermute | solution.py:689
  73.6 22.5 %collective-permute-start.2 = (bf16[2,512,128]{2,1,0:T(8,128)(2,1)S(1)}, bf16[2,512,128]{2,1,0:T(8,128)(2,1)S(1)}, u32[]{:S(2)}, u32[]{:S(2)}) collective-permute-start(bf16[2,512,128]{2,1,0:T(8,128)(2,1)S(1)} %get-tuple-element.44), channel_id=1, source_target_pairs={{0,8},{8,0},{1,9},{9,1},{2,10},{10,2},{3,11},{11,3},{4,12},{12,4},... | collective-permute-start | bytes 786440 | tf_op jit(solution)/shard_map/ppermute | solution.py:689
  76.5 22.7 %collective-permute-start.5 = (f32[2,128,128]{2,1,0:T(8,128)S(1)}, f32[2,128,128]{2,1,0:T(8,128)S(1)}, u32[]{:S(2)}, u32[]{:S(2)}) collective-permute-start(f32[2,128,128]{2,1,0:T(8,128)S(1)} %get-tuple-element.53), channel_id=1, source_target_pairs={{0,8},{1,9},{2,10},{3,11},{4,12},{5,13},{6,14},{7,15},{16,24},{17,... | collective-permute-start | bytes 393224 | tf_op jit(solution)/shard_map/ppermute | solution.py:803
  97.9 10.6 %collective-permute-start.4 = (f32[264,128]{1,0:T(8,128)S(1)}, f32[264,128]{1,0:T(8,128)S(1)}, u32[]{:S(2)}, u32[]{:S(2)}) collective-permute-start(f32[264,128]{1,0:T(8,128)S(1)} %get-tuple-element.50.own_ref), channel_id=1, source_target_pairs={{0,8},{8,0},{1,9},{9,1},{2,10},{10,2},{3,11},{11,3},{4,12},{12,4},... | collective-permute-start | bytes 405512 | tf_op jit(solution)/shard_map/ppermute | solution.py:689
  115.8 16.8 %collective-permute-start.6 = (bf16[4,528,128]{2,1,0:T(8,128)(2,1)S(1)}, bf16[4,528,128]{2,1,0:T(8,128)(2,1)S(1)}, u32[]{:S(2)}, u32[]{:S(2)}) collective-permute-start(bf16[4,528,128]{2,1,0:T(8,128)(2,1)S(1)} %pick_second.2), channel_id=1, source_target_pairs={{0,1},{1,0},{2,3},{3,2},{4,5},{5,4},{6,7},{7,6},{8,9},{9,8},{10,11... | collective-permute-start | bytes 1622024 | tf_op jit(solution)/shard_map/ppermute | solution.py:689
  116.9 15.7 %collective-permute-start.7 = (bf16[4,272,128]{2,1,0:T(8,128)(2,1)S(1)}, bf16[4,272,128]{2,1,0:T(8,128)(2,1)S(1)}, u32[]{:S(2)}, u32[]{:S(2)}) collective-permute-start(bf16[4,272,128]{2,1,0:T(8,128)(2,1)S(1)} %pick_second.3), channel_id=1, source_target_pairs={{0,1},{1,0},{2,3},{3,2},{4,5},{5,4},{6,7},{7,6},{8,9},{9,8},{10,11... | collective-permute-start | bytes 835592 | tf_op jit(solution)/shard_map/ppermute | solution.py:689
  129.8 2.8 %collective-permute-start.8 = (f32[16,8,128]{2,1,0:T(8,128)S(1)}, f32[16,8,128]{2,1,0:T(8,128)S(1)}, u32[]{:S(2)}, u32[]{:S(2)}) collective-permute-start(f32[16,8,128]{2,1,0:T(8,128)S(1)} %all_to_all.15.skip_ref), channel_id=1, source_target_pairs={{0,1},{1,0},{2,3},{3,2},{4,5},{5,4},{6,7},{7,6},{8,9},{9,8},{10,11... | collective-permute-start | bytes 196616 | tf_op jit(solution)/shard_map/ppermute | solution.py:689

commit v4 on v3

--- a/solution.py
+++ b/solution.py
@@ -294,7 +294,7 @@
     for one in copies[16:]:
         one.wait()
     over_blocks(backward, "gather")
-    ends_ref[...] = jnp.where(z == 0, s_ref[...], a_ref[...])
+    ends_ref[...] = jnp.where(z == 0, s_ref[...], a_ref[...]).astype(bf16)
 
 
 def pick_second(source, out_ref, sems):
@@ -304,7 +304,7 @@
 def first_forward(place_ref, skip_ref, rows_ref, run_ref, tok_ref, sh_ref, ends_ref, keep_ref, send_ref, state_ref, s_ref):
     z = place_ref[0]
     c = constants()
-    s_ref[...] = jnp.where(z == 1, ends_ref[...], 0.0)
+    s_ref[...] = jnp.where(z == 1, ends_ref[...].astype(f32), 0.0)
 
     def step(b):
         writes, reads = vectors(sh_ref, b, 0)
@@ -339,7 +339,7 @@
 def first_backward(place_ref, skip_ref, rows_ref, run_ref, sh_ref, cot_ref, ends_ref, keep_ref, send_ref, adjoint_ref, a_ref):
     z = place_ref[0]
     c = constants()
-    a_ref[...] = jnp.where(z == 0, ends_ref[...], 0.0)
+    a_ref[...] = jnp.where(z == 0, ends_ref[...].astype(f32), 0.0)
 
     def step(i):
         b = BLOCKS - 1 - i
@@ -373,7 +373,7 @@
 
 
 def regrid_forward(
-    place_ref, rows_ref, sh_ref, cot_ref, keep_ref, got_ref, u2_ref, s_ref, skip_ref, grid_ref
+    place_ref, rows_ref, sh_ref, cot_ref, keep_ref, got_ref, u2_ref, ends_ref, skip_ref, grid_ref, s_ref
 ):
     z = place_ref[0]
     c = constants()
@@ -404,6 +404,7 @@
         update(s_ref, [one[1] for one in scale], writes, values)
 
     over_blocks(step, "regrid")
+    ends_ref[...] = s_ref[...].astype(bf16)
 
 
 def regrid_backward(
@@ -523,7 +524,7 @@
 def second_forward(place_ref, rows_ref, run_ref, sh_ref, cot_ref, u2_ref, adjoint_ref, ends_ref, out_ref, s_ref):
     core = place_ref[2]
     c = constants()
-    s_ref[...] = ends_ref[...]
+    s_ref[...] = ends_ref[...].astype(f32)
 
     def step(b):
         d_writes, d_reads, rows, kept, writes_two, _ = block_gradients(
@@ -745,6 +746,7 @@
     other = swap(theirs, "core")
 
     carry = ((2, LANES, LANES), f32)
+    sent = ((2, LANES, LANES), bf16)
     saved = ((BLOCKS, 2, 2 * LANES, LANES), bf16)
     half_grid = ((2, 512, LANES), bf16)
     block = ((BLOCKS, 2, BLOCK, LANES), bf16)
@@ -757,7 +759,7 @@
             ((BLOCKS, TOKEN_ROWS, LANES), bf16),
             ((BLOCKS, COT_ROWS, LANES), bf16),
             ((BLOCKS, SHARED_ROWS, LANES), bf16),
-            carry,
+            sent,
             ((2, BLOCKS, 32, LANES), bf16),
             ((BLOCKS, 8, LANES), f32),
         ],
@@ -798,7 +800,7 @@
     )
     got_back = swap(send_back, "z")
     u2, end, skip_two = call(
-        regrid_forward, [block, carry, few], [grids], place, rows, sh, cot, keep, got
+        regrid_forward, [block, sent, few], [grids, carry], place, rows, sh, cot, keep, got
     )
     end = lax.ppermute(end, "z", [(0, 1)])
     dy1, end_own = call(

time: 153 us -> 149 us (0.974)
  waiting for transfers between devices: 47.3 us -> 40.9 us
  starting transfers between devices: 31.2 us -> 33.7 us
    ppermute x8, waiting for transfers between devices: 22.4 us -> 16 us  [swap(): return lax.ppermute(values, axis, [(0, 1), (1, 0)])]
    ppermute x8, starting transfers between devices: 19.4 us -> 22 us  [swap(): return lax.ppermute(values, axis, [(0, 1), (1, 0)])]
  transfers between devices with their start and end apart: 10 -> 10, of which waited for: 6 -> 6; matrix products, arithmetic and copies ran while one was open for 0% -> 0% of each run, Pallas kernels for 11% -> 12%
where the time goes in v4:
time: 149 us
  Pallas kernels  41 us (28%)
  waiting for transfers between devices  40.9 us (27%)
  starting transfers between devices  33.7 us (23%)
  blocking collectives  31.2 us (21%)
    pallas_call x12, Pallas kernels, call(): pl.pallas_call(kernel, out_shape=shapes if many else shapes[0], in_specs=...  41 us
    all_to_all x1, waiting for transfers between devices, over_x(): return lax.all_to_all(values, 'x', split_axis=0, concat_axis=0, tiled=True)  24.9 us
    ppermute x8, starting transfers between devices, swap(): return lax.ppermute(values, axis, [(0, 1), (1, 0)])  22 us
    all_to_all x1, blocking collectives, over_x(): return lax.all_to_all(values, 'x', split_axis=0, concat_axis=0, tiled=True)  18.3 us
    ppermute x8, waiting for transfers between devices, swap(): return lax.ppermute(values, axis, [(0, 1), (1, 0)])  16 us
    all_to_all x1, blocking collectives, on_device(): lax.all_to_all(skip_sums, 'dp', split_axis=0, concat_axis=0, tiled=True)  12.9 us
    ppermute x1, starting transfers between devices, on_device(): end = lax.ppermute(end, 'z', [(0, 1)])  6.87 us
    all_to_all x1, starting transfers between devices, over_x(): return lax.all_to_all(values, 'x', split_axis=0, concat_axis=0, tiled=True)  4.85 us
  transfers between devices with their start and end apart: 10, of which 6 were waited for; matrix products, arithmetic and copies ran while one was open for 0% of the time, Pallas kernels for 12%

profile of v4, /device:TPU:1, one launch (start us, length us, event | category | flops | bytes accessed | tf_op | source)
XLA Modules:
  0.0 148.9 jit_solution(3428396469957452277)
XLA Ops:
  0.6 3.0 %pack_kernel.1 = bf16[4,2096,128]{2,1,0:T(8,128)(2,1)} custom-call(bf16[128,2048]{1,0:T(8,128)(2,1)} %bitcast.23, f32[32,128]{1,0:T(8,128)} %bitcast.28, f32[32,128]{1,0:T(8,128)} %bitcast.29, bf16[128,128]{1,0:T(8,128)(2,1)} %bitcast.24, bf16[128,128]{1,0:T(8,128)(2,1)} %bitcast.25, bf16[128,128]{1,0:T(8,128)(2,1)} %bitcast.26, bf16[128,128]{1,0:T(8,128)(2,1)} %bitcast.27, ...), custom_call_target="tpu_custom_call" | custom-call | flops 2000000000 | bytes 1000000 | tf_op jit(solution)/shard_map/pack_kernel/pallas_call | solution.py:672
  3.7 4.9 %all-to-all-start = ((bf16[4,2096,128]{2,1,0:T(8,128)(2,1)}), bf16[4,2096,128]{2,1,0:T(8,128)(2,1)S(1)}, u32[]{:S(2)}, u32[]{:S(2)}) async-start(bf16[4,2096,128]{2,1,0:T(8,128)(2,1)} %pack_kernel.1), calls=%async_computation | async-start | bytes 4292608 | tf_op jit(solution)/shard_map/all_to_all | solution.py:694
  8.5 24.9 %all-to-all-done.own = bf16[4,2096,128]{2,1,0:T(8,128)(2,1)S(1)} async-done(((bf16[4,2096,128]{2,1,0:T(8,128)(2,1)}), bf16[4,2096,128]{2,1,0:T(8,128)(2,1)S(1)}, u32[]{:S(2)}, u32[]{:S(2)}) %all-to-all-start) | async-done | bytes 2146336 | tf_op jit(solution)/shard_map/all_to_all | solution.py:694
  33.4 1.2 constant_dynamic-slice_fusion
  34.6 2.9 %collective-permute-start = (bf16[4,1312,128]{2,1,0:T(8,128)(2,1)}, bf16[4,1312,128]{2,1,0:T(8,128)(2,1)S(1)}, u32[]{:S(2)}, u32[]{:S(2)}) collective-permute-start(bf16[4,1312,128]{2,1,0:T(8,128)(2,1)} %constant_dynamic-slice_fusion), channel_id=1, source_target_pairs={{0,1},{1,0},{2,3},{3,2},{4,5},{5,4},{6,7},{7,6},{8,9},{9,8},{10,11... | collective-permute-start | bytes 4030472 | tf_op jit(solution)/shard_map/ppermute | solution.py:690
  37.5 0.1 pad_add_fusion.place_ref
  37.6 0.0 copy-start.1
  37.6 2.8 %collective-permute-done.other = bf16[4,1312,128]{2,1,0:T(8,128)(2,1)S(1)} collective-permute-done((bf16[4,1312,128]{2,1,0:T(8,128)(2,1)}, bf16[4,1312,128]{2,1,0:T(8,128)(2,1)S(1)}, u32[]{:S(2)}, u32[]{:S(2)}) %collective-permute-start) | collective-permute-done | bytes 1343520 | tf_op jit(solution)/shard_map/ppermute | solution.py:690
  40.4 6.5 %gather_kernel.1 = (bf16[8,272,128]{2,1,0:T(8,128)(2,1)S(1)}, bf16[8,512,128]{2,1,0:T(8,128)(2,1)S(1)}, bf16[8,528,128]{2,1,0:T(8,128)(2,1)S(1)}, bf16[2,128,128...) custom-call(s32[3]{0:T(128)S(1)} %pad_add_fusion.place_ref, ...), custom_call_target="tpu_custom_call" | custom-call | flops 5000000000 | bytes 1000000 | tf_op jit(solution)/shard_map/gather_kernel/pallas_call | solution.py:672
  47.0 7.0 %collective-permute-start.1 = (bf16[2,128,128]{2,1,0:T(8,128)(2,1)S(1)}, bf16[2,128,128]{2,1,0:T(8,128)(2,1)S(1)}, u32[]{:S(2)}, u32[]{:S(2)}) collective-permute-start(bf16[2,128,128]{2,1,0:T(8,128)(2,1)S(1)} %get-tuple-element.42), channel_id=1, source_target_pairs={{0,8},{8,0},{1,9},{9,1},{2,10},{10,2},{3,11},{11,3},{4,12},{12,4},... | collective-permute-start | bytes 196616 | tf_op jit(solution)/shard_map/ppermute | solution.py:690
  54.0 2.2 %collective-permute-done.1.ends_ref = bf16[2,128,128]{2,1,0:T(8,128)(2,1)S(1)} collective-permute-done((bf16[2,128,128]{2,1,0:T(8,128)(2,1)S(1)}, bf16[2,128,128]{2,1,0:T(8,128)(2,1)S(1)}, u32[]{:S(2)}, u32[]{:S(2)}) %collective-permute-start.1) | collective-permute-done | bytes 65568 | tf_op jit(solution)/shard_map/ppermute | solution.py:690
  56.1 0.0 copy-done.1
  56.1 0.0 copy-start
  56.1 5.0 %first_forward.1 = (bf16[2,512,128]{2,1,0:T(8,128)(2,1)S(1)}, bf16[2,512,128]{2,1,0:T(8,128)(2,1)S(1)}, bf16[8,2,256,128]{3,2,1,0:T(8,128)(2,1)S(1)}) custom-call(s32[3]{0:T(128)S(1)} %pad_add_fusion.place_ref, f32[32]{0:T(128)S(1)} %copy-done.1, bf16[2,8,32,128]{3,2,1,0:T(8,128)(2,1)S(1)} %get-tuple-element.37.rows_ref, ...), custom_call_target="tpu_custom_call" | custom-call | flops 5000000000 | bytes 1000000 | tf_op jit(solution)/shard_map/first_forward/pallas_call | solution.py:672
  61.2 5.0 %collective-permute-start.3 = (bf16[2,512,128]{2,1,0:T(8,128)(2,1)S(1)}, bf16[2,512,128]{2,1,0:T(8,128)(2,1)S(1)}, u32[]{:S(2)}, u32[]{:S(2)}) collective-permute-start(bf16[2,512,128]{2,1,0:T(8,128)(2,1)S(1)} %get-tuple-element.46), channel_id=1, source_target_pairs={{0,8},{8,0},{1,9},{9,1},{2,10},{10,2},{3,11},{11,3},{4,12},{12,4},... | collective-permute-start | bytes 786440 | tf_op jit(solution)/shard_map/ppermute | solution.py:690
  66.2 0.0 copy-done
  66.2 5.9 %first_backward.1 = (bf16[2,512,128]{2,1,0:T(8,128)(2,1)S(1)}, bf16[2,512,128]{2,1,0:T(8,128)(2,1)S(1)}, bf16[8,2,256,128]{3,2,1,0:T(8,128)(2,1)S(1)}) custom-call(s32[3]{0:T(128)S(1)} %pad_add_fusion.place_ref, f32[32]{0:T(128)S(1)} %copy-done, bf16[2,8,32,128]{3,2,1,0:T(8,128)(2,1)S(1)} %get-tuple-element.37.rows_ref, ...), custom_call_target="tpu_custom_call" | custom-call | flops 5000000000 | bytes 1000000 | tf_op jit(solution)/shard_map/first_backward/pallas_call | solution.py:672
  72.1 0.5 collective-permute-start.2
  72.6 0.0 collective-permute-done.3.got_ref
  72.6 2.5 %regrid_forward.1 = (bf16[8,2,128,128]{3,2,1,0:T(8,128)(2,1)S(1)}, bf16[2,128,128]{2,1,0:T(8,128)(2,1)S(1)}, f32[8,128]{1,0:T(8,128)S(1)}) custom-call(s32[3]{0:T(128)S(1)} %pad_add_fusion.place_ref, bf16[2,8,32,128]{3,2,1,0:T(8,128)(2,1)S(1)} %get-tuple-element.37.rows_ref, bf16[8,528,128]{2,1,0:T(8,128)(2,1)S(1)} %get-tuple-element.40.sh_ref, ...), custom_call_target="tpu_custom_call" | custom-call | flops 5000000000 | bytes 1000000 | tf_op jit(solution)/shard_map/regrid_forward/pallas_call | solution.py:672
  75.2 6.9 %collective-permute-start.5 = (bf16[2,128,128]{2,1,0:T(8,128)(2,1)S(1)}, bf16[2,128,128]{2,1,0:T(8,128)(2,1)S(1)}, u32[]{:S(2)}, u32[]{:S(2)}) collective-permute-start(bf16[2,128,128]{2,1,0:T(8,128)(2,1)S(1)} %get-tuple-element.53), channel_id=1, source_target_pairs={{0,8},{1,9},{2,10},{3,11},{4,12},{5,13},{6,14},{7,15},{16,24},{17,... | collective-permute-start | bytes 196616 | tf_op jit(solution)/shard_map/ppermute | solution.py:805
  82.0 9.6 %collective-permute-done.2.got_ref = bf16[2,512,128]{2,1,0:T(8,128)(2,1)S(1)} collective-permute-done((bf16[2,512,128]{2,1,0:T(8,128)(2,1)S(1)}, bf16[2,512,128]{2,1,0:T(8,128)(2,1)S(1)}, u32[]{:S(2)}, u32[]{:S(2)}) %collective-permute-start.2) | collective-permute-done | bytes 262176 | tf_op jit(solution)/shard_map/ppermute | solution.py:690
  91.6 1.9 %regrid_backward.1 = (bf16[8,2,128,128]{3,2,1,0:T(8,128)(2,1)S(1)}, f32[264,128]{1,0:T(8,128)S(1)}) custom-call(s32[3]{0:T(128)S(1)} %pad_add_fusion.place_ref, bf16[2,8,32,128]{3,2,1,0:T(8,128)(2,1)S(1)} %get-tuple-element.37.rows_ref, bf16[8,272,128]{2,1,0:T(8,128)(2,1)S(1)} %get-tuple-element.39.tok_ref, ...), custom_call_target="tpu_custom_call" | custom-call | flops 5000000000 | bytes 1000000 | tf_op jit(solution)/shard_map/regrid_backward/pallas_call | solution.py:672
  93.5 2.4 %collective-permute-start.4 = (f32[264,128]{1,0:T(8,128)S(1)}, f32[264,128]{1,0:T(8,128)S(1)}, u32[]{:S(2)}, u32[]{:S(2)}) collective-permute-start(f32[264,128]{1,0:T(8,128)S(1)} %get-tuple-element.50.own_ref), channel_id=1, source_target_pairs={{0,8},{8,0},{1,9},{9,1},{2,10},{10,2},{3,11},{11,3},{4,12},{12,4},... | collective-permute-start | bytes 405512 | tf_op jit(solution)/shard_map/ppermute | solution.py:690
  95.9 0.0 collective-permute-done.5.ends_ref
  95.9 6.7 %second_forward.1._second.source.own_two_ref = bf16[2,4,272,128]{3,2,1,0:T(8,128)(2,1)S(1)} custom-call(s32[3]{0:T(128)S(1)} %pad_add_fusion.place_ref, bf16[2,8,32,128]{3,2,1,0:T(8,128)(2,1)S(1)} %get-tuple-element.37.rows_ref, f32[8,8,128]{2,1,0:T(8,128)S(1)} %get-tuple-element.38.run_ref, bf16[8,528,128]{2,1,0:T(8,128)(2,1)S(1)} %get-tuple-element.40.sh_ref, ...), custom_call_target="tpu_custom_call" | custom-call | flops 8000000000 | bytes 1000000 | tf_op jit(solution)/shard_map/second_forward/pallas_call | solution.py:672
  102.6 0.5 collective-permute-done.4.ends_ref
  103.1 6.6 %second_backward.1 = (bf16[2,4,528,128]{3,2,1,0:T(8,128)(2,1)S(1)}, f32[16,8,128]{2,1,0:T(8,128)S(1)}) custom-call(s32[3]{0:T(128)S(1)} %pad_add_fusion.place_ref, f32[32]{0:T(128)S(1)} %copy-done.1, bf16[2,8,32,128]{3,2,1,0:T(8,128)(2,1)S(1)} %get-tuple-element.37.rows_ref, f32[8,8,128]{2,1,0:T(8,128)S(1)} %get-tuple-element.38.run_ref, ...), custom_call_target="tpu_custom_call" | custom-call | flops 8000000000 | bytes 1000000 | tf_op jit(solution)/shard_map/second_backward/pallas_call | solution.py:672
  109.7 0.7 pick_second.2
  110.4 2.1 %collective-permute-start.6 = (bf16[4,528,128]{2,1,0:T(8,128)(2,1)S(1)}, bf16[4,528,128]{2,1,0:T(8,128)(2,1)S(1)}, u32[]{:S(2)}, u32[]{:S(2)}) collective-permute-start(bf16[4,528,128]{2,1,0:T(8,128)(2,1)S(1)} %pick_second.2), channel_id=1, source_target_pairs={{0,1},{1,0},{2,3},{3,2},{4,5},{5,4},{6,7},{7,6},{8,9},{9,8},{10,11... | collective-permute-start | bytes 1622024 | tf_op jit(solution)/shard_map/ppermute | solution.py:690
  112.6 0.4 pick_second.3
  113.0 0.1 collective-permute-start.7
  113.1 12.9 %all_to_all.15.skip_ref = f32[16,8,128]{2,1,0:T(8,128)S(1)} all-to-all(f32[16,8,128]{2,1,0:T(8,128)S(1)} %get-tuple-element.55), channel_id=1, replica_groups=mesh['dp'=16,'z'=2,'x'=4,'core'=2] {'dp'}, dimensions={0} | all-to-all | bytes 131072 | tf_op jit(solution)/shard_map/all_to_all | solution.py:854
  126.0 1.9 %collective-permute-start.8 = (f32[16,8,128]{2,1,0:T(8,128)S(1)}, f32[16,8,128]{2,1,0:T(8,128)S(1)}, u32[]{:S(2)}, u32[]{:S(2)}) collective-permute-start(f32[16,8,128]{2,1,0:T(8,128)S(1)} %all_to_all.15.skip_ref), channel_id=1, source_target_pairs={{0,1},{1,0},{2,3},{3,2},{4,5},{5,4},{6,7},{7,6},{8,9},{9,8},{10,11... | collective-permute-start | bytes 196616 | tf_op jit(solution)/shard_map/ppermute | solution.py:690
  127.9 0.9 collective-permute-done.8.skip_other_ref
  128.8 0.0 collective-permute-done.7.other_two_ref
  128.8 0.0 collective-permute-done.6.other_ref
  128.8 0.1 pair_kernel.1
  128.9 18.3 %all_to_all.16.back_ref = bf16[4,1120,128]{2,1,0:T(8,128)(2,1)S(1)} all-to-all(bf16[4,1120,128]{2,1,0:T(8,128)(2,1)S(1)} %pair_kernel.1), channel_id=1, replica_groups=mesh['dp'=16,'z'=2,'x'=4,'core'=2] {'x'}, dimensions={0} | all-to-all | bytes 2293760 | tf_op jit(solution)/shard_map/all_to_all | solution.py:694
  147.3 1.6 %last_kernel.1 = (bf16[128,2048]{1,0:T(8,128)(2,1)}, bf16[128,128]{1,0:T(8,128)(2,1)}, bf16[128,128]{1,0:T(8,128)(2,1)}, bf16[128,128]{1,0:T(8,128)(2,1)}, bf16[...) custom-call(s32[3]{0:T(128)S(1)} %pad_add_fusion.place_ref, ...), custom_call_target="tpu_custom_call" | custom-call | flops 1000000000 | bytes 1000000 | tf_op jit(solution)/shard_map/last_kernel/pallas_call | solution.py:672
Async XLA Ops:
  3.7 29.8 %all-to-all-start = ((bf16[4,2096,128]{2,1,0:T(8,128)(2,1)}), bf16[4,2096,128]{2,1,0:T(8,128)(2,1)S(1)}, u32[]{:S(2)}, u32[]{:S(2)}) async-start(bf16[4,2096,128]{2,1,0:T(8,128)(2,1)} %pack_kernel.1), calls=%async_computation | async-start | bytes 4292608 | tf_op jit(solution)/shard_map/all_to_all | solution.py:694
  34.6 5.8 %collective-permute-start = (bf16[4,1312,128]{2,1,0:T(8,128)(2,1)}, bf16[4,1312,128]{2,1,0:T(8,128)(2,1)S(1)}, u32[]{:S(2)}, u32[]{:S(2)}) collective-permute-start(bf16[4,1312,128]{2,1,0:T(8,128)(2,1)} %constant_dynamic-slice_fusion), channel_id=1, source_target_pairs={{0,1},{1,0},{2,3},{3,2},{4,5},{5,4},{6,7},{7,6},{8,9},{9,8},{10,11... | collective-permute-start | bytes 4030472 | tf_op jit(solution)/shard_map/ppermute | solution.py:690
  37.6 18.5 %copy-start.1 = (f32[32]{0:T(128)S(1)}, f32[32]{0:T(128)}, u32[]{:S(2)}) copy-start(f32[32]{0:T(128)} %skip_ref.5) | copy-start | bytes 388
  47.0 9.2 %collective-permute-start.1 = (bf16[2,128,128]{2,1,0:T(8,128)(2,1)S(1)}, bf16[2,128,128]{2,1,0:T(8,128)(2,1)S(1)}, u32[]{:S(2)}, u32[]{:S(2)}) collective-permute-start(bf16[2,128,128]{2,1,0:T(8,128)(2,1)S(1)} %get-tuple-element.42), channel_id=1, source_target_pairs={{0,8},{8,0},{1,9},{9,1},{2,10},{10,2},{3,11},{11,3},{4,12},{12,4},... | collective-permute-start | bytes 196616 | tf_op jit(solution)/shard_map/ppermute | solution.py:690
  56.1 10.1 %copy-start = (f32[32]{0:T(128)S(1)}, f32[32]{0:T(128)}, u32[]{:S(2)}) copy-start(f32[32]{0:T(128)} %skip_ref.3) | copy-start | bytes 388
  61.2 11.4 %collective-permute-start.3 = (bf16[2,512,128]{2,1,0:T(8,128)(2,1)S(1)}, bf16[2,512,128]{2,1,0:T(8,128)(2,1)S(1)}, u32[]{:S(2)}, u32[]{:S(2)}) collective-permute-start(bf16[2,512,128]{2,1,0:T(8,128)(2,1)S(1)} %get-tuple-element.46), channel_id=1, source_target_pairs={{0,8},{8,0},{1,9},{9,1},{2,10},{10,2},{3,11},{11,3},{4,12},{12,4},... | collective-permute-start | bytes 786440 | tf_op jit(solution)/shard_map/ppermute | solution.py:690
  72.1 19.5 %collective-permute-start.2 = (bf16[2,512,128]{2,1,0:T(8,128)(2,1)S(1)}, bf16[2,512,128]{2,1,0:T(8,128)(2,1)S(1)}, u32[]{:S(2)}, u32[]{:S(2)}) collective-permute-start(bf16[2,512,128]{2,1,0:T(8,128)(2,1)S(1)} %get-tuple-element.44), channel_id=1, source_target_pairs={{0,8},{8,0},{1,9},{9,1},{2,10},{10,2},{3,11},{11,3},{4,12},{12,4},... | collective-permute-start | bytes 786440 | tf_op jit(solution)/shard_map/ppermute | solution.py:690
  75.2 20.7 %collective-permute-start.5 = (bf16[2,128,128]{2,1,0:T(8,128)(2,1)S(1)}, bf16[2,128,128]{2,1,0:T(8,128)(2,1)S(1)}, u32[]{:S(2)}, u32[]{:S(2)}) collective-permute-start(bf16[2,128,128]{2,1,0:T(8,128)(2,1)S(1)} %get-tuple-element.53), channel_id=1, source_target_pairs={{0,8},{1,9},{2,10},{3,11},{4,12},{5,13},{6,14},{7,15},{16,24},{17,... | collective-permute-start | bytes 196616 | tf_op jit(solution)/shard_map/ppermute | solution.py:805
  93.5 9.6 %collective-permute-start.4 = (f32[264,128]{1,0:T(8,128)S(1)}, f32[264,128]{1,0:T(8,128)S(1)}, u32[]{:S(2)}, u32[]{:S(2)}) collective-permute-start(f32[264,128]{1,0:T(8,128)S(1)} %get-tuple-element.50.own_ref), channel_id=1, source_target_pairs={{0,8},{8,0},{1,9},{9,1},{2,10},{10,2},{3,11},{11,3},{4,12},{12,4},... | collective-permute-start | bytes 405512 | tf_op jit(solution)/shard_map/ppermute | solution.py:690
  110.4 18.4 %collective-permute-start.6 = (bf16[4,528,128]{2,1,0:T(8,128)(2,1)S(1)}, bf16[4,528,128]{2,1,0:T(8,128)(2,1)S(1)}, u32[]{:S(2)}, u32[]{:S(2)}) collective-permute-start(bf16[4,528,128]{2,1,0:T(8,128)(2,1)S(1)} %pick_second.2), channel_id=1, source_target_pairs={{0,1},{1,0},{2,3},{3,2},{4,5},{5,4},{6,7},{7,6},{8,9},{9,8},{10,11... | collective-permute-start | bytes 1622024 | tf_op jit(solution)/shard_map/ppermute | solution.py:690
  113.0 15.8 %collective-permute-start.7 = (bf16[4,272,128]{2,1,0:T(8,128)(2,1)S(1)}, bf16[4,272,128]{2,1,0:T(8,128)(2,1)S(1)}, u32[]{:S(2)}, u32[]{:S(2)}) collective-permute-start(bf16[4,272,128]{2,1,0:T(8,128)(2,1)S(1)} %pick_second.3), channel_id=1, source_target_pairs={{0,1},{1,0},{2,3},{3,2},{4,5},{5,4},{6,7},{7,6},{8,9},{9,8},{10,11... | collective-permute-start | bytes 835592 | tf_op jit(solution)/shard_map/ppermute | solution.py:690
  126.0 2.8 %collective-permute-start.8 = (f32[16,8,128]{2,1,0:T(8,128)S(1)}, f32[16,8,128]{2,1,0:T(8,128)S(1)}, u32[]{:S(2)}, u32[]{:S(2)}) collective-permute-start(f32[16,8,128]{2,1,0:T(8,128)S(1)} %all_to_all.15.skip_ref), channel_id=1, source_target_pairs={{0,1},{1,0},{2,3},{3,2},{4,5},{5,4},{6,7},{7,6},{8,9},{9,8},{10,11... | collective-permute-start | bytes 196616 | tf_op jit(solution)/shard_map/ppermute | solution.py:690

commit v5 on v4

--- a/solution.py
+++ b/solution.py
@@ -20,7 +20,7 @@
 COT_ROWS = 512
 BLOCKS = 8
 SKIP_SCALE = 1.0 / math.sqrt(16 * 2048 * 64)
-UNROLL = {"gather": 8, "first": 4, "regrid": 8, "second": 4}
+UNROLL = {"gather": 8, "first": 8, "regrid": 8, "second": 8}
 
 f32 = jnp.float32
 bf16 = jnp.bfloat16

time: 149 us -> 148 us (level)
  transfers between devices with their start and end apart: 10 -> 10, of which waited for: 6 -> 6; matrix products, arithmetic and copies ran while one was open for 0% -> 0% of each run, Pallas kernels for 12% -> 11%
where the time goes in v5:
time: 148 us
  waiting for transfers between devices  41.2 us (28%)
  Pallas kernels  40 us (27%)
  starting transfers between devices  33.7 us (23%)
  blocking collectives  31 us (21%)
    pallas_call x12, Pallas kernels, call(): pl.pallas_call(kernel, out_shape=shapes if many else shapes[0], in_specs=...  40 us
    all_to_all x1, waiting for transfers between devices, over_x(): return lax.all_to_all(values, 'x', split_axis=0, concat_axis=0, tiled=True)  24.9 us
    ppermute x8, starting transfers between devices, swap(): return lax.ppermute(values, axis, [(0, 1), (1, 0)])  22 us
    all_to_all x1, blocking collectives, over_x(): return lax.all_to_all(values, 'x', split_axis=0, concat_axis=0, tiled=True)  18.3 us
    ppermute x8, waiting for transfers between devices, swap(): return lax.ppermute(values, axis, [(0, 1), (1, 0)])  16.3 us
    all_to_all x1, blocking collectives, on_device(): lax.all_to_all(skip_sums, 'dp', split_axis=0, concat_axis=0, tiled=True)  12.6 us
    ppermute x1, starting transfers between devices, on_device(): end = lax.ppermute(end, 'z', [(0, 1)])  6.88 us
    all_to_all x1, starting transfers between devices, over_x(): return lax.all_to_all(values, 'x', split_axis=0, concat_axis=0, tiled=True)  4.85 us
  transfers between devices with their start and end apart: 10, of which 6 were waited for; matrix products, arithmetic and copies ran while one was open for 0% of the time, Pallas kernels for 11%

profile of v5, /device:TPU:1, one launch (start us, length us, event | category | flops | bytes accessed | tf_op | source)
XLA Modules:
  0.0 147.9 jit_solution(15214074468167648317)
XLA Ops:
  0.6 3.0 %pack_kernel.1 = bf16[4,2096,128]{2,1,0:T(8,128)(2,1)} custom-call(bf16[128,2048]{1,0:T(8,128)(2,1)} %bitcast.23, f32[32,128]{1,0:T(8,128)} %bitcast.28, f32[32,128]{1,0:T(8,128)} %bitcast.29, bf16[128,128]{1,0:T(8,128)(2,1)} %bitcast.24, bf16[128,128]{1,0:T(8,128)(2,1)} %bitcast.25, bf16[128,128]{1,0:T(8,128)(2,1)} %bitcast.26, bf16[128,128]{1,0:T(8,128)(2,1)} %bitcast.27, ...), custom_call_target="tpu_custom_call" | custom-call | flops 2000000000 | bytes 1000000 | tf_op jit(solution)/shard_map/pack_kernel/pallas_call | solution.py:672
  3.7 4.9 %all-to-all-start = ((bf16[4,2096,128]{2,1,0:T(8,128)(2,1)}), bf16[4,2096,128]{2,1,0:T(8,128)(2,1)S(1)}, u32[]{:S(2)}, u32[]{:S(2)}) async-start(bf16[4,2096,128]{2,1,0:T(8,128)(2,1)} %pack_kernel.1), calls=%async_computation | async-start | bytes 4292608 | tf_op jit(solution)/shard_map/all_to_all | solution.py:694
  8.5 24.9 %all-to-all-done.own = bf16[4,2096,128]{2,1,0:T(8,128)(2,1)S(1)} async-done(((bf16[4,2096,128]{2,1,0:T(8,128)(2,1)}), bf16[4,2096,128]{2,1,0:T(8,128)(2,1)S(1)}, u32[]{:S(2)}, u32[]{:S(2)}) %all-to-all-start) | async-done | bytes 2146336 | tf_op jit(solution)/shard_map/all_to_all | solution.py:694
  33.4 1.2 constant_dynamic-slice_fusion
  34.6 2.9 %collective-permute-start = (bf16[4,1312,128]{2,1,0:T(8,128)(2,1)}, bf16[4,1312,128]{2,1,0:T(8,128)(2,1)S(1)}, u32[]{:S(2)}, u32[]{:S(2)}) collective-permute-start(bf16[4,1312,128]{2,1,0:T(8,128)(2,1)} %constant_dynamic-slice_fusion), channel_id=1, source_target_pairs={{0,1},{1,0},{2,3},{3,2},{4,5},{5,4},{6,7},{7,6},{8,9},{9,8},{10,11... | collective-permute-start | bytes 4030472 | tf_op jit(solution)/shard_map/ppermute | solution.py:690
  37.5 0.1 pad_add_fusion.place_ref
  37.6 0.0 copy-start.1
  37.6 2.8 %collective-permute-done.other = bf16[4,1312,128]{2,1,0:T(8,128)(2,1)S(1)} collective-permute-done((bf16[4,1312,128]{2,1,0:T(8,128)(2,1)}, bf16[4,1312,128]{2,1,0:T(8,128)(2,1)S(1)}, u32[]{:S(2)}, u32[]{:S(2)}) %collective-permute-start) | collective-permute-done | bytes 1343520 | tf_op jit(solution)/shard_map/ppermute | solution.py:690
  40.4 6.5 %gather_kernel.1 = (bf16[8,272,128]{2,1,0:T(8,128)(2,1)S(1)}, bf16[8,512,128]{2,1,0:T(8,128)(2,1)S(1)}, bf16[8,528,128]{2,1,0:T(8,128)(2,1)S(1)}, bf16[2,128,128...) custom-call(s32[3]{0:T(128)S(1)} %pad_add_fusion.place_ref, ...), custom_call_target="tpu_custom_call" | custom-call | flops 5000000000 | bytes 1000000 | tf_op jit(solution)/shard_map/gather_kernel/pallas_call | solution.py:672
  47.0 7.0 %collective-permute-start.1 = (bf16[2,128,128]{2,1,0:T(8,128)(2,1)S(1)}, bf16[2,128,128]{2,1,0:T(8,128)(2,1)S(1)}, u32[]{:S(2)}, u32[]{:S(2)}) collective-permute-start(bf16[2,128,128]{2,1,0:T(8,128)(2,1)S(1)} %get-tuple-element.42), channel_id=1, source_target_pairs={{0,8},{8,0},{1,9},{9,1},{2,10},{10,2},{3,11},{11,3},{4,12},{12,4},... | collective-permute-start | bytes 196616 | tf_op jit(solution)/shard_map/ppermute | solution.py:690
  54.0 2.2 %collective-permute-done.1.ends_ref = bf16[2,128,128]{2,1,0:T(8,128)(2,1)S(1)} collective-permute-done((bf16[2,128,128]{2,1,0:T(8,128)(2,1)S(1)}, bf16[2,128,128]{2,1,0:T(8,128)(2,1)S(1)}, u32[]{:S(2)}, u32[]{:S(2)}) %collective-permute-start.1) | collective-permute-done | bytes 65568 | tf_op jit(solution)/shard_map/ppermute | solution.py:690
  56.1 0.0 copy-done.1
  56.1 0.0 copy-start
  56.1 4.7 %first_forward.1 = (bf16[2,512,128]{2,1,0:T(8,128)(2,1)S(1)}, bf16[2,512,128]{2,1,0:T(8,128)(2,1)S(1)}, bf16[8,2,256,128]{3,2,1,0:T(8,128)(2,1)S(1)}) custom-call(s32[3]{0:T(128)S(1)} %pad_add_fusion.place_ref, f32[32]{0:T(128)S(1)} %copy-done.1, bf16[2,8,32,128]{3,2,1,0:T(8,128)(2,1)S(1)} %get-tuple-element.37.rows_ref, ...), custom_call_target="tpu_custom_call" | custom-call | flops 5000000000 | bytes 1000000 | tf_op jit(solution)/shard_map/first_forward/pallas_call | solution.py:672
  60.9 5.1 %collective-permute-start.3 = (bf16[2,512,128]{2,1,0:T(8,128)(2,1)S(1)}, bf16[2,512,128]{2,1,0:T(8,128)(2,1)S(1)}, u32[]{:S(2)}, u32[]{:S(2)}) collective-permute-start(bf16[2,512,128]{2,1,0:T(8,128)(2,1)S(1)} %get-tuple-element.46), channel_id=1, source_target_pairs={{0,8},{8,0},{1,9},{9,1},{2,10},{10,2},{3,11},{11,3},{4,12},{12,4},... | collective-permute-start | bytes 786440 | tf_op jit(solution)/shard_map/ppermute | solution.py:690
  65.9 0.0 copy-done
  65.9 5.7 %first_backward.1 = (bf16[2,512,128]{2,1,0:T(8,128)(2,1)S(1)}, bf16[2,512,128]{2,1,0:T(8,128)(2,1)S(1)}, bf16[8,2,256,128]{3,2,1,0:T(8,128)(2,1)S(1)}) custom-call(s32[3]{0:T(128)S(1)} %pad_add_fusion.place_ref, f32[32]{0:T(128)S(1)} %copy-done, bf16[2,8,32,128]{3,2,1,0:T(8,128)(2,1)S(1)} %get-tuple-element.37.rows_ref, ...), custom_call_target="tpu_custom_call" | custom-call | flops 5000000000 | bytes 1000000 | tf_op jit(solution)/shard_map/first_backward/pallas_call | solution.py:672
  71.6 0.7 collective-permute-start.2
  72.3 0.0 collective-permute-done.3.got_ref
  72.3 2.5 %regrid_forward.1 = (bf16[8,2,128,128]{3,2,1,0:T(8,128)(2,1)S(1)}, bf16[2,128,128]{2,1,0:T(8,128)(2,1)S(1)}, f32[8,128]{1,0:T(8,128)S(1)}) custom-call(s32[3]{0:T(128)S(1)} %pad_add_fusion.place_ref, bf16[2,8,32,128]{3,2,1,0:T(8,128)(2,1)S(1)} %get-tuple-element.37.rows_ref, bf16[8,528,128]{2,1,0:T(8,128)(2,1)S(1)} %get-tuple-element.40.sh_ref, ...), custom_call_target="tpu_custom_call" | custom-call | flops 5000000000 | bytes 1000000 | tf_op jit(solution)/shard_map/regrid_forward/pallas_call | solution.py:672
  74.8 6.9 %collective-permute-start.5 = (bf16[2,128,128]{2,1,0:T(8,128)(2,1)S(1)}, bf16[2,128,128]{2,1,0:T(8,128)(2,1)S(1)}, u32[]{:S(2)}, u32[]{:S(2)}) collective-permute-start(bf16[2,128,128]{2,1,0:T(8,128)(2,1)S(1)} %get-tuple-element.53), channel_id=1, source_target_pairs={{0,8},{1,9},{2,10},{3,11},{4,12},{5,13},{6,14},{7,15},{16,24},{17,... | collective-permute-start | bytes 196616 | tf_op jit(solution)/shard_map/ppermute | solution.py:805
  81.7 9.6 %collective-permute-done.2.got_ref = bf16[2,512,128]{2,1,0:T(8,128)(2,1)S(1)} collective-permute-done((bf16[2,512,128]{2,1,0:T(8,128)(2,1)S(1)}, bf16[2,512,128]{2,1,0:T(8,128)(2,1)S(1)}, u32[]{:S(2)}, u32[]{:S(2)}) %collective-permute-start.2) | collective-permute-done | bytes 262176 | tf_op jit(solution)/shard_map/ppermute | solution.py:690
  91.3 1.9 %regrid_backward.1 = (bf16[8,2,128,128]{3,2,1,0:T(8,128)(2,1)S(1)}, f32[264,128]{1,0:T(8,128)S(1)}) custom-call(s32[3]{0:T(128)S(1)} %pad_add_fusion.place_ref, bf16[2,8,32,128]{3,2,1,0:T(8,128)(2,1)S(1)} %get-tuple-element.37.rows_ref, bf16[8,272,128]{2,1,0:T(8,128)(2,1)S(1)} %get-tuple-element.39.tok_ref, ...), custom_call_target="tpu_custom_call" | custom-call | flops 5000000000 | bytes 1000000 | tf_op jit(solution)/shard_map/regrid_backward/pallas_call | solution.py:672
  93.2 2.2 %collective-permute-start.4 = (f32[264,128]{1,0:T(8,128)S(1)}, f32[264,128]{1,0:T(8,128)S(1)}, u32[]{:S(2)}, u32[]{:S(2)}) collective-permute-start(f32[264,128]{1,0:T(8,128)S(1)} %get-tuple-element.50.own_ref), channel_id=1, source_target_pairs={{0,8},{8,0},{1,9},{9,1},{2,10},{10,2},{3,11},{11,3},{4,12},{12,4},... | collective-permute-start | bytes 405512 | tf_op jit(solution)/shard_map/ppermute | solution.py:690
  95.4 0.0 collective-permute-done.5.ends_ref
  95.4 6.4 %second_forward.1._second.source.own_two_ref = bf16[2,4,272,128]{3,2,1,0:T(8,128)(2,1)S(1)} custom-call(s32[3]{0:T(128)S(1)} %pad_add_fusion.place_ref, bf16[2,8,32,128]{3,2,1,0:T(8,128)(2,1)S(1)} %get-tuple-element.37.rows_ref, f32[8,8,128]{2,1,0:T(8,128)S(1)} %get-tuple-element.38.run_ref, bf16[8,528,128]{2,1,0:T(8,128)(2,1)S(1)} %get-tuple-element.40.sh_ref, ...), custom_call_target="tpu_custom_call" | custom-call | flops 8000000000 | bytes 1000000 | tf_op jit(solution)/shard_map/second_forward/pallas_call | solution.py:672
  101.8 0.8 collective-permute-done.4.ends_ref
  102.6 6.3 %second_backward.1 = (bf16[2,4,528,128]{3,2,1,0:T(8,128)(2,1)S(1)}, f32[16,8,128]{2,1,0:T(8,128)S(1)}) custom-call(s32[3]{0:T(128)S(1)} %pad_add_fusion.place_ref, f32[32]{0:T(128)S(1)} %copy-done.1, bf16[2,8,32,128]{3,2,1,0:T(8,128)(2,1)S(1)} %get-tuple-element.37.rows_ref, f32[8,8,128]{2,1,0:T(8,128)S(1)} %get-tuple-element.38.run_ref, ...), custom_call_target="tpu_custom_call" | custom-call | flops 8000000000 | bytes 1000000 | tf_op jit(solution)/shard_map/second_backward/pallas_call | solution.py:672
  108.9 0.7 pick_second.2
  109.7 2.2 %collective-permute-start.6 = (bf16[4,528,128]{2,1,0:T(8,128)(2,1)S(1)}, bf16[4,528,128]{2,1,0:T(8,128)(2,1)S(1)}, u32[]{:S(2)}, u32[]{:S(2)}) collective-permute-start(bf16[4,528,128]{2,1,0:T(8,128)(2,1)S(1)} %pick_second.2), channel_id=1, source_target_pairs={{0,1},{1,0},{2,3},{3,2},{4,5},{5,4},{6,7},{7,6},{8,9},{9,8},{10,11... | collective-permute-start | bytes 1622024 | tf_op jit(solution)/shard_map/ppermute | solution.py:690
  111.8 0.4 pick_second.3
  112.2 0.1 collective-permute-start.7
  112.4 12.6 %all_to_all.15.skip_ref = f32[16,8,128]{2,1,0:T(8,128)S(1)} all-to-all(f32[16,8,128]{2,1,0:T(8,128)S(1)} %get-tuple-element.55), channel_id=1, replica_groups=mesh['dp'=16,'z'=2,'x'=4,'core'=2] {'dp'}, dimensions={0} | all-to-all | bytes 131072 | tf_op jit(solution)/shard_map/all_to_all | solution.py:854
  125.0 1.9 %collective-permute-start.8 = (f32[16,8,128]{2,1,0:T(8,128)S(1)}, f32[16,8,128]{2,1,0:T(8,128)S(1)}, u32[]{:S(2)}, u32[]{:S(2)}) collective-permute-start(f32[16,8,128]{2,1,0:T(8,128)S(1)} %all_to_all.15.skip_ref), channel_id=1, source_target_pairs={{0,1},{1,0},{2,3},{3,2},{4,5},{5,4},{6,7},{7,6},{8,9},{9,8},{10,11... | collective-permute-start | bytes 196616 | tf_op jit(solution)/shard_map/ppermute | solution.py:690
  126.9 0.9 collective-permute-done.8.skip_other_ref
  127.8 0.0 collective-permute-done.7.other_two_ref
  127.8 0.0 collective-permute-done.6.other_ref
  127.8 0.1 pair_kernel.1
  128.0 18.3 %all_to_all.16.back_ref = bf16[4,1120,128]{2,1,0:T(8,128)(2,1)S(1)} all-to-all(bf16[4,1120,128]{2,1,0:T(8,128)(2,1)S(1)} %pair_kernel.1), channel_id=1, replica_groups=mesh['dp'=16,'z'=2,'x'=4,'core'=2] {'x'}, dimensions={0} | all-to-all | bytes 2293760 | tf_op jit(solution)/shard_map/all_to_all | solution.py:694
  146.3 1.6 %last_kernel.1 = (bf16[128,2048]{1,0:T(8,128)(2,1)}, bf16[128,128]{1,0:T(8,128)(2,1)}, bf16[128,128]{1,0:T(8,128)(2,1)}, bf16[128,128]{1,0:T(8,128)(2,1)}, bf16[...) custom-call(s32[3]{0:T(128)S(1)} %pad_add_fusion.place_ref, ...), custom_call_target="tpu_custom_call" | custom-call | flops 1000000000 | bytes 1000000 | tf_op jit(solution)/shard_map/last_kernel/pallas_call | solution.py:672
Async XLA Ops:
  3.7 29.8 %all-to-all-start = ((bf16[4,2096,128]{2,1,0:T(8,128)(2,1)}), bf16[4,2096,128]{2,1,0:T(8,128)(2,1)S(1)}, u32[]{:S(2)}, u32[]{:S(2)}) async-start(bf16[4,2096,128]{2,1,0:T(8,128)(2,1)} %pack_kernel.1), calls=%async_computation | async-start | bytes 4292608 | tf_op jit(solution)/shard_map/all_to_all | solution.py:694
  34.6 5.8 %collective-permute-start = (bf16[4,1312,128]{2,1,0:T(8,128)(2,1)}, bf16[4,1312,128]{2,1,0:T(8,128)(2,1)S(1)}, u32[]{:S(2)}, u32[]{:S(2)}) collective-permute-start(bf16[4,1312,128]{2,1,0:T(8,128)(2,1)} %constant_dynamic-slice_fusion), channel_id=1, source_target_pairs={{0,1},{1,0},{2,3},{3,2},{4,5},{5,4},{6,7},{7,6},{8,9},{9,8},{10,11... | collective-permute-start | bytes 4030472 | tf_op jit(solution)/shard_map/ppermute | solution.py:690
  37.6 18.5 %copy-start.1 = (f32[32]{0:T(128)S(1)}, f32[32]{0:T(128)}, u32[]{:S(2)}) copy-start(f32[32]{0:T(128)} %skip_ref.5) | copy-start | bytes 388
  47.0 9.2 %collective-permute-start.1 = (bf16[2,128,128]{2,1,0:T(8,128)(2,1)S(1)}, bf16[2,128,128]{2,1,0:T(8,128)(2,1)S(1)}, u32[]{:S(2)}, u32[]{:S(2)}) collective-permute-start(bf16[2,128,128]{2,1,0:T(8,128)(2,1)S(1)} %get-tuple-element.42), channel_id=1, source_target_pairs={{0,8},{8,0},{1,9},{9,1},{2,10},{10,2},{3,11},{11,3},{4,12},{12,4},... | collective-permute-start | bytes 196616 | tf_op jit(solution)/shard_map/ppermute | solution.py:690
  56.1 9.8 %copy-start = (f32[32]{0:T(128)S(1)}, f32[32]{0:T(128)}, u32[]{:S(2)}) copy-start(f32[32]{0:T(128)} %skip_ref.3) | copy-start | bytes 388
  60.9 11.4 %collective-permute-start.3 = (bf16[2,512,128]{2,1,0:T(8,128)(2,1)S(1)}, bf16[2,512,128]{2,1,0:T(8,128)(2,1)S(1)}, u32[]{:S(2)}, u32[]{:S(2)}) collective-permute-start(bf16[2,512,128]{2,1,0:T(8,128)(2,1)S(1)} %get-tuple-element.46), channel_id=1, source_target_pairs={{0,8},{8,0},{1,9},{9,1},{2,10},{10,2},{3,11},{11,3},{4,12},{12,4},... | collective-permute-start | bytes 786440 | tf_op jit(solution)/shard_map/ppermute | solution.py:690
  71.6 19.7 %collective-permute-start.2 = (bf16[2,512,128]{2,1,0:T(8,128)(2,1)S(1)}, bf16[2,512,128]{2,1,0:T(8,128)(2,1)S(1)}, u32[]{:S(2)}, u32[]{:S(2)}) collective-permute-start(bf16[2,512,128]{2,1,0:T(8,128)(2,1)S(1)} %get-tuple-element.44), channel_id=1, source_target_pairs={{0,8},{8,0},{1,9},{9,1},{2,10},{10,2},{3,11},{11,3},{4,12},{12,4},... | collective-permute-start | bytes 786440 | tf_op jit(solution)/shard_map/ppermute | solution.py:690
  74.8 20.6 %collective-permute-start.5 = (bf16[2,128,128]{2,1,0:T(8,128)(2,1)S(1)}, bf16[2,128,128]{2,1,0:T(8,128)(2,1)S(1)}, u32[]{:S(2)}, u32[]{:S(2)}) collective-permute-start(bf16[2,128,128]{2,1,0:T(8,128)(2,1)S(1)} %get-tuple-element.53), channel_id=1, source_target_pairs={{0,8},{1,9},{2,10},{3,11},{4,12},{5,13},{6,14},{7,15},{16,24},{17,... | collective-permute-start | bytes 196616 | tf_op jit(solution)/shard_map/ppermute | solution.py:805
  93.2 9.4 %collective-permute-start.4 = (f32[264,128]{1,0:T(8,128)S(1)}, f32[264,128]{1,0:T(8,128)S(1)}, u32[]{:S(2)}, u32[]{:S(2)}) collective-permute-start(f32[264,128]{1,0:T(8,128)S(1)} %get-tuple-element.50.own_ref), channel_id=1, source_target_pairs={{0,8},{8,0},{1,9},{9,1},{2,10},{10,2},{3,11},{11,3},{4,12},{12,4},... | collective-permute-start | bytes 405512 | tf_op jit(solution)/shard_map/ppermute | solution.py:690
  109.7 18.1 %collective-permute-start.6 = (bf16[4,528,128]{2,1,0:T(8,128)(2,1)S(1)}, bf16[4,528,128]{2,1,0:T(8,128)(2,1)S(1)}, u32[]{:S(2)}, u32[]{:S(2)}) collective-permute-start(bf16[4,528,128]{2,1,0:T(8,128)(2,1)S(1)} %pick_second.2), channel_id=1, source_target_pairs={{0,1},{1,0},{2,3},{3,2},{4,5},{5,4},{6,7},{7,6},{8,9},{9,8},{10,11... | collective-permute-start | bytes 1622024 | tf_op jit(solution)/shard_map/ppermute | solution.py:690
  112.2 15.6 %collective-permute-start.7 = (bf16[4,272,128]{2,1,0:T(8,128)(2,1)S(1)}, bf16[4,272,128]{2,1,0:T(8,128)(2,1)S(1)}, u32[]{:S(2)}, u32[]{:S(2)}) collective-permute-start(bf16[4,272,128]{2,1,0:T(8,128)(2,1)S(1)} %pick_second.3), channel_id=1, source_target_pairs={{0,1},{1,0},{2,3},{3,2},{4,5},{5,4},{6,7},{7,6},{8,9},{9,8},{10,11... | collective-permute-start | bytes 835592 | tf_op jit(solution)/shard_map/ppermute | solution.py:690
  125.0 2.8 %collective-permute-start.8 = (f32[16,8,128]{2,1,0:T(8,128)S(1)}, f32[16,8,128]{2,1,0:T(8,128)S(1)}, u32[]{:S(2)}, u32[]{:S(2)}) collective-permute-start(f32[16,8,128]{2,1,0:T(8,128)S(1)} %all_to_all.15.skip_ref), channel_id=1, source_target_pairs={{0,1},{1,0},{2,3},{3,2},{4,5},{5,4},{6,7},{7,6},{8,9},{9,8},{10,11... | collective-permute-start | bytes 196616 | tf_op jit(solution)/shard_map/ppermute | solution.py:690
